TPU v7x, 512 devices: a whole 4x4x16 slice. The times are simulated.
512 devices in a mesh: gx: 16 (over z), gy: 32 (over x, y, core).
Axes of the slice: x: 4, y: 4, z: 16, core: 2. Of those that a mesh axis runs over, the one named last changes fastest.
Arguments:
- normals: bfloat16 [16384, 3, 64], P(('gx', 'gy')), may hold values from -6 to 6
- owners: int32 [16384, 1], P(('gx', 'gy')), may hold values from 0 to 31; in each aligned block of 32 rows (0 to 31, 32 to 63, ...) at most 2 rows name the same one
- cells: int32 [16384, 64], P(('gx', 'gy')), may hold values from 0 to 16383
- target: float32 [128, 256, 256], P('gx', 'gy'), may hold values from -4 to 4
Outputs:
- indicator: float32 [128, 256, 256], P('gx', 'gy')
- slope: float32 [3, 128, 256, 256], P(None, 'gx', 'gy')
- normal_grad: float32 [16384, 3, 64], P(('gx', 'gy'))
Inputs may be any that keep to these rules, and one draw needn't show every extreme that they name: `owners`: among the 32 blocks of one device no owner is named more than 2 times, and some device names some owner exactly 2 times.
All inputs are finite; a program needn't handle non-finite values.
Results may differ from a plain program's by a relative error of at most 0.0004.
Values may be sent and summed in bfloat16 or wider, within the bound.
No kernel may reach another device: no remote copies, remote signals or barrier semaphores. Data moves between devices by JAX's collectives and lax.ppermute only.
A program may use at most 128 MiB of HBM per device.

v0:
```python
import math

import jax
import jax.numpy as jnp
import ml_dtypes
import numpy as np
from jax import lax
from jax.experimental import pallas as pl
from jax.experimental.pallas import tpu as pltpu
from jax.sharding import PartitionSpec as P

GX, GY = 16, 32
BX, BY, NZ = 8, 8, 256
NX, NY = GX * BX, GY * BY
KZ = NZ // 2 // GY
KB = NY // BY // GX
BLOCKS, POINTS, CAP = 32, 64, 2
WIDTH = 64.0
F32, BF16 = jnp.float32, jnp.bfloat16


def halves(table):
    high = table.astype(ml_dtypes.bfloat16)
    low = (table - high.astype(np.float64)).astype(ml_dtypes.bfloat16)
    return np.stack([high, low])


def unit(turns):
    return np.exp(-2j * np.pi * turns)


def parts_of(w):
    return np.stack([np.stack([w.real, -w.imag]), np.stack([w.imag, w.real])])


Y_CLASS = np.array([[h, -h if h else 16] for h in range(GX)])
X_CLASS = np.array([k if k <= 8 else k - 16 for k in range(16)])


def make_tables():
    z = np.arange(NZ)
    kz = np.arange(NZ // 2)
    w = unit((kz[:, None] * z[None, :] % NZ) / NZ)
    zf = np.stack([w.real, w.imag])
    zf[1, 0] = np.where(z % 2 == 0, 1.0, -1.0)
    zb = 2.0 * zf
    zb[:, 0] = zf[:, 0]
    zb = zb / (NX * NY * NZ)
    order = lambda t: t.reshape(2, GY, KZ, NZ).transpose(1, 0, 2, 3).reshape(NZ, NZ)
    g = np.arange(GY)
    wy = parts_of(unit(Y_CLASS.reshape(-1)[:, None] * g[None, :] / GY))
    y_rows = np.einsum("abkg,zw->akzgbw", wy, np.eye(KZ)).reshape(NZ, NZ)
    g = np.arange(GX)
    wx = parts_of(unit(X_CLASS[:, None] * g[None, :] / GX))
    x_rows = np.einsum("abkg,zw->akzgbw", wx, np.eye(KB * KZ)).reshape(NZ, NZ)
    e = np.arange(8)
    w8 = unit((e[:, None] * e[None, :] % 8) / 8)
    y_lanes = np.concatenate([np.kron(np.eye(16), w8.real), np.kron(np.eye(16), w8.imag)], 1)
    x8 = lambda t: np.kron(np.eye(2), np.kron(t, np.eye(8)))
    x_lanes = np.concatenate([x8(w8.real), x8(w8.imag)], 1)
    ty = unit(np.repeat(Y_CLASS.reshape(-1), KZ)[:, None] * np.tile(e, 16)[None, :] / NY)
    tx = unit(
        np.repeat(X_CLASS, KB * KZ)[:, None] * np.tile(np.repeat(e, 8), 2)[None, :] / NX
    )
    twist = lambda t: np.stack([t.real, -t.imag]).astype(np.float32)
    mirror = np.zeros((2, 2, 128, 128), np.float32)
    for m in range(2):
        for n in range(2):
            for f in range(2):
                for a in range(8):
                    for b in range(8):
                        src = f * 64 + (-a - m) % 8 * 8 + (-b - n) % 8
                        mirror[m, n, src, f * 64 + a * 8 + b] = 1.0
    return dict(
        zf=halves(order(zf)),
        zb=halves(order(zb)),
        y_rows=halves(y_rows),
        x_rows=halves(x_rows),
        y_lanes=halves(y_lanes),
        x_lanes=halves(x_lanes),
        ty=twist(ty),
        tx=twist(tx),
        mirror=mirror.reshape(512, 128).astype(ml_dtypes.bfloat16),
    )


TABLES = make_tables()


def split(x):
    high = x.astype(BF16)
    return high, (x - high.astype(F32)).astype(BF16)


def mm(a, b, ca=1, cb=0):
    return lax.dot_general(a, b, (((ca,), (cb,)), ((), ())), preferred_element_type=F32)


def mm3(a, b, ca=1, cb=0):
    return mm(a[0], b[0], ca, cb) + (mm(a[0], b[1], ca, cb) + mm(a[1], b[0], ca, cb))


def lanes_of(pairs, table, sign):
    stacked = jnp.concatenate([pairs[0][0], pairs[1][0], pairs[0][1], pairs[1][1]], 0)
    out = mm3(split(stacked), table)
    rows = pairs[0][0].shape[0]
    result = []
    for i in range(2):
        a = out[i * rows : (i + 1) * rows]
        b = out[(2 + i) * rows : (3 + i) * rows]
        if sign > 0:
            result.append((a[:, :128] - b[:, 128:], a[:, 128:] + b[:, :128]))
        else:
            result.append((a[:, :128] + b[:, 128:], b[:, :128] - a[:, 128:]))
    return result


def twisted(pairs, twist, sign):
    c, s = twist[0], twist[1]
    if sign > 0:
        return [(a * c + b * s, b * c - a * s) for a, b in pairs]
    return [(a * c - b * s, b * c + a * s) for a, b in pairs]


def halves_of(real, imag):
    return [(real[:, i * 128 : (i + 1) * 128], imag[:, i * 128 : (i + 1) * 128]) for i in range(2)]


def whole_of(pairs):
    return tuple(jnp.concatenate([pairs[0][c], pairs[1][c]], 1) for c in range(2))


def table_of(ref):
    return ref[0], ref[1]


def iota(shape, dim):
    return lax.broadcasted_iota(jnp.int32, shape, dim)


def places(route, first, count):
    rows = jnp.concatenate([route[s] for s in range(first, first + count)], 1)
    cell = rows[3:4]
    column = jnp.floor(cell * (1.0 / NZ))
    return rows, column, cell - column * NZ


STEP = 4


def splat_body(route, target, zf, out):
    width = STEP * CAP * POINTS
    columns = iota((BX * BY, width), 0).astype(F32)
    levels = iota((NZ, width), 0).astype(F32)
    field = jnp.zeros((3 * BX * BY, NZ), F32)
    for first in range(0, GY, STEP):
        rows, column, level = places(route, first, STEP)
        here = columns == column
        weighted = [jnp.where(here, rows[j : j + 1], 0.0) for j in range(3)]
        weighted = jnp.concatenate(weighted, 0).astype(BF16)
        hot = jnp.where(levels == level, 1.0, 0.0).astype(BF16)
        field = field + mm(weighted, hot, 1, 1)
    both = jnp.concatenate([field, target[...].reshape(BX * BY, NZ)], 0)
    out[...] = mm3(table_of(zf), split(both), 1, 1).reshape(out.shape)


def forward_y_body(got, rows, lanes, twist, out):
    x = mm3(table_of(rows), split(got[...].reshape(NZ, NZ)))
    pairs = twisted(halves_of(x[:128], x[128:]), twist, 1)
    real, imag = whole_of(lanes_of(pairs, table_of(lanes), 1))
    out[:, 0:8, :] = real.reshape(GX, 8, NZ)
    out[:, 8:16, :] = imag.reshape(GX, 8, NZ)


def filters(gx, gy):
    shape = (128, 128)
    row, lane = iota(shape, 0), iota(shape, 1)
    kxb = row >> 3
    kx = kxb + 16 * ((lane >> 3) & 7)
    second = (row >> 2) & 1
    kb = jnp.where(second == 0, gx, jnp.where(gx == 0, 16, GY - gx))
    ka = (lane & 7) - jnp.where((second == 1) & (gx != 0), 1, 0)
    ky = (kb + 32 * ka) & (NY - 1)
    kz = KZ * gy + (row & 3)
    kx = jnp.where(kxb > 8, kx - 16, kx) & (NX - 1)
    ux = jnp.where(kx < NX // 2, kx, kx - NX).astype(F32)
    uy = jnp.where(ky < NY // 2, ky, ky - NY).astype(F32)
    ox = jnp.where(kx == NX // 2, 0.0, ux)
    oy = jnp.where(ky == NY // 2, 0.0, uy)
    oz = kz.astype(F32)
    gain = math.sqrt(float(NX * NY * NZ) * float(BX * BY * NZ) / (float(BLOCKS * POINTS) * 700.0))
    plane = ux * ux + uy * uy

    def base(ksq):
        return gain * jnp.exp(ksq * (-1.0 / (2.0 * WIDTH**2))) / jnp.maximum(ksq, 1.0)

    packed = kz == 0
    base0 = base(plane + oz * oz)
    base1 = jnp.where(packed, base(plane + float(NZ // 2) ** 2), base0)
    mean, diff = (base0 + base1) * 0.5, (base0 - base1) * 0.5
    left = -jnp.where(lane < 64, ox, oy)
    right = -jnp.where(lane < 64, oz, 0.0)
    return (left * mean, right * mean), (left * diff, right * diff)


def mirrored(pairs, gx, mirror):
    shape = (128, 128)
    row, other = iota(shape, 0), iota(shape, 1)
    swap = jnp.where(gx == 0, 0, 4)
    partner = (((16 - (row >> 3)) & 15) << 3) | ((row & 7) ^ swap)
    moves = jnp.where(other == partner, 1.0, 0.0).astype(BF16)
    wide = jnp.concatenate([pairs[0][0], pairs[1][0], pairs[0][1], pairs[1][1]], 1)
    high, low = split(wide)
    moved = mm(moves, high) + mm(moves, low)
    stacked = jnp.concatenate([moved[:, i * 128 : (i + 1) * 128] for i in range(4)], 0)
    row = iota((512, 128), 0) & 127
    half_x = (row >> 3) == 8
    half_y = (((row >> 2) & 1) == 1) & (gx == 0)
    total = jnp.zeros((512, 128), F32)
    for case in range(4):
        here = (half_x == (case >= 2)) & (half_y == (case % 2 == 1))
        high, low = split(jnp.where(here, stacked, 0.0))
        table = mirror[case * 128 : (case + 1) * 128, :]
        total = total + mm(high, table) + mm(low, table)
    quarter = [total[i * 128 : (i + 1) * 128] for i in range(4)]
    return [(quarter[0], -quarter[2]), (quarter[1], -quarter[3])]


def spectrum_body(place, got, rows, lanes, twist, mirror, out):
    gx, gy = place[0], place[1]
    x = mm3(table_of(rows), split(got[...].reshape(NZ, NZ)))
    pairs = twisted(halves_of(x[:128], x[128:]), twist, 1)
    pairs = lanes_of(pairs, table_of(lanes), 1)
    mean, diff = filters(gx, gy)
    other = mirrored(pairs, gx, mirror)
    low = iota((128, 128), 1) < 64

    def summed(a, b, c):
        both = [a[0] * b[0][c] + a[1] * b[1][c]]
        return both[0] + pltpu.roll(both[0], 64, 1)

    def target_of(b, c):
        return jnp.where(low, pltpu.roll(b[1][c], 64, 1), b[1][c])

    s = [summed(mean, pairs, c) + summed(diff, other, c) for c in range(2)]
    s2 = [summed(diff, pairs, c) + summed(mean, other, c) for c in range(2)]
    t = (-target_of(pairs, 1), target_of(pairs, 0))
    t2 = (-target_of(other, 1), target_of(other, 0))
    chi = (-s[1], s[0])
    grads = []
    for i in range(2):
        grads.append(
            tuple(
                0.25 * (mean[i] * (s[c] + t[c]) + diff[i] * (s2[c] + t2[c])) for c in range(2)
            )
        )
    grads[1] = tuple(jnp.where(low, grads[1][c], chi[c]) for c in range(2))
    pairs = lanes_of(grads, table_of(lanes), -1)
    pairs = twisted(pairs, twist, -1)
    both = jnp.concatenate(whole_of(pairs), 0)
    out[...] = mm3(table_of(rows), split(both), 0, 0).reshape(out.shape)


def inverse_y_body(got, rows, lanes, twist, out):
    real = got[:, 0:8, :].reshape(128, NZ)
    imag = got[:, 8:16, :].reshape(128, NZ)
    pairs = lanes_of(halves_of(real, imag), table_of(lanes), -1)
    pairs = twisted(pairs, twist, -1)
    both = jnp.concatenate(whole_of(pairs), 0)
    out[...] = mm3(table_of(rows), split(both), 0, 0).reshape(out.shape)


def pick_body(got, zb, route, chi, edges, picked):
    values = mm3(split(got[...].reshape(NZ, NZ)), table_of(zb), 0, 0)
    cells = BX * BY
    solid = values[3 * cells :]
    chi[...] = solid.reshape(BX, BY, NZ)
    edges[0] = solid[0:BY]
    edges[1] = solid[cells - BY :]
    for x in range(BX):
        edges[2, x : x + 1, :] = solid[x * BY : x * BY + 1]
        edges[3, x : x + 1, :] = solid[x * BY + BY - 1 : x * BY + BY]
    high, low = split(values[: 3 * cells])
    width = STEP * CAP * POINTS
    columns = iota((cells, width), 0).astype(F32)
    levels = iota((NZ, width), 0).astype(F32)
    for first in range(0, GY, STEP):
        _, column, level = places(route, first, STEP)
        hot = jnp.where(levels == level, 1.0, 0.0).astype(BF16)
        at_level = mm(high, hot) + mm(low, hot)
        here = columns == column
        lines = [
            jnp.sum(jnp.where(here, at_level[j * cells : (j + 1) * cells], 0.0), 0, keepdims=True)
            for j in range(3)
        ]
        lines = jnp.concatenate(lines + [jnp.zeros((1, width), F32)], 0)
        for s in range(STEP):
            picked[first + s] = lines[:, s * 128 : (s + 1) * 128]


def slope_body(chi, x_low, x_high, y_low, y_high, out):
    for x in range(BX):
        here = chi[x]
        before = chi[x - 1] if x > 0 else x_low[0]
        after = chi[x + 1] if x < BX - 1 else x_high[0]
        out[0, x] = (after - before) * 0.5
        side = iota((BY, NZ), 0)
        up = jnp.where(side == BY - 1, y_high[0, x : x + 1, :], pltpu.roll(here, BY - 1, 0))
        down = jnp.where(side == 0, y_low[0, x : x + 1, :], pltpu.roll(here, 1, 0))
        out[1, x] = (up - down) * 0.5
        out[2, x] = (pltpu.roll(here, NZ - 1, 1) - pltpu.roll(here, 1, 1)) * 0.5


def route_body(owners, normals, cells, out, count):
    row = iota((4, 128), 0)
    half = iota((4, 128), 1) >> 6
    empty = jnp.where(row == 3, -1.0, 0.0)
    for o in range(GY):
        out[o] = empty
        count[o] = 0
    for b in range(BLOCKS):
        owner = owners[b]
        rank = count[owner]
        count[owner] = rank + 1
        value = jnp.concatenate([normals[b].astype(F32), cells[b : b + 1, :].astype(F32)], 0)
        value = jnp.concatenate([value, value], 1)
        out[owner] = jnp.where(half == rank, value, out[owner])


def return_body(owners, got, out, count):
    for o in range(GY):
        count[o] = 0
    for b in range(BLOCKS):
        owner = owners[b]
        rank = count[owner]
        count[owner] = rank + 1
        value = got[owner]
        value = jnp.where(rank == 0, value[:, :64], value[:, 64:])
        out[b] = value[0:3]


VMEM = pl.BlockSpec(memory_space=pltpu.VMEM)
SMEM = pl.BlockSpec(memory_space=pltpu.SMEM)


def call(body, name, outs, *operands, scalars=0, scratch=()):
    shapes = [jax.ShapeDtypeStruct(s, F32) for s in outs]
    single = len(shapes) == 1
    return pl.pallas_call(
        body,
        name=name,
        out_shape=shapes[0] if single else shapes,
        in_specs=[SMEM] * scalars + [VMEM] * (len(operands) - scalars),
        out_specs=VMEM if single else [VMEM] * len(shapes),
        scratch_shapes=list(scratch),
        compiler_params=pltpu.CompilerParams(vmem_limit_bytes=40 * 1024 * 1024),
    )(*operands)


def swap(x, axis):
    return lax.all_to_all(x, axis, split_axis=0, concat_axis=0, tiled=True)


def shifted(x, axis, step):
    count = lax.axis_size(axis)
    return lax.ppermute(x, axis, [(i, (i + step) % count) for i in range(count)])


def local(normals, owners, cells, target):
    table = {k: jnp.asarray(v) for k, v in TABLES.items()}
    owner = owners.reshape(BLOCKS)
    counts = (pltpu.SMEM((GY,), jnp.int32),)
    place = jnp.stack([lax.axis_index("gx"), lax.axis_index("gy")]).astype(jnp.int32)

    message = (GY, 4, CAP * POINTS)
    sent = call(route_body, "route", [message], owner, normals, cells, scalars=1, scratch=counts)
    route = swap(sent, "gy")
    by_z, by_x = (GY, 8, NZ), (GX, 16, NZ)
    spread = call(splat_body, "splat", [by_z], route, target, table["zf"])
    got = swap(spread, "gy")
    y_args = (table["y_rows"], table["y_lanes"], table["ty"])
    spread = call(forward_y_body, "forward_y", [by_x], got, *y_args)
    got = swap(spread, "gx")
    x_args = (table["x_rows"], table["x_lanes"], table["tx"], table["mirror"])
    spread = call(spectrum_body, "spectrum", [by_x], place, got, *x_args, scalars=1)
    got = swap(spread, "gx")
    spread = call(inverse_y_body, "inverse_y", [by_z], got, *y_args)
    got = swap(spread, "gy")
    chi, edges, picked = call(
        pick_body, "pick", [(BX, BY, NZ), (4, 8, NZ), message], got, table["zb"], route
    )
    returned = swap(picked, "gy")
    x_low = shifted(edges[1:2], "gx", 1)
    x_high = shifted(edges[0:1], "gx", -1)
    y_low = shifted(edges[3:4], "gy", 1)
    y_high = shifted(edges[2:3], "gy", -1)
    slope = call(slope_body, "slope", [(3, BX, BY, NZ)], chi, x_low, x_high, y_low, y_high)
    normal_grad = call(
        return_body, "deliver", [(BLOCKS, 3, POINTS)], owner, returned, scalars=1, scratch=counts
    )
    return chi, slope, normal_grad


def solution(mesh):
    placed = (
        P(("gx", "gy"), None, None),
        P(("gx", "gy"), None),
        P(("gx", "gy"), None),
        P("gx", "gy", None),
    )
    return jax.shard_map(
        local,
        mesh=mesh,
        in_specs=placed,
        out_specs=(P("gx", "gy", None), P(None, "gx", "gy", None), P(("gx", "gy"), None, None)),
        check_vma=False,
    )
```

profile of v0, /device:TPU:1, one launch (start us, length us, event | category | flops | bytes accessed | tf_op | source)
XLA Modules:
  0.0 134.8 jit_solution(12090659352548179731)
XLA Ops:
  0.6 0.8 copy.16.normals
  1.5 0.7 copy-done.11
  2.2 0.7 copy-done.12
  2.8 0.7 route.1
  3.5 17.0 %all_to_all.30.route = f32[32,4,128]{2,1,0:T(4,128)S(1)} all-to-all(f32[32,4,128]{2,1,0:T(4,128)S(1)} %route.1), channel_id=1, replica_groups=mesh['gx'=16,'gy'=32] {'gy'}, dimensions={0} | all-to-all | bytes 131072 | tf_op jit(solution)/shard_map/all_to_all | solution.py:361
  20.5 0.8 copy-done.9
  21.4 1.3 splat.1
  22.7 12.6 %all_to_all.31.got = f32[32,8,256]{2,1,0:T(8,128)S(1)} all-to-all(f32[32,8,256]{2,1,0:T(8,128)S(1)} %splat.1), channel_id=1, replica_groups=mesh['gx'=16,'gy'=32] {'gy'}, dimensions={0} | all-to-all | bytes 524288 | tf_op jit(solution)/shard_map/all_to_all | solution.py:361
  35.3 1.5 %forward_y.1 = f32[16,16,256]{2,1,0:T(8,128)} custom-call(f32[32,8,256]{2,1,0:T(8,128)S(1)} %all_to_all.31.got, bf16[2,256,256]{2,1,0:T(8,128)(2,1)S(1)} %copy-done, bf16[2,128,256]{2,1,0:T(8,128)(2,1)S(1)} %copy-done.1, f32[2,128,128]{2,1,0:T(8,128)S(1)} %copy-done.2), custom_call_target="tpu_custom_call" | custom-call | tf_op jit(solution)/shard_map/forward_y/pallas_call | solution.py:349
  36.8 13.8 %all-to-all-start.2 = ((f32[16,16,256]{2,1,0:T(8,128)}), f32[16,16,256]{2,1,0:T(8,128)S(1)}, u32[]{:S(2)}, u32[]{:S(2)}) async-start(f32[16,16,256]{2,1,0:T(8,128)} %forward_y.1), calls=%async_computation.2 | async-start | bytes 524288 | tf_op jit(solution)/shard_map/all_to_all | solution.py:361
  50.8 14.1 %all-to-all-done.2.got = f32[16,16,256]{2,1,0:T(8,128)S(1)} async-done(((f32[16,16,256]{2,1,0:T(8,128)}), f32[16,16,256]{2,1,0:T(8,128)S(1)}, u32[]{:S(2)}, u32[]{:S(2)}) %all-to-all-start.2) | async-done | bytes 262176 | tf_op jit(solution)/shard_map/all_to_all | solution.py:361
  64.9 3.4 %spectrum.1 = f32[16,16,256]{2,1,0:T(8,128)S(1)} custom-call(s32[2]{0:T(128)S(1)} %pad_add_fusion.place, f32[16,16,256]{2,1,0:T(8,128)S(1)} %all-to-all-done.2.got, bf16[2,256,256]{2,1,0:T(8,128)(2,1)S(1)} %copy-done.5, bf16[2,128,256]{2,1,0:T(8,128)(2,1)S(1)} %copy-done.6, f32[2,128,128]{2,1,0:T(8,128)S(1)} %copy-done.7, bf16[512,128]{1,0:T(8,128)(2,1)S(1)} %copy-done.8), custom_call_target="tpu_custom_call" | custom-call | tf_op jit(solution)/shard_map/spectrum/pallas_call | solution.py:349
  68.3 23.3 %all_to_all.32.got = f32[16,16,256]{2,1,0:T(8,128)S(1)} all-to-all(f32[16,16,256]{2,1,0:T(8,128)S(1)} %spectrum.1), channel_id=1, replica_groups=mesh['gx'=16,'gy'=32] {'gx'}, dimensions={0} | all-to-all | bytes 524288 | tf_op jit(solution)/shard_map/all_to_all | solution.py:361
  91.6 0.8 inverse_y.1
  92.4 18.0 %all_to_all.33.got = f32[32,8,256]{2,1,0:T(8,128)S(1)} all-to-all(f32[32,8,256]{2,1,0:T(8,128)S(1)} %inverse_y.1), channel_id=1, replica_groups=mesh['gx'=16,'gy'=32] {'gy'}, dimensions={0} | all-to-all | bytes 524288 | tf_op jit(solution)/shard_map/all_to_all | solution.py:361
  110.4 2.1 %pick.1 = (f32[8,8,256]{2,1,0:T(8,128)}, f32[4,8,256]{2,1,0:T(8,128)S(1)}, f32[32,4,128]{2,1,0:T(4,128)}) custom-call(f32[32,8,256]{2,1,0:T(8,128)S(1)} %all_to_all.33.got, bf16[2,256,256]{2,1,0:T(8,128)(2,1)S(1)} %copy-done.3, f32[32,4,128]{2,1,0:T(4,128)S(1)} %all_to_all.30.route), custom_call_target="tpu_custom_call" | custom-call | tf_op jit(solution)/shard_map/pick/pallas_call | solution.py:349
  112.5 3.7 %all-to-all-start.5 = ((f32[32,4,128]{2,1,0:T(4,128)}), f32[32,4,128]{2,1,0:T(4,128)S(1)}, u32[]{:S(2)}, u32[]{:S(2)}) async-start(f32[32,4,128]{2,1,0:T(4,128)} %get-tuple-element.8), calls=%async_computation.5 | async-start | bytes 131072 | tf_op jit(solution)/shard_map/all_to_all | solution.py:361
  116.2 3.4 %collective-permute-start = (f32[1,8,256]{2,1,0:T(8,128)S(1)}, f32[1,8,256]{2,1,0:T(8,128)S(1)}, u32[]{:S(2)}, u32[]{:S(2)}) collective-permute-start(f32[1,8,256]{2,1,0:T(8,128)S(1)} %get-tuple-element.15), channel_id=1, source_target_pairs={{0,32},{32,64},{64,96},{96,128},{128,160},{160,192},{192,224},{224... | collective-permute-start | bytes 24584 | tf_op jit(solution)/shard_map/ppermute | solution.py:366
  119.6 4.3 %collective-permute-start.1 = (f32[1,8,256]{2,1,0:T(8,128)S(1)}, f32[1,8,256]{2,1,0:T(8,128)S(1)}, u32[]{:S(2)}, u32[]{:S(2)}) collective-permute-start(f32[1,8,256]{2,1,0:T(8,128)S(1)} %get-tuple-element.14), channel_id=1, source_target_pairs={{0,480},{32,0},{64,32},{96,64},{128,96},{160,128},{192,160},{224,1... | collective-permute-start | bytes 24584 | tf_op jit(solution)/shard_map/ppermute | solution.py:366
  123.9 3.8 %collective-permute-start.2 = (f32[1,8,256]{2,1,0:T(8,128)S(1)}, f32[1,8,256]{2,1,0:T(8,128)S(1)}, u32[]{:S(2)}, u32[]{:S(2)}) collective-permute-start(f32[1,8,256]{2,1,0:T(8,128)S(1)} %get-tuple-element.13), channel_id=1, source_target_pairs={{0,1},{1,2},{2,3},{3,4},{4,5},{5,6},{6,7},{7,8},{8,9},{9,10},{10,1... | collective-permute-start | bytes 24584 | tf_op jit(solution)/shard_map/ppermute | solution.py:366
  127.7 1.9 %collective-permute-start.3 = (f32[1,8,256]{2,1,0:T(8,128)S(1)}, f32[1,8,256]{2,1,0:T(8,128)S(1)}, u32[]{:S(2)}, u32[]{:S(2)}) collective-permute-start(f32[1,8,256]{2,1,0:T(8,128)S(1)} %get-tuple-element.12), channel_id=1, source_target_pairs={{0,31},{1,0},{2,1},{3,2},{4,3},{5,4},{6,5},{7,6},{8,7},{9,8},{10,9... | collective-permute-start | bytes 24584 | tf_op jit(solution)/shard_map/ppermute | solution.py:366
  129.7 3.0 %collective-permute-done.3.y_high = f32[1,8,256]{2,1,0:T(8,128)S(1)} collective-permute-done((f32[1,8,256]{2,1,0:T(8,128)S(1)}, f32[1,8,256]{2,1,0:T(8,128)S(1)}, u32[]{:S(2)}, u32[]{:S(2)}) %collective-permute-start.3) | collective-permute-done | bytes 8224 | tf_op jit(solution)/shard_map/ppermute | solution.py:366
  132.7 0.8 slope.1
  133.5 0.7 deliver.1
  (32 shorter events, 0.8 us)
Async XLA Ops:
  0.6 19.9 %copy-start.4 = (bf16[2,256,256]{2,1,0:T(8,128)(2,1)S(1)}, bf16[2,256,256]{2,1,0:T(8,128)(2,1)}, u32[]{:S(2)}) copy-start(bf16[2,256,256]{2,1,0:T(8,128)(2,1)} %constant.27.clone.zf) | copy-start | bytes 786436
  1.4 0.7 copy-start.11
  2.2 0.7 copy-start.12
  20.5 0.8 copy-start.9
  22.7 12.7 %copy-start = (bf16[2,256,256]{2,1,0:T(8,128)(2,1)S(1)}, bf16[2,256,256]{2,1,0:T(8,128)(2,1)}, u32[]{:S(2)}) copy-start(bf16[2,256,256]{2,1,0:T(8,128)(2,1)} %constant.29.clone.rows) | copy-start | bytes 786436
  22.7 12.7 %copy-start.1 = (bf16[2,128,256]{2,1,0:T(8,128)(2,1)S(1)}, bf16[2,128,256]{2,1,0:T(8,128)(2,1)}, u32[]{:S(2)}) copy-start(bf16[2,128,256]{2,1,0:T(8,128)(2,1)} %constant.31.clone.lanes) | copy-start | bytes 393220
  22.7 12.6 %copy-start.2 = (f32[2,128,128]{2,1,0:T(8,128)S(1)}, f32[2,128,128]{2,1,0:T(8,128)}, u32[]{:S(2)}) copy-start(f32[2,128,128]{2,1,0:T(8,128)} %constant.33.clone.twist) | copy-start | bytes 393220
  35.3 29.5 %copy-start.8 = (bf16[512,128]{1,0:T(8,128)(2,1)S(1)}, bf16[512,128]{1,0:T(8,128)(2,1)}, u32[]{:S(2)}) copy-start(bf16[512,128]{1,0:T(8,128)(2,1)} %constant.35.clone.mirror) | copy-start | bytes 393220
  36.8 28.0 %copy-start.5 = (bf16[2,256,256]{2,1,0:T(8,128)(2,1)S(1)}, bf16[2,256,256]{2,1,0:T(8,128)(2,1)}, u32[]{:S(2)}) copy-start(bf16[2,256,256]{2,1,0:T(8,128)(2,1)} %constant.30.clone.rows) | copy-start | bytes 786436
  36.8 28.0 %copy-start.6 = (bf16[2,128,256]{2,1,0:T(8,128)(2,1)S(1)}, bf16[2,128,256]{2,1,0:T(8,128)(2,1)}, u32[]{:S(2)}) copy-start(bf16[2,128,256]{2,1,0:T(8,128)(2,1)} %constant.32.clone.lanes) | copy-start | bytes 393220
  36.8 28.0 %copy-start.7 = (f32[2,128,128]{2,1,0:T(8,128)S(1)}, f32[2,128,128]{2,1,0:T(8,128)}, u32[]{:S(2)}) copy-start(f32[2,128,128]{2,1,0:T(8,128)} %constant.34.clone.twist) | copy-start | bytes 393220
  36.8 28.0 %all-to-all-start.2 = ((f32[16,16,256]{2,1,0:T(8,128)}), f32[16,16,256]{2,1,0:T(8,128)S(1)}, u32[]{:S(2)}, u32[]{:S(2)}) async-start(f32[16,16,256]{2,1,0:T(8,128)} %forward_y.1), calls=%async_computation.2 | async-start | bytes 524288 | tf_op jit(solution)/shard_map/all_to_all | solution.py:361
  92.4 18.0 %copy-start.3 = (bf16[2,256,256]{2,1,0:T(8,128)(2,1)S(1)}, bf16[2,256,256]{2,1,0:T(8,128)(2,1)}, u32[]{:S(2)}) copy-start(bf16[2,256,256]{2,1,0:T(8,128)(2,1)} %constant.28.clone.zb) | copy-start | bytes 786436
  112.5 21.0 %all-to-all-start.5 = ((f32[32,4,128]{2,1,0:T(4,128)}), f32[32,4,128]{2,1,0:T(4,128)S(1)}, u32[]{:S(2)}, u32[]{:S(2)}) async-start(f32[32,4,128]{2,1,0:T(4,128)} %get-tuple-element.8), calls=%async_computation.5 | async-start | bytes 131072 | tf_op jit(solution)/shard_map/all_to_all | solution.py:361
  116.2 16.5 %copy-start.10 = (f32[8,8,256]{2,1,0:T(8,128)S(1)}, f32[8,8,256]{2,1,0:T(8,128)}, u32[]{:S(2)}) copy-start(f32[8,8,256]{2,1,0:T(8,128)} %get-tuple-element.9.chi) | copy-start | bytes 196612
  116.2 13.5 %collective-permute-start = (f32[1,8,256]{2,1,0:T(8,128)S(1)}, f32[1,8,256]{2,1,0:T(8,128)S(1)}, u32[]{:S(2)}, u32[]{:S(2)}) collective-permute-start(f32[1,8,256]{2,1,0:T(8,128)S(1)} %get-tuple-element.15), channel_id=1, source_target_pairs={{0,32},{32,64},{64,96},{96,128},{128,160},{160,192},{192,224},{224... | collective-permute-start | bytes 24584 | tf_op jit(solution)/shard_map/ppermute | solution.py:366
  119.6 10.0 %collective-permute-start.1 = (f32[1,8,256]{2,1,0:T(8,128)S(1)}, f32[1,8,256]{2,1,0:T(8,128)S(1)}, u32[]{:S(2)}, u32[]{:S(2)}) collective-permute-start(f32[1,8,256]{2,1,0:T(8,128)S(1)} %get-tuple-element.14), channel_id=1, source_target_pairs={{0,480},{32,0},{64,32},{96,64},{128,96},{160,128},{192,160},{224,1... | collective-permute-start | bytes 24584 | tf_op jit(solution)/shard_map/ppermute | solution.py:366
  123.9 5.8 %collective-permute-start.2 = (f32[1,8,256]{2,1,0:T(8,128)S(1)}, f32[1,8,256]{2,1,0:T(8,128)S(1)}, u32[]{:S(2)}, u32[]{:S(2)}) collective-permute-start(f32[1,8,256]{2,1,0:T(8,128)S(1)} %get-tuple-element.13), channel_id=1, source_target_pairs={{0,1},{1,2},{2,3},{3,4},{4,5},{5,6},{6,7},{7,8},{8,9},{9,10},{10,1... | collective-permute-start | bytes 24584 | tf_op jit(solution)/shard_map/ppermute | solution.py:366
  127.7 5.0 %collective-permute-start.3 = (f32[1,8,256]{2,1,0:T(8,128)S(1)}, f32[1,8,256]{2,1,0:T(8,128)S(1)}, u32[]{:S(2)}, u32[]{:S(2)}) collective-permute-start(f32[1,8,256]{2,1,0:T(8,128)S(1)} %get-tuple-element.12), channel_id=1, source_target_pairs={{0,31},{1,0},{2,1},{3,2},{4,3},{5,4},{6,5},{7,6},{8,7},{9,8},{10,9... | collective-permute-start | bytes 24584 | tf_op jit(solution)/shard_map/ppermute | solution.py:366
  132.7 0.8 copy-start.13
where the time goes:
time: 136 us; the launch traced here: 135 us
  blocking collectives  70.9 us (52%)
  starting transfers between devices  30.9 us (23%)
  waiting for transfers between devices  17.1 us (13%)
  Pallas kernels  11.2 us (8%)
  local copies, waits for them, and re-layouts  3.7 us (3%)
    all_to_all x4, blocking collectives, swap(): return lax.all_to_all(x, axis, split_axis=0, concat_axis=0, tiled=True)  70.9 us
    all_to_all x2, starting transfers between devices, swap(): return lax.all_to_all(x, axis, split_axis=0, concat_axis=0, tiled=True)  17.5 us
    all_to_all x2, waiting for transfers between devices, swap(): return lax.all_to_all(x, axis, split_axis=0, concat_axis=0, tiled=True)  14.1 us
    ppermute x4, starting transfers between devices, shifted(): lax.ppermute(x, axis, [(i, (i + step) % count) for i in range(count)])  13.4 us
    pallas_call x8, Pallas kernels, call(): pl.pallas_call(body, name=name, out_shape=shapes[0] if single else shapes...  11.2 us
    unnamed x30, local copies, waits for them, and re-layouts  3.69 us
    ppermute x4, waiting for transfers between devices, shifted(): lax.ppermute(x, axis, [(i, (i + step) % count) for i in range(count)])  3.02 us
  transfers between devices with their start and end apart: 6, of which 2 were waited for; matrix products, arithmetic and copies ran while one was open for 0% of the time, Pallas kernels for 1%

commit v1 on v0

v1 whole, which is shorter than its diff:
```python
import math

import jax
import jax.numpy as jnp
import ml_dtypes
import numpy as np
from jax import lax
from jax.experimental import pallas as pl
from jax.experimental.pallas import tpu as pltpu
from jax.sharding import PartitionSpec as P

GX, GY = 16, 32
BX, BY, NZ = 8, 8, 256
NX, NY = GX * BX, GY * BY
KZ = NZ // 2 // GY
KB = NY // BY // GX
BLOCKS, POINTS, CAP = 32, 64, 2
WIDTH = 64.0
F32, BF16 = jnp.float32, jnp.bfloat16


def halves(table):
    high = table.astype(ml_dtypes.bfloat16)
    low = (table - high.astype(np.float64)).astype(ml_dtypes.bfloat16)
    return np.stack([high, low])


def unit(turns):
    return np.exp(-2j * np.pi * turns)


def parts_of(w):
    return np.stack([np.stack([w.real, -w.imag]), np.stack([w.imag, w.real])])


Y_CLASS = np.array([[h, -h if h else 16] for h in range(GX)])
X_CLASS = np.array([k if k <= 8 else k - 16 for k in range(16)])


def make_tables():
    z = np.arange(NZ)
    kz = np.arange(NZ // 2)
    w = unit((kz[:, None] * z[None, :] % NZ) / NZ)
    zf = np.stack([w.real, w.imag])
    zf[1, 0] = np.where(z % 2 == 0, 1.0, -1.0)
    zb = 2.0 * zf
    zb[:, 0] = zf[:, 0]
    zb = zb / (NX * NY * NZ)
    order = lambda t: t.reshape(2, GY, KZ, NZ).transpose(1, 0, 2, 3).reshape(NZ, NZ)
    g = np.arange(GY)
    wy = parts_of(unit(Y_CLASS.reshape(-1)[:, None] * g[None, :] / GY))
    y_rows = np.einsum("abkg,zw->akzgbw", wy, np.eye(KZ)).reshape(NZ, NZ)
    g = np.arange(GX)
    wx = parts_of(unit(X_CLASS[:, None] * g[None, :] / GX))
    x_rows = np.einsum("abkg,zw->akzgbw", wx, np.eye(KB * KZ)).reshape(NZ, NZ)
    e = np.arange(8)
    w8 = unit((e[:, None] * e[None, :] % 8) / 8)
    y_lanes = np.concatenate([np.kron(np.eye(16), w8.real), np.kron(np.eye(16), w8.imag)], 1)
    x8 = lambda t: np.kron(np.eye(2), np.kron(t, np.eye(8)))
    x_lanes = np.concatenate([x8(w8.real), x8(w8.imag)], 1)
    ty = unit(np.repeat(Y_CLASS.reshape(-1), KZ)[:, None] * np.tile(e, 16)[None, :] / NY)
    tx = unit(
        np.repeat(X_CLASS, KB * KZ)[:, None] * np.tile(np.repeat(e, 8), 2)[None, :] / NX
    )
    ky = np.repeat(Y_CLASS.reshape(-1), KZ)[:, None] + GY * e[None, :]
    slope_y = np.tile(np.sin(2 * np.pi * (ky % NY) / NY), (1, 16))
    kx = np.repeat(X_CLASS, KB * KZ)[:, None] + GX * np.repeat(e, 8)[None, :]
    slope_x = np.tile(np.sin(2 * np.pi * (kx % NX) / NX), (1, 2))
    twist = lambda t, s: np.stack([t.real, -t.imag, s]).astype(np.float32)
    mirror = np.zeros((2, 2, 128, 128), np.float32)
    for m in range(2):
        for n in range(2):
            for f in range(2):
                for a in range(8):
                    for b in range(8):
                        src = f * 64 + (-a - m) % 8 * 8 + (-b - n) % 8
                        mirror[m, n, src, f * 64 + a * 8 + b] = 1.0
    return dict(
        zf=halves(order(zf)),
        zb=halves(order(zb)),
        y_rows=halves(y_rows),
        x_rows=halves(x_rows),
        y_lanes=halves(y_lanes),
        x_lanes=halves(x_lanes),
        ty=twist(ty, slope_y),
        tx=twist(tx, slope_x),
        mirror=mirror.reshape(512, 128).astype(ml_dtypes.bfloat16),
    )


TABLES = make_tables()


def split(x):
    high = x.astype(BF16)
    return high, (x - high.astype(F32)).astype(BF16)


def mm(a, b, ca=1, cb=0):
    return lax.dot_general(a, b, (((ca,), (cb,)), ((), ())), preferred_element_type=F32)


def mm3(a, b, ca=1, cb=0):
    return mm(a[0], b[0], ca, cb) + (mm(a[0], b[1], ca, cb) + mm(a[1], b[0], ca, cb))


def lanes_of(pairs, table, sign):
    count, rows = len(pairs), pairs[0][0].shape[0]
    stacked = jnp.concatenate([p[0] for p in pairs] + [p[1] for p in pairs], 0)
    out = mm3(split(stacked), table)
    result = []
    for i in range(count):
        a = out[i * rows : (i + 1) * rows]
        b = out[(count + i) * rows : (count + i + 1) * rows]
        if sign > 0:
            result.append((a[:, :128] - b[:, 128:], a[:, 128:] + b[:, :128]))
        else:
            result.append((a[:, :128] + b[:, 128:], b[:, :128] - a[:, 128:]))
    return result


def twisted(pairs, twist, sign):
    c, s = twist[0], twist[1]
    if sign > 0:
        return [(a * c + b * s, b * c - a * s) for a, b in pairs]
    return [(a * c - b * s, b * c + a * s) for a, b in pairs]


def halves_of(real, imag):
    return [(real[:, i * 128 : (i + 1) * 128], imag[:, i * 128 : (i + 1) * 128]) for i in range(2)]


def whole_of(pairs):
    return tuple(jnp.concatenate([p[c] for p in pairs], 1) for c in range(2))


def table_of(ref):
    return ref[0], ref[1]


def iota(shape, dim):
    return lax.broadcasted_iota(jnp.int32, shape, dim)


def places(route, first, count):
    rows = jnp.concatenate([route[s] for s in range(first, first + count)], 1)
    cell = rows[3:4]
    column = jnp.floor(cell * (1.0 / NZ))
    return rows, column, cell - column * NZ


def kz_of(rows):
    row = iota((rows, 128), 0)
    return (KZ * (row >> 3) + (row & 3)).astype(F32)


def odd(k, length):
    k = k & (length - 1)
    u = jnp.where(k < length // 2, k, k - length).astype(F32)
    return u, jnp.where(k == length // 2, 0.0, u)


def ky_of(gx, row, lane):
    second = ((row >> 2) & 1) == 1
    kb = jnp.where(second, jnp.where(gx == 0, 16, -gx), gx)
    return kb + GY * (lane & 7)


def oy_of():
    row, lane = iota((128, 128), 0), iota((128, 128), 1)
    return odd(ky_of(row >> 3, row, lane), NY)[1]


STEP = 4


def splat_body(route, target, zf, out):
    width = STEP * CAP * POINTS
    columns = iota((BX * BY, width), 0).astype(F32)
    levels = iota((NZ, width), 0).astype(F32)
    field = jnp.zeros((3 * BX * BY, NZ), F32)
    for first in range(0, GY, STEP):
        rows, column, level = places(route, first, STEP)
        here = columns == column
        weighted = [jnp.where(here, rows[j : j + 1], 0.0) for j in range(3)]
        weighted = jnp.concatenate(weighted, 0).astype(BF16)
        hot = jnp.where(levels == level, 1.0, 0.0).astype(BF16)
        field = field + mm(weighted, hot, 1, 1)
    both = jnp.concatenate([field, target[...].reshape(BX * BY, NZ)], 0)
    spread = mm3(table_of(zf), split(both), 1, 1)
    right = spread[:, 128:]
    right = jnp.where(iota((NZ, 128), 1) < 64, right * kz_of(NZ), right)
    out[...] = jnp.concatenate([spread[:, :128], right], 1).reshape(out.shape)


def forward_y_body(got, rows, lanes, twist, out):
    x = mm3(table_of(rows), split(got[...].reshape(NZ, NZ)))
    pairs = twisted(halves_of(x[:128], x[128:]), twist, 1)
    left, right = lanes_of(pairs, table_of(lanes), 1)
    low = iota((128, 128), 1) < 64
    oy = oy_of()
    for c in range(2):
        both = jnp.where(low, left[c], oy * left[c] + pltpu.roll(right[c], 64, 1))
        out[:, 8 * c : 8 * c + 8, :] = both.reshape(GX, 8, 128)
    target = jnp.where(low, pltpu.roll(right[0], 64, 1), right[1])
    out[:, 16:24, :] = target.reshape(GX, 8, 128)


def filters(gx, gy):
    shape = (128, 128)
    row, lane = iota(shape, 0), iota(shape, 1)
    kxb = row >> 3
    ux, ox = odd(kxb + GX * ((lane >> 3) & 7) - jnp.where(kxb > 8, GX, 0), NX)
    uy, _ = odd(ky_of(gx, row, lane), NY)
    kz = KZ * gy + (row & 3)
    uz = kz.astype(F32)
    gain = math.sqrt(float(NX * NY * NZ) * float(BX * BY * NZ) / (float(BLOCKS * POINTS) * 700.0))
    plane = ux * ux + uy * uy

    def base(ksq):
        return gain * jnp.exp(ksq * (-1.0 / (2.0 * WIDTH**2))) / jnp.maximum(ksq, 1.0)

    base0 = base(plane + uz * uz)
    base1 = jnp.where(kz == 0, base(plane + float(NZ // 2) ** 2), base0)
    return ox, (base0 + base1) * 0.5, (base0 - base1) * 0.5


def mirrored(pair, gx, mirror):
    row, other = iota((128, 128), 0), iota((128, 128), 1)
    swap = jnp.where(gx == 0, 0, 4)
    partner = (((16 - (row >> 3)) & 15) << 3) | ((row & 7) ^ swap)
    moves = jnp.where(other == partner, 1.0, 0.0).astype(BF16)
    high, low = split(jnp.concatenate(pair, 1))
    moved = mm(moves, high) + mm(moves, low)
    stacked = jnp.concatenate([moved[:, :128], moved[:, 128:]], 0)
    row = iota((256, 128), 0) & 127
    half_x = (row >> 3) == 8
    half_y = (((row >> 2) & 1) == 1) & (gx == 0)
    total = jnp.zeros((256, 128), F32)
    for case in range(4):
        here = (half_x == (case >= 2)) & (half_y == (case % 2 == 1))
        high, low = split(jnp.where(here, stacked, 0.0))
        table = mirror[case * 128 : (case + 1) * 128, :]
        total = total + mm(high, table) + mm(low, table)
    return total[:128], -total[128:]


def turned(pair):
    return -pair[1], pair[0]


def spectrum_body(place, got, rows, lanes, twist, mirror, out):
    gx, gy = place[0], place[1]
    target = got[:, 16:24, :].reshape(128, 128)
    target = jnp.concatenate(
        [target.reshape(GX, 8, 128), pltpu.roll(target, 64, 1).reshape(GX, 8, 128)], 1
    )
    x = jnp.concatenate([got[:, 0:16, :].reshape(NZ, 128), target.reshape(NZ, 128)], 1)
    x = mm3(table_of(rows), split(x))
    pairs = twisted(halves_of(x[:128], x[128:]), twist, 1)
    left, right = lanes_of(pairs, table_of(lanes), 1)
    ox, mean, diff = filters(gx, gy)
    low = iota((128, 128), 1) < 64
    swapped = lambda x: pltpu.roll(x, 64, 1)

    div = [jnp.where(low, ox * left[c], left[c]) for c in range(2)]
    div = turned([d + swapped(d) for d in div])
    target = [jnp.where(low, right[c], swapped(right[c])) for c in range(2)]
    other = mirrored([jnp.where(low, div[c], target[c]) for c in range(2)], gx, mirror)
    div2 = [jnp.where(low, other[c], swapped(other[c])) for c in range(2)]
    target2 = [jnp.where(low, swapped(other[c]), other[c]) for c in range(2)]
    chi = [-(mean * div[c] + diff * div2[c]) for c in range(2)]
    chi2 = [-(mean * div2[c] + diff * div[c]) for c in range(2)]
    h = [
        0.25 * (mean * (chi[c] - target[c]) + diff * (chi2[c] - target2[c])) for c in range(2)
    ]
    h = turned(h)
    slope = turned([twist[2] * chi[c] for c in range(2)])
    pairs = [
        tuple(jnp.where(low, chi[c], slope[c]) for c in range(2)),
        tuple(jnp.where(low, ox * h[c], h[c]) for c in range(2)),
    ]
    pairs = twisted(lanes_of(pairs, table_of(lanes), -1), twist, -1)
    both = jnp.concatenate(whole_of(pairs), 0)
    out[...] = mm3(table_of(rows), split(both), 0, 0).reshape(out.shape)


def inverse_y_body(got, rows, lanes, twist, out):
    real = got[:, 0:8, :].reshape(128, NZ)
    imag = got[:, 8:16, :].reshape(128, NZ)
    left, right = halves_of(real, imag)
    low = iota((128, 128), 1) < 64
    oy = oy_of()
    slope = turned([twist[2] * left[c] for c in range(2)])
    third = tuple(jnp.where(low, slope[c], oy * right[c]) for c in range(2))
    pairs = lanes_of([left, right, third], table_of(lanes), -1)
    pairs = twisted(pairs, twist, -1)
    both = jnp.concatenate(whole_of(pairs), 0)
    out[...] = mm3(table_of(rows), split(both), 0, 0).reshape(out.shape)


def pick_body(got, zb, route, chi, slope, picked):
    fields = got[...].reshape(NZ, 384)
    middle = fields[:, 128:256]
    middle = jnp.where(iota((NZ, 128), 1) < 64, middle, middle * kz_of(NZ))
    fields = jnp.concatenate([fields[:, :128], middle, fields[:, 256:]], 1)
    values = mm3(split(fields), table_of(zb), 0, 0)
    cells = BX * BY
    solid, slope_x, grad_x, grad_z, slope_y, grad_y = (
        values[i * cells : (i + 1) * cells] for i in range(6)
    )
    brick = (BX, BY, NZ)
    chi[...] = solid.reshape(brick)
    slope[0] = slope_x.reshape(brick)
    slope[1] = slope_y.reshape(brick)
    slope_z = (pltpu.roll(solid, NZ - 1, 1) - pltpu.roll(solid, 1, 1)) * 0.5
    slope[2] = slope_z.reshape(brick)
    high, low = split(jnp.concatenate([grad_x, grad_y, grad_z], 0))
    width = STEP * CAP * POINTS
    columns = iota((cells, width), 0).astype(F32)
    levels = iota((NZ, width), 0).astype(F32)
    for first in range(0, GY, STEP):
        _, column, level = places(route, first, STEP)
        hot = jnp.where(levels == level, 1.0, 0.0).astype(BF16)
        at_level = mm(high, hot) + mm(low, hot)
        here = columns == column
        lines = [
            jnp.sum(jnp.where(here, at_level[j * cells : (j + 1) * cells], 0.0), 0, keepdims=True)
            for j in range(3)
        ]
        lines = jnp.concatenate(lines + [jnp.zeros((1, width), F32)], 0)
        for s in range(STEP):
            picked[first + s] = lines[:, s * 128 : (s + 1) * 128]


def route_body(owners, normals, cells, out, count):
    row = iota((4, 128), 0)
    half = iota((4, 128), 1) >> 6
    empty = jnp.where(row == 3, -1.0, 0.0)
    parts = [normals[j].astype(F32) for j in range(3)] + [cells[...].astype(F32)]
    for o in range(GY):
        out[o] = empty
        count[o] = 0
    for b in range(BLOCKS):
        owner = owners[b]
        rank = count[owner]
        count[owner] = rank + 1
        value = jnp.concatenate([p[b : b + 1] for p in parts], 0)
        value = jnp.concatenate([value, value], 1)
        out[owner] = jnp.where(half == rank, value, out[owner])


def return_body(owners, got, out, count):
    for o in range(GY):
        count[o] = 0
    for b in range(BLOCKS):
        owner = owners[b]
        rank = count[owner]
        count[owner] = rank + 1
        value = got[owner]
        value = jnp.where(rank == 0, value[:, :64], value[:, 64:])
        for j in range(3):
            out[j, b : b + 1, :] = value[j : j + 1]


VMEM = pl.BlockSpec(memory_space=pltpu.VMEM)
SMEM = pl.BlockSpec(memory_space=pltpu.SMEM)


def call(body, name, outs, *operands, scalars=0, scratch=()):
    shapes = [jax.ShapeDtypeStruct(s, F32) for s in outs]
    single = len(shapes) == 1
    return pl.pallas_call(
        body,
        name=name,
        out_shape=shapes[0] if single else shapes,
        in_specs=[SMEM] * scalars + [VMEM] * (len(operands) - scalars),
        out_specs=VMEM if single else [VMEM] * len(shapes),
        scratch_shapes=list(scratch),
        compiler_params=pltpu.CompilerParams(vmem_limit_bytes=40 * 1024 * 1024),
    )(*operands)


def swap(x, axis):
    return lax.all_to_all(x, axis, split_axis=0, concat_axis=0, tiled=True)


def local(normals, owners, cells, target):
    table = {k: jnp.asarray(v) for k, v in TABLES.items()}
    owner = owners.reshape(BLOCKS)
    counts = (pltpu.SMEM((GY,), jnp.int32),)
    place = jnp.stack([lax.axis_index("gx"), lax.axis_index("gy")]).astype(jnp.int32)

    message = (GY, 4, CAP * POINTS)
    by_part = jnp.moveaxis(normals, 1, 0)
    sent = call(route_body, "route", [message], owner, by_part, cells, scalars=1, scratch=counts)
    route = swap(sent, "gy")
    spread = call(splat_body, "splat", [(GY, 8, 256)], route, target, table["zf"])
    got = swap(spread, "gy")
    y_args = (table["y_rows"], table["y_lanes"], table["ty"])
    spread = call(forward_y_body, "forward_y", [(GX, 24, 128)], got, *y_args)
    got = swap(spread, "gx")
    x_args = (table["x_rows"], table["x_lanes"], table["tx"], table["mirror"])
    spread = call(spectrum_body, "spectrum", [(GX, 16, 256)], place, got, *x_args, scalars=1)
    got = swap(spread, "gx")
    spread = call(inverse_y_body, "inverse_y", [(GY, 8, 384)], got, *y_args)
    got = swap(spread, "gy")
    brick = (BX, BY, NZ)
    chi, slope, picked = call(
        pick_body, "pick", [brick, (3,) + brick, message], got, table["zb"], route
    )
    returned = swap(picked, "gy")
    normal_grad = call(
        return_body, "deliver", [(3, BLOCKS, POINTS)], owner, returned, scalars=1, scratch=counts
    )
    return chi, slope, jnp.moveaxis(normal_grad, 0, 1)


def solution(mesh):
    placed = (
        P(("gx", "gy"), None, None),
        P(("gx", "gy"), None),
        P(("gx", "gy"), None),
        P("gx", "gy", None),
    )
    return jax.shard_map(
        local,
        mesh=mesh,
        in_specs=placed,
        out_specs=(P("gx", "gy", None), P(None, "gx", "gy", None), P(("gx", "gy"), None, None)),
        check_vma=False,
    )
```

time: 136 us -> 123 us (0.904)
  starting transfers between devices: 30.9 us -> 13.8 us
  blocking collectives: 70.9 us -> 81.1 us
  waiting for transfers between devices: 17.1 us -> 13.1 us
    ppermute x4 -> x0, starting transfers between devices: 13.4 us -> none  [shifted(): lax.ppermute(x, axis, [(i, (i + step) % count) for i in range(count)])]
    all_to_all x4 -> x5, blocking collectives: 70.9 us -> 81.1 us  [swap(): return lax.all_to_all(x, axis, split_axis=0, concat_axis=0, tiled=True)]
    all_to_all x2 -> x1, starting transfers between devices: 17.5 us -> 13.8 us  [swap(): return lax.all_to_all(x, axis, split_axis=0, concat_axis=0, tiled=True)]
    ppermute x4 -> x0, waiting for transfers between devices: 3.02 us -> none  [shifted(): lax.ppermute(x, axis, [(i, (i + step) % count) for i in range(count)])]
    all_to_all x2 -> x1, waiting for transfers between devices: 14.1 us -> 13.1 us  [swap(): return lax.all_to_all(x, axis, split_axis=0, concat_axis=0, tiled=True)]
    unnamed x30 -> x28, local copies, waits for them, and re-layouts: 3.69 us -> 3.04 us
    pallas_call x8 -> x7, Pallas kernels: 11.2 us -> 10.8 us  [call(): pl.pallas_call(body, name=name, out_shape=shapes[0] if single else shapes...]
  transfers between devices with their start and end apart: 6 -> 1, of which waited for: 2 -> 1; matrix products, arithmetic and copies ran while one was open for 0% -> 0% of each run, Pallas kernels for 1% -> 0%
where the time goes in v1:
time: 123 us
  blocking collectives  81.1 us (66%)
  starting transfers between devices  13.8 us (11%)
  waiting for transfers between devices  13.1 us (11%)
  Pallas kernels  10.8 us (9%)
  local copies, waits for them, and re-layouts  3.04 us (2%)
    all_to_all x5, blocking collectives, swap(): return lax.all_to_all(x, axis, split_axis=0, concat_axis=0, tiled=True)  81.1 us
    all_to_all x1, starting transfers between devices, swap(): return lax.all_to_all(x, axis, split_axis=0, concat_axis=0, tiled=True)  13.8 us
    all_to_all x1, waiting for transfers between devices, swap(): return lax.all_to_all(x, axis, split_axis=0, concat_axis=0, tiled=True)  13.1 us
    pallas_call x7, Pallas kernels, call(): pl.pallas_call(body, name=name, out_shape=shapes[0] if single else shapes...  10.8 us
    unnamed x28, local copies, waits for them, and re-layouts  3.04 us
  transfers between devices with their start and end apart: 1, of which 1 were waited for; matrix products, arithmetic and copies ran while one was open for 0% of the time, Pallas kernels for 0%

profile of v1, /device:TPU:1, one launch (start us, length us, event | category | flops | bytes accessed | tf_op | source)
XLA Modules:
  0.0 122.7 jit_solution(2188647494484824463)
XLA Ops:
  0.6 0.0 copy-start.3
  0.7 0.8 copy-done.10
  1.4 0.7 copy-done.11
  2.1 0.7 copy-done.12
  2.8 0.7 route.1
  3.5 17.0 %all_to_all.30.route = f32[32,4,128]{2,1,0:T(4,128)S(1)} all-to-all(f32[32,4,128]{2,1,0:T(4,128)S(1)} %route.1), channel_id=1, replica_groups=mesh['gx'=16,'gy'=32] {'gy'}, dimensions={0} | all-to-all | bytes 131072 | tf_op jit(solution)/shard_map/all_to_all | solution.py:385
  20.5 0.8 copy-done.9
  21.3 1.3 %splat.1 = f32[32,8,256]{2,1,0:T(8,128)S(1)} custom-call(f32[32,4,128]{2,1,0:T(4,128)S(1)} %all_to_all.30.route, f32[8,8,256]{2,1,0:T(8,128)S(1)} %copy-done.9, bf16[2,256,256]{2,1,0:T(8,128)(2,1)S(1)} %copy-done.3), custom_call_target="tpu_custom_call" | custom-call | tf_op jit(solution)/shard_map/splat/pallas_call | solution.py:373
  22.6 0.0 copy-start
  22.7 0.0 copy-start.1
  22.7 12.6 %all_to_all.31.got = f32[32,8,256]{2,1,0:T(8,128)S(1)} all-to-all(f32[32,8,256]{2,1,0:T(8,128)S(1)} %splat.1), channel_id=1, replica_groups=mesh['gx'=16,'gy'=32] {'gy'}, dimensions={0} | all-to-all | bytes 524288 | tf_op jit(solution)/shard_map/all_to_all | solution.py:385
  35.3 0.0 copy-start.6
  35.3 0.0 copy-start.8
  35.3 1.5 %forward_y.1 = f32[16,24,128]{2,1,0:T(8,128)} custom-call(f32[32,8,256]{2,1,0:T(8,128)S(1)} %all_to_all.31.got, bf16[2,256,256]{2,1,0:T(8,128)(2,1)S(1)} %copy-done, bf16[2,128,256]{2,1,0:T(8,128)(2,1)S(1)} %copy-done.2, f32[3,128,128]{2,1,0:T(8,128)S(1)} %copy-done.1), custom_call_target="tpu_custom_call" | custom-call | tf_op jit(solution)/shard_map/forward_y/pallas_call | solution.py:373
  36.9 13.8 %all-to-all-start.2 = ((f32[16,24,128]{2,1,0:T(8,128)}), f32[16,24,128]{2,1,0:T(8,128)S(1)}, u32[]{:S(2)}, u32[]{:S(2)}) async-start(f32[16,24,128]{2,1,0:T(8,128)} %forward_y.1), calls=%async_computation.2 | async-start | bytes 393216 | tf_op jit(solution)/shard_map/all_to_all | solution.py:385
  50.7 0.1 pad_add_fusion.place
  50.8 13.1 %all-to-all-done.2.got = f32[16,24,128]{2,1,0:T(8,128)S(1)} async-done(((f32[16,24,128]{2,1,0:T(8,128)}), f32[16,24,128]{2,1,0:T(8,128)S(1)}, u32[]{:S(2)}, u32[]{:S(2)}) %all-to-all-start.2) | async-done | bytes 196640 | tf_op jit(solution)/shard_map/all_to_all | solution.py:385
  63.9 3.2 %spectrum.1 = f32[16,16,256]{2,1,0:T(8,128)S(1)} custom-call(s32[2]{0:T(128)S(1)} %pad_add_fusion.place, f32[16,24,128]{2,1,0:T(8,128)S(1)} %all-to-all-done.2.got, bf16[2,256,256]{2,1,0:T(8,128)(2,1)S(1)} %copy-done.5, bf16[2,128,256]{2,1,0:T(8,128)(2,1)S(1)} %copy-done.8, f32[3,128,128]{2,1,0:T(8,128)S(1)} %copy-done.6, bf16[512,128]{1,0:T(8,128)(2,1)S(1)} %copy-done.7), custom_call_target="tpu_custom_call" | custom-call | tf_op jit(solution)/shard_map/spectrum/pallas_call | solution.py:373
  67.0 21.3 %all_to_all.32.got = f32[16,16,256]{2,1,0:T(8,128)S(1)} all-to-all(f32[16,16,256]{2,1,0:T(8,128)S(1)} %spectrum.1), channel_id=1, replica_groups=mesh['gx'=16,'gy'=32] {'gx'}, dimensions={0} | all-to-all | bytes 524288 | tf_op jit(solution)/shard_map/all_to_all | solution.py:385
  88.3 1.2 inverse_y.1
  89.5 19.5 %all_to_all.33.got = f32[32,8,384]{2,1,0:T(8,128)S(1)} all-to-all(f32[32,8,384]{2,1,0:T(8,128)S(1)} %inverse_y.1), channel_id=1, replica_groups=mesh['gx'=16,'gy'=32] {'gy'}, dimensions={0} | all-to-all | bytes 786432 | tf_op jit(solution)/shard_map/all_to_all | solution.py:385
  109.0 1.6 %pick.1 = (f32[8,8,256]{2,1,0:T(8,128)}, f32[3,8,8,256]{3,2,1,0:T(8,128)}, f32[32,4,128]{2,1,0:T(4,128)S(1)}) custom-call(f32[32,8,384]{2,1,0:T(8,128)S(1)} %all_to_all.33.got, bf16[2,256,256]{2,1,0:T(8,128)(2,1)S(1)} %copy-done.4, f32[32,4,128]{2,1,0:T(4,128)S(1)} %all_to_all.30.route), custom_call_target="tpu_custom_call" | custom-call | tf_op jit(solution)/shard_map/pick/pallas_call | solution.py:373
  110.6 10.7 %all_to_all.34.got = f32[32,4,128]{2,1,0:T(4,128)S(1)} all-to-all(f32[32,4,128]{2,1,0:T(4,128)S(1)} %get-tuple-element.8), channel_id=1, replica_groups=mesh['gx'=16,'gy'=32] {'gy'}, dimensions={0} | all-to-all | bytes 131072 | tf_op jit(solution)/shard_map/all_to_all | solution.py:385
  121.4 1.3 %deliver.1 = f32[3,32,64]{2,1,0:T(8,128)} custom-call(s32[32]{0:T(128)S(1)} %bitcast.7, f32[32,4,128]{2,1,0:T(4,128)S(1)} %all_to_all.34.got), custom_call_target="tpu_custom_call" | custom-call | tf_op jit(solution)/shard_map/deliver/pallas_call | solution.py:373
  (19 shorter events, 0.0 us)
Async XLA Ops:
  0.6 19.9 %copy-start.3 = (bf16[2,256,256]{2,1,0:T(8,128)(2,1)S(1)}, bf16[2,256,256]{2,1,0:T(8,128)(2,1)}, u32[]{:S(2)}) copy-start(bf16[2,256,256]{2,1,0:T(8,128)(2,1)} %constant.27.clone.zf) | copy-start | bytes 786436
  0.6 0.8 copy-start.10
  1.4 0.7 copy-start.11
  2.1 0.7 copy-start.12
  20.5 0.8 copy-start.9
  21.3 14.0 %copy-start.2 = (bf16[2,128,256]{2,1,0:T(8,128)(2,1)S(1)}, bf16[2,128,256]{2,1,0:T(8,128)(2,1)}, u32[]{:S(2)}) copy-start(bf16[2,128,256]{2,1,0:T(8,128)(2,1)} %constant.31.clone.lanes) | copy-start | bytes 393220
  22.6 12.7 %copy-start = (bf16[2,256,256]{2,1,0:T(8,128)(2,1)S(1)}, bf16[2,256,256]{2,1,0:T(8,128)(2,1)}, u32[]{:S(2)}) copy-start(bf16[2,256,256]{2,1,0:T(8,128)(2,1)} %constant.29.clone.rows) | copy-start | bytes 786436
  22.7 12.6 %copy-start.1 = (f32[3,128,128]{2,1,0:T(8,128)S(1)}, f32[3,128,128]{2,1,0:T(8,128)}, u32[]{:S(2)}) copy-start(f32[3,128,128]{2,1,0:T(8,128)} %constant.33.clone.twist) | copy-start | bytes 589828
  35.3 28.5 %copy-start.6 = (f32[3,128,128]{2,1,0:T(8,128)S(1)}, f32[3,128,128]{2,1,0:T(8,128)}, u32[]{:S(2)}) copy-start(f32[3,128,128]{2,1,0:T(8,128)} %constant.34.clone.twist) | copy-start | bytes 589828
  35.3 28.5 %copy-start.8 = (bf16[2,128,256]{2,1,0:T(8,128)(2,1)S(1)}, bf16[2,128,256]{2,1,0:T(8,128)(2,1)}, u32[]{:S(2)}) copy-start(bf16[2,128,256]{2,1,0:T(8,128)(2,1)} %constant.32.clone.lanes) | copy-start | bytes 393220
  36.9 27.0 %copy-start.5 = (bf16[2,256,256]{2,1,0:T(8,128)(2,1)S(1)}, bf16[2,256,256]{2,1,0:T(8,128)(2,1)}, u32[]{:S(2)}) copy-start(bf16[2,256,256]{2,1,0:T(8,128)(2,1)} %constant.30.clone.rows) | copy-start | bytes 786436
  36.9 27.0 %copy-start.7 = (bf16[512,128]{1,0:T(8,128)(2,1)S(1)}, bf16[512,128]{1,0:T(8,128)(2,1)}, u32[]{:S(2)}) copy-start(bf16[512,128]{1,0:T(8,128)(2,1)} %constant.35.clone.mirror) | copy-start | bytes 393220
  36.9 27.0 %all-to-all-start.2 = ((f32[16,24,128]{2,1,0:T(8,128)}), f32[16,24,128]{2,1,0:T(8,128)S(1)}, u32[]{:S(2)}, u32[]{:S(2)}) async-start(f32[16,24,128]{2,1,0:T(8,128)} %forward_y.1), calls=%async_computation.2 | async-start | bytes 393216 | tf_op jit(solution)/shard_map/all_to_all | solution.py:385
  89.5 19.6 %copy-start.4 = (bf16[2,256,256]{2,1,0:T(8,128)(2,1)S(1)}, bf16[2,256,256]{2,1,0:T(8,128)(2,1)}, u32[]{:S(2)}) copy-start(bf16[2,256,256]{2,1,0:T(8,128)(2,1)} %constant.28.clone.zb) | copy-start | bytes 786436
  110.6 10.7 %copy-start.13 = (s32[32,1]{0,1:T(1,128)S(1)}, s32[32,1]{0,1:T(1,128)}, u32[]{:S(2)}) copy-start(s32[32,1]{0,1:T(1,128)} %param.14) | copy-start | bytes 388

commit v2 on v1

--- a/solution.py
+++ b/solution.py
@@ -218,7 +218,8 @@
     plane = ux * ux + uy * uy
 
     def base(ksq):
-        return gain * jnp.exp(ksq * (-1.0 / (2.0 * WIDTH**2))) / jnp.maximum(ksq, 1.0)
+        value = gain * jnp.exp(ksq * (-1.0 / (2.0 * WIDTH**2))) / jnp.maximum(ksq, 1.0)
+        return jnp.where(ksq == 0.0, 0.0, value)
 
     base0 = base(plane + uz * uz)
     base1 = jnp.where(kz == 0, base(plane + float(NZ // 2) ** 2), base0)
@@ -226,31 +227,35 @@
 
 
 def mirrored(pair, gx, mirror):
-    row, other = iota((128, 128), 0), iota((128, 128), 1)
+    row, other = iota((32, 128), 0), iota((32, 128), 1)
     swap = jnp.where(gx == 0, 0, 4)
-    partner = (((16 - (row >> 3)) & 15) << 3) | ((row & 7) ^ swap)
+    partner = (((16 - (row >> 1)) & 15) << 3) | (((row & 1) << 2) ^ swap)
     moves = jnp.where(other == partner, 1.0, 0.0).astype(BF16)
     high, low = split(jnp.concatenate(pair, 1))
     moved = mm(moves, high) + mm(moves, low)
-    stacked = jnp.concatenate([moved[:, :128], moved[:, 128:]], 0)
-    row = iota((256, 128), 0) & 127
-    half_x = (row >> 3) == 8
-    half_y = (((row >> 2) & 1) == 1) & (gx == 0)
-    total = jnp.zeros((256, 128), F32)
-    for case in range(4):
-        here = (half_x == (case >= 2)) & (half_y == (case % 2 == 1))
-        high, low = split(jnp.where(here, stacked, 0.0))
-        table = mirror[case * 128 : (case + 1) * 128, :]
-        total = total + mm(high, table) + mm(low, table)
-    return total[:128], -total[128:]
+    moved = jnp.concatenate([moved[:, :128], moved[:, 128:]], 0)
+    row = iota((64, 128), 0) & 31
+    half_x = (row >> 1) == 8
+    half_y = ((row & 1) == 1) & (gx == 0)
+    cases = [
+        jnp.where((half_x == (case >= 2)) & (half_y == (case % 2 == 1)), moved, 0.0)
+        for case in range(4)
+    ]
+    high, low = split(jnp.concatenate(cases, 1))
+    turned_back = mm(high, mirror[...]) + mm(low, mirror[...])
+    high, low = split(jnp.concatenate([turned_back[:32], -turned_back[32:]], 1))
+    row, other = iota((128, 32), 0), iota((128, 32), 1)
+    home = jnp.where(row == other * 4, 1.0, 0.0).astype(BF16)
+    total = mm(home, high) + mm(home, low)
+    return total[:, :128], total[:, 128:]
 
 
 def turned(pair):
     return -pair[1], pair[0]
 
 
-def spectrum_body(place, got, rows, lanes, twist, mirror, out):
-    gx, gy = place[0], place[1]
+def spectrum_body(got, rows, lanes, twist, mirror, out):
+    gx, gy = lax.axis_index("gx"), lax.axis_index("gy")
     target = got[:, 16:24, :].reshape(128, 128)
     target = jnp.concatenate(
         [target.reshape(GX, 8, 128), pltpu.roll(target, 64, 1).reshape(GX, 8, 128)], 1
@@ -333,14 +338,23 @@
             picked[first + s] = lines[:, s * 128 : (s + 1) * 128]
 
 
-def route_body(owners, normals, cells, out, count):
+def route_body(*refs):
+    sources, (out, target, zf), (owners, normals, cells, count, sems) = refs[:5], refs[5:8], refs[8:]
+    fetches = [
+        pltpu.make_async_copy(source, place, sems.at[i])
+        for i, (source, place) in enumerate(zip(sources, (owners, normals, cells, target, zf)))
+    ]
+    for fetch in fetches:
+        fetch.start()
     row = iota((4, 128), 0)
     half = iota((4, 128), 1) >> 6
     empty = jnp.where(row == 3, -1.0, 0.0)
-    parts = [normals[j].astype(F32) for j in range(3)] + [cells[...].astype(F32)]
     for o in range(GY):
         out[o] = empty
         count[o] = 0
+    for fetch in fetches[:3]:
+        fetch.wait()
+    parts = [normals[j].astype(F32) for j in range(3)] + [cells[...].astype(F32)]
     for b in range(BLOCKS):
         owner = owners[b]
         rank = count[owner]
@@ -348,9 +362,11 @@
         value = jnp.concatenate([p[b : b + 1] for p in parts], 0)
         value = jnp.concatenate([value, value], 1)
         out[owner] = jnp.where(half == rank, value, out[owner])
-
-
-def return_body(owners, got, out, count):
+    for fetch in fetches[3:]:
+        fetch.wait()
+
+
+def return_body(owners, got, out, count, rows):
     for o in range(GY):
         count[o] = 0
     for b in range(BLOCKS):
@@ -358,29 +374,34 @@
         rank = count[owner]
         count[owner] = rank + 1
         value = got[owner]
-        value = jnp.where(rank == 0, value[:, :64], value[:, 64:])
-        for j in range(3):
-            out[j, b : b + 1, :] = value[j : j + 1]
+        rows[b] = jnp.where(rank == 0, value, pltpu.roll(value, 64, 1))
+    for j in range(3):
+        out[j] = rows[:, j, :][:, :64]
 
 
 VMEM = pl.BlockSpec(memory_space=pltpu.VMEM)
 SMEM = pl.BlockSpec(memory_space=pltpu.SMEM)
-
-
-def call(body, name, outs, *operands, scalars=0, scratch=()):
-    shapes = [jax.ShapeDtypeStruct(s, F32) for s in outs]
+HBM = pl.BlockSpec(memory_space=pltpu.HBM)
+
+
+def call(body, name, outs, *operands, specs=None, scratch=()):
+    shapes = [s if hasattr(s, "dtype") else jax.ShapeDtypeStruct(s, F32) for s in outs]
     single = len(shapes) == 1
     return pl.pallas_call(
         body,
         name=name,
         out_shape=shapes[0] if single else shapes,
-        in_specs=[SMEM] * scalars + [VMEM] * (len(operands) - scalars),
+        in_specs=specs or [VMEM] * len(operands),
         out_specs=VMEM if single else [VMEM] * len(shapes),
         scratch_shapes=list(scratch),
         compiler_params=pltpu.CompilerParams(vmem_limit_bytes=40 * 1024 * 1024),
     )(*operands)
 
 
+def kept(x):
+    return pltpu.with_memory_space_constraint(x, pltpu.HBM)
+
+
 def swap(x, axis):
     return lax.all_to_all(x, axis, split_axis=0, concat_axis=0, tiled=True)
 
@@ -388,30 +409,51 @@
 def local(normals, owners, cells, target):
     table = {k: jnp.asarray(v) for k, v in TABLES.items()}
     owner = owners.reshape(BLOCKS)
-    counts = (pltpu.SMEM((GY,), jnp.int32),)
-    place = jnp.stack([lax.axis_index("gx"), lax.axis_index("gy")]).astype(jnp.int32)
-
+    counts = pltpu.SMEM((GY,), jnp.int32)
+    brick = (BX, BY, NZ)
     message = (GY, 4, CAP * POINTS)
+
     by_part = jnp.moveaxis(normals, 1, 0)
-    sent = call(route_body, "route", [message], owner, by_part, cells, scalars=1, scratch=counts)
+    scratch = (
+        pltpu.SMEM(owner.shape, jnp.int32),
+        pltpu.VMEM(by_part.shape, BF16),
+        pltpu.VMEM(cells.shape, jnp.int32),
+        counts,
+        pltpu.SemaphoreType.DMA((5,)),
+    )
+    tables_z = jax.ShapeDtypeStruct(table["zf"].shape, BF16)
+    sources = (owner, by_part, cells, target, table["zf"])
+    sent, target_here, zf = call(
+        route_body,
+        "route",
+        [message, brick, tables_z],
+        *map(kept, sources),
+        specs=[HBM] * 5,
+        scratch=scratch,
+    )
     route = swap(sent, "gy")
-    spread = call(splat_body, "splat", [(GY, 8, 256)], route, target, table["zf"])
+    spread = call(splat_body, "splat", [(GY, 8, 256)], route, target_here, zf)
     got = swap(spread, "gy")
     y_args = (table["y_rows"], table["y_lanes"], table["ty"])
     spread = call(forward_y_body, "forward_y", [(GX, 24, 128)], got, *y_args)
     got = swap(spread, "gx")
     x_args = (table["x_rows"], table["x_lanes"], table["tx"], table["mirror"])
-    spread = call(spectrum_body, "spectrum", [(GX, 16, 256)], place, got, *x_args, scalars=1)
+    spread = call(spectrum_body, "spectrum", [(GX, 16, 256)], got, *x_args)
     got = swap(spread, "gx")
     spread = call(inverse_y_body, "inverse_y", [(GY, 8, 384)], got, *y_args)
     got = swap(spread, "gy")
-    brick = (BX, BY, NZ)
     chi, slope, picked = call(
         pick_body, "pick", [brick, (3,) + brick, message], got, table["zb"], route
     )
     returned = swap(picked, "gy")
     normal_grad = call(
-        return_body, "deliver", [(3, BLOCKS, POINTS)], owner, returned, scalars=1, scratch=counts
+        return_body,
+        "deliver",
+        [(3, BLOCKS, POINTS)],
+        owner,
+        returned,
+        specs=[SMEM, VMEM],
+        scratch=(counts, pltpu.VMEM((BLOCKS, 4, CAP * POINTS), F32)),
     )
     return chi, slope, jnp.moveaxis(normal_grad, 0, 1)
 

time: 123 us -> 119 us (0.967)
  blocking collectives: 81.1 us -> 108 us
  starting transfers between devices: 13.8 us -> 0 us
  waiting for transfers between devices: 13.1 us -> 0 us
  local copies, waits for them, and re-layouts: 3.04 us -> 0.06 us
    all_to_all x5 -> x6, blocking collectives: 81.1 us -> 108 us  [swap(): return lax.all_to_all(x, axis, split_axis=0, concat_axis=0, tiled=True)]
    all_to_all x1 -> x0, starting transfers between devices: 13.8 us -> none  [swap(): return lax.all_to_all(x, axis, split_axis=0, concat_axis=0, tiled=True)]
    all_to_all x1 -> x0, waiting for transfers between devices: 13.1 us -> none  [swap(): return lax.all_to_all(x, axis, split_axis=0, concat_axis=0, tiled=True)]
    unnamed x28 -> x18, local copies, waits for them, and re-layouts: 3.04 us -> 0.06 us
  transfers between devices with their start and end apart: 1 -> 0, of which waited for: 1 -> 0; matrix products, arithmetic and copies ran while one was open for 0% -> 0% of each run, Pallas kernels for 0% -> 0%
where the time goes in v2:
time: 119 us; the launch traced here: 118 us
  blocking collectives  108 us (91%)
  Pallas kernels  9.78 us (8%)
    all_to_all x6, blocking collectives, swap(): return lax.all_to_all(x, axis, split_axis=0, concat_axis=0, tiled=True)  108 us
    pallas_call x7, Pallas kernels, call(): pl.pallas_call(body, name=name, out_shape=shapes[0] if single else shapes...  9.78 us

profile of v2, /device:TPU:1, one launch (start us, length us, event | category | flops | bytes accessed | tf_op | source)
XLA Modules:
  0.0 118.5 jit_solution(10329467888422057376)
XLA Ops:
  0.6 1.1 route.1
  1.7 17.0 %all_to_all.30.route = f32[32,4,128]{2,1,0:T(4,128)S(1)} all-to-all(f32[32,4,128]{2,1,0:T(4,128)S(1)} %get-tuple-element.9), channel_id=1, replica_groups=mesh['gx'=16,'gy'=32] {'gy'}, dimensions={0} | all-to-all | bytes 131072 | tf_op jit(solution)/shard_map/all_to_all | solution.py:406
  18.7 1.3 %splat.1 = f32[32,8,256]{2,1,0:T(8,128)S(1)} custom-call(f32[32,4,128]{2,1,0:T(4,128)S(1)} %all_to_all.30.route, f32[8,8,256]{2,1,0:T(8,128)S(1)} %get-tuple-element.10.target, bf16[2,256,256]{2,1,0:T(8,128)(2,1)S(1)} %get-tuple-element.11.zf), custom_call_target="tpu_custom_call" | custom-call | tf_op jit(solution)/shard_map/splat/pallas_call | solution.py:390
  20.0 0.0 copy-start
  20.0 0.0 copy-start.1
  20.0 12.6 %all_to_all.31.got = f32[32,8,256]{2,1,0:T(8,128)S(1)} all-to-all(f32[32,8,256]{2,1,0:T(8,128)S(1)} %splat.1), channel_id=1, replica_groups=mesh['gx'=16,'gy'=32] {'gy'}, dimensions={0} | all-to-all | bytes 524288 | tf_op jit(solution)/shard_map/all_to_all | solution.py:406
  32.6 0.0 copy-done.2
  32.7 0.0 copy-start.5
  32.7 0.0 copy-start.7
  32.7 0.9 forward_y.1
  33.5 0.0 copy-start.4
  33.6 0.0 copy-start.6
  33.6 26.8 %all_to_all.32.got = f32[16,24,128]{2,1,0:T(8,128)S(1)} all-to-all(f32[16,24,128]{2,1,0:T(8,128)S(1)} %forward_y.1), channel_id=1, replica_groups=mesh['gx'=16,'gy'=32] {'gx'}, dimensions={0} | all-to-all | bytes 393216 | tf_op jit(solution)/shard_map/all_to_all | solution.py:406
  60.3 0.0 copy-done.4
  60.3 0.0 copy-done.6
  60.3 2.4 %spectrum.1 = f32[16,16,256]{2,1,0:T(8,128)S(1)} custom-call(f32[16,24,128]{2,1,0:T(8,128)S(1)} %all_to_all.32.got, bf16[2,256,256]{2,1,0:T(8,128)(2,1)S(1)} %copy-done.4, bf16[2,128,256]{2,1,0:T(8,128)(2,1)S(1)} %copy-done.7, f32[3,128,128]{2,1,0:T(8,128)S(1)} %copy-done.5, bf16[512,128]{1,0:T(8,128)(2,1)S(1)} %copy-done.6), custom_call_target="tpu_custom_call" | custom-call | tf_op jit(solution)/shard_map/spectrum/pallas_call | solution.py:390
  62.8 21.3 %all_to_all.33.got = f32[16,16,256]{2,1,0:T(8,128)S(1)} all-to-all(f32[16,16,256]{2,1,0:T(8,128)S(1)} %spectrum.1), channel_id=1, replica_groups=mesh['gx'=16,'gy'=32] {'gx'}, dimensions={0} | all-to-all | bytes 524288 | tf_op jit(solution)/shard_map/all_to_all | solution.py:406
  84.0 1.2 inverse_y.1
  85.2 0.0 copy-start.3
  85.2 19.5 %all_to_all.34.got = f32[32,8,384]{2,1,0:T(8,128)S(1)} all-to-all(f32[32,8,384]{2,1,0:T(8,128)S(1)} %inverse_y.1), channel_id=1, replica_groups=mesh['gx'=16,'gy'=32] {'gy'}, dimensions={0} | all-to-all | bytes 786432 | tf_op jit(solution)/shard_map/all_to_all | solution.py:406
  104.8 1.6 %pick.1 = (f32[8,8,256]{2,1,0:T(8,128)}, f32[3,8,8,256]{3,2,1,0:T(8,128)}, f32[32,4,128]{2,1,0:T(4,128)S(1)}) custom-call(f32[32,8,384]{2,1,0:T(8,128)S(1)} %all_to_all.34.got, bf16[2,256,256]{2,1,0:T(8,128)(2,1)S(1)} %copy-done.3, f32[32,4,128]{2,1,0:T(4,128)S(1)} %all_to_all.30.route), custom_call_target="tpu_custom_call" | custom-call | tf_op jit(solution)/shard_map/pick/pallas_call | solution.py:390
  106.4 0.0 copy-start.8
  106.4 10.7 %all_to_all.35.got = f32[32,4,128]{2,1,0:T(4,128)S(1)} all-to-all(f32[32,4,128]{2,1,0:T(4,128)S(1)} %get-tuple-element.14), channel_id=1, replica_groups=mesh['gx'=16,'gy'=32] {'gy'}, dimensions={0} | all-to-all | bytes 131072 | tf_op jit(solution)/shard_map/all_to_all | solution.py:406
  117.1 1.4 %deliver.1 = f32[3,32,64]{2,1,0:T(8,128)} custom-call(s32[32]{0:T(128)S(1)} %bitcast.4, f32[32,4,128]{2,1,0:T(4,128)S(1)} %all_to_all.35.got), custom_call_target="tpu_custom_call" | custom-call | tf_op jit(solution)/shard_map/deliver/pallas_call | solution.py:390
  (7 shorter events, 0.0 us)
Async XLA Ops:
  18.7 14.0 %copy-start.2 = (bf16[2,128,256]{2,1,0:T(8,128)(2,1)S(1)}, bf16[2,128,256]{2,1,0:T(8,128)(2,1)}, u32[]{:S(2)}) copy-start(bf16[2,128,256]{2,1,0:T(8,128)(2,1)} %constant.22.clone.lanes) | copy-start | bytes 393220
  20.0 12.7 %copy-start = (bf16[2,256,256]{2,1,0:T(8,128)(2,1)S(1)}, bf16[2,256,256]{2,1,0:T(8,128)(2,1)}, u32[]{:S(2)}) copy-start(bf16[2,256,256]{2,1,0:T(8,128)(2,1)} %constant.20.clone.rows) | copy-start | bytes 786436
  20.0 12.6 %copy-start.1 = (f32[3,128,128]{2,1,0:T(8,128)S(1)}, f32[3,128,128]{2,1,0:T(8,128)}, u32[]{:S(2)}) copy-start(f32[3,128,128]{2,1,0:T(8,128)} %constant.24.clone.twist) | copy-start | bytes 589828
  32.7 27.7 %copy-start.5 = (f32[3,128,128]{2,1,0:T(8,128)S(1)}, f32[3,128,128]{2,1,0:T(8,128)}, u32[]{:S(2)}) copy-start(f32[3,128,128]{2,1,0:T(8,128)} %constant.25.clone.twist) | copy-start | bytes 589828
  32.7 27.7 %copy-start.7 = (bf16[2,128,256]{2,1,0:T(8,128)(2,1)S(1)}, bf16[2,128,256]{2,1,0:T(8,128)(2,1)}, u32[]{:S(2)}) copy-start(bf16[2,128,256]{2,1,0:T(8,128)(2,1)} %constant.23.clone.lanes) | copy-start | bytes 393220
  33.5 26.8 %copy-start.4 = (bf16[2,256,256]{2,1,0:T(8,128)(2,1)S(1)}, bf16[2,256,256]{2,1,0:T(8,128)(2,1)}, u32[]{:S(2)}) copy-start(bf16[2,256,256]{2,1,0:T(8,128)(2,1)} %constant.21.clone.rows) | copy-start | bytes 786436
  33.6 26.8 %copy-start.6 = (bf16[512,128]{1,0:T(8,128)(2,1)S(1)}, bf16[512,128]{1,0:T(8,128)(2,1)}, u32[]{:S(2)}) copy-start(bf16[512,128]{1,0:T(8,128)(2,1)} %constant.26.clone.mirror) | copy-start | bytes 393220
  85.2 19.6 %copy-start.3 = (bf16[2,256,256]{2,1,0:T(8,128)(2,1)S(1)}, bf16[2,256,256]{2,1,0:T(8,128)(2,1)}, u32[]{:S(2)}) copy-start(bf16[2,256,256]{2,1,0:T(8,128)(2,1)} %constant.19.clone.zb) | copy-start | bytes 786436
  106.4 10.7 %copy-start.8 = (s32[32,1]{0,1:T(1,128)S(1)}, s32[32,1]{0,1:T(1,128)}, u32[]{:S(2)}) copy-start(s32[32,1]{0,1:T(1,128)} %param.14) | copy-start | bytes 388

commit v3 on v2

--- a/solution.py
+++ b/solution.py
@@ -83,7 +83,7 @@
         y_lanes=halves(y_lanes),
         x_lanes=halves(x_lanes),
         ty=twist(ty, slope_y),
-        tx=twist(tx, slope_x),
+        tx=twist(tx, slope_x)[:2],
         mirror=mirror.reshape(512, 128).astype(ml_dtypes.bfloat16),
     )
 
@@ -193,17 +193,82 @@
     out[...] = jnp.concatenate([spread[:, :128], right], 1).reshape(out.shape)
 
 
+def swapped(x):
+    return pltpu.roll(x, 64, 1)
+
+
+def low_half(rows=128):
+    return iota((rows, 128), 1) < 64
+
+
+def packed_of(real, imag):
+    low = low_half()
+    return jnp.where(low, real, swapped(imag)), jnp.where(low, swapped(real), imag)
+
+
+def weight_of(gx, gy):
+    row, lane = iota((128, 128), 0), iota((128, 128), 1)
+    gx = row >> 3 if gx is None else gx
+    uy, _ = odd(ky_of(gx, row, lane), NY)
+    uz = (KZ * gy + (row & 3)).astype(F32)
+    return jnp.sqrt(uy * uy + uz * uz + 1.0)
+
+
+BITS, SPLIT, BIAS, EDGE_BITS = 20, 11, 128, 30
+ROWS = 18
+
+
+def scale_of(exponent, bits):
+    return jnp.exp2((bits - exponent).astype(F32))
+
+
+def exponent_of(x):
+    top = jnp.max(jnp.abs(x), 1, keepdims=True)
+    power = jnp.floor(jnp.log2(jnp.maximum(top, 1e-26)) + 0.001) + 1.0
+    return power.astype(jnp.int32)
+
+
+def fixed(x, exponent, bits):
+    return jnp.floor(x * scale_of(exponent, bits) + 0.5).astype(jnp.int32)
+
+
+def encode(fields, exponents):
+    a, b, c = (fixed(x, e, BITS) for x, e in zip(fields, exponents))
+    e = [x + BIAS for x in exponents]
+    mark = e[0] | (e[1] << 8) | (e[2] << 16)
+    lane = iota((128, 128), 1)
+    bit = jnp.where(lane < 24, (mark >> (lane & 31)) & 1, 0)
+    first = (a << SPLIT) | (c & 0x7FF)
+    second = (b << SPLIT) | ((c >> SPLIT) & 0x3FF) | (bit << 10)
+    return first, second
+
+
+def decode(first, second):
+    lane = iota((128, 128), 1)
+    bit = ((second >> 10) & 1) << (lane & 7)
+    exponents = []
+    for i in range(3):
+        here = jnp.where((lane >> 3) == i, bit, 0).astype(F32)
+        exponents.append(jnp.sum(here, 1, keepdims=True).astype(jnp.int32) - BIAS)
+    a, b = first >> SPLIT, second >> SPLIT
+    c = (((second & 0x3FF) << 22) >> SPLIT) | (first & 0x7FF)
+    fields = [x.astype(F32) / scale_of(e, BITS) for x, e in zip((a, b, c), exponents)]
+    return fields, exponents
+
+
 def forward_y_body(got, rows, lanes, twist, out):
     x = mm3(table_of(rows), split(got[...].reshape(NZ, NZ)))
     pairs = twisted(halves_of(x[:128], x[128:]), twist, 1)
     left, right = lanes_of(pairs, table_of(lanes), 1)
-    low = iota((128, 128), 1) < 64
+    low = low_half()
     oy = oy_of()
-    for c in range(2):
-        both = jnp.where(low, left[c], oy * left[c] + pltpu.roll(right[c], 64, 1))
-        out[:, 8 * c : 8 * c + 8, :] = both.reshape(GX, 8, 128)
-    target = jnp.where(low, pltpu.roll(right[0], 64, 1), right[1])
-    out[:, 16:24, :] = target.reshape(GX, 8, 128)
+    real, imag = (jnp.where(low, left[c], oy * left[c] + swapped(right[c])) for c in range(2))
+    target = jnp.where(low, swapped(right[0]), right[1])
+    part_x, part_yz = packed_of(real, imag)
+    fields = (part_x, part_yz / weight_of(None, lax.axis_index("gy")), target)
+    first, second = encode(fields, [exponent_of(x) for x in fields])
+    out[:, 0:8, :] = first.reshape(GX, 8, 128)
+    out[:, 8:16, :] = second.reshape(GX, 8, 128)
 
 
 def filters(gx, gy):
@@ -254,19 +319,20 @@
     return -pair[1], pair[0]
 
 
-def spectrum_body(got, rows, lanes, twist, mirror, out):
+def spectrum_body(got, rows, lanes, twist, mirror, out, edges):
     gx, gy = lax.axis_index("gx"), lax.axis_index("gy")
-    target = got[:, 16:24, :].reshape(128, 128)
-    target = jnp.concatenate(
-        [target.reshape(GX, 8, 128), pltpu.roll(target, 64, 1).reshape(GX, 8, 128)], 1
-    )
-    x = jnp.concatenate([got[:, 0:16, :].reshape(NZ, 128), target.reshape(NZ, 128)], 1)
+    words = (got[:, i * 8 : i * 8 + 8, :].reshape(128, 128) for i in range(2))
+    (part_x, part_yz, target), _ = decode(*words)
+    part_yz = part_yz * weight_of(gx, gy)
+    x = [*packed_of(part_x, part_yz), target, swapped(target)]
+    x = [part.reshape(GX, 8, 128) for part in x]
+    x = [jnp.concatenate(x[i : i + 2], 1).reshape(NZ, 128) for i in (0, 2)]
+    x = jnp.concatenate(x, 1)
     x = mm3(table_of(rows), split(x))
     pairs = twisted(halves_of(x[:128], x[128:]), twist, 1)
     left, right = lanes_of(pairs, table_of(lanes), 1)
     ox, mean, diff = filters(gx, gy)
-    low = iota((128, 128), 1) < 64
-    swapped = lambda x: pltpu.roll(x, 64, 1)
+    low = low_half()
 
     div = [jnp.where(low, ox * left[c], left[c]) for c in range(2)]
     div = turned([d + swapped(d) for d in div])
@@ -280,21 +346,55 @@
         0.25 * (mean * (chi[c] - target[c]) + diff * (chi2[c] - target2[c])) for c in range(2)
     ]
     h = turned(h)
-    slope = turned([twist[2] * chi[c] for c in range(2)])
-    pairs = [
-        tuple(jnp.where(low, chi[c], slope[c]) for c in range(2)),
-        tuple(jnp.where(low, ox * h[c], h[c]) for c in range(2)),
-    ]
+    pairs = [chi, tuple(jnp.where(low, ox * h[c], h[c]) for c in range(2))]
     pairs = twisted(lanes_of(pairs, table_of(lanes), -1), twist, -1)
     both = jnp.concatenate(whole_of(pairs), 0)
-    out[...] = mm3(table_of(rows), split(both), 0, 0).reshape(out.shape)
-
-
-def inverse_y_body(got, rows, lanes, twist, out):
-    real = got[:, 0:8, :].reshape(128, NZ)
-    imag = got[:, 8:16, :].reshape(128, NZ)
-    left, right = halves_of(real, imag)
-    low = iota((128, 128), 1) < 64
+    x = mm3(table_of(rows), split(both), 0, 0).reshape(GX, 16, NZ)
+    chi, _ = packed_of(*(x[:, c : c + 8, :128].reshape(128, 128) for c in (0, 8)))
+    gradients = packed_of(*(x[:, c : c + 8, 128:].reshape(128, 128) for c in (0, 8)))
+
+    below = jnp.concatenate([chi[120:], chi[:120]], 0)
+    above = jnp.concatenate([chi[8:], chi[:8]], 0)
+    lane = iota((128, 128), 1) >> 3
+    edge = jnp.where(lane == 0, pltpu.roll(below, 72, 1), 0.0)
+    edge = jnp.where(lane == 1, pltpu.roll(above, 8, 1), edge)
+    edge = jnp.where(lane == 2, pltpu.roll(below, 24, 1), edge)
+    edge = jnp.where(lane == 3, pltpu.roll(above, 88, 1), edge)
+    grad_x, h = gradients
+    fields = (chi, grad_x, h * weight_of(gx, gy))
+    exponents = [exponent_of(x) for x in fields]
+    exponents[0] = jnp.maximum(exponents[0], exponent_of(edge))
+    first, second = encode(fields, exponents)
+    edges[...] = fixed(edge, exponents[0], EDGE_BITS)
+    folded = edges[pl.ds(0, 32, stride=4), :]
+    for i in range(1, 4):
+        piece = pltpu.roll(edges[pl.ds(i, 32, stride=4), :], 32 * i, 1)
+        folded = jnp.where((iota((32, 128), 1) >> 5) == i, piece, folded)
+    for g in range(GX):
+        at = g * ROWS
+        out[at : at + 8, :] = first[g * 8 : g * 8 + 8]
+        out[at + 8 : at + 16, :] = second[g * 8 : g * 8 + 8]
+        out[at + 16 : at + 18, :] = folded[g * 2 : g * 2 + 2]
+
+
+def inverse_y_body(got, rows, lanes, twist, out, edges):
+    pick = lambda at, count: [got[g * ROWS + at : g * ROWS + at + count, :] for g in range(GX)]
+    first, second = (jnp.concatenate(pick(at, 8), 0) for at in (0, 8))
+    folded = jnp.concatenate(pick(16, 2), 0)
+    (chi, grad_x, h), exponents = decode(first, second)
+    h = h / weight_of(None, lax.axis_index("gy"))
+    edges[pl.ds(0, 32, stride=4), :] = folded
+    for i in range(1, 4):
+        edges[pl.ds(i, 32, stride=4), :] = pltpu.roll(folded, 128 - 32 * i, 1)
+    edge = edges[...].astype(F32) / scale_of(exponents[0], EDGE_BITS)
+    lane = iota((128, 128), 1) >> 3
+    edge48, edge96 = pltpu.roll(edge, 48, 1), pltpu.roll(edge, 96, 1)
+    after = jnp.where(lane == 7, edge48, pltpu.roll(chi, 120, 1))
+    after = jnp.where(lane == 15, edge96, after)
+    before = jnp.where(lane == 0, edge, pltpu.roll(chi, 8, 1))
+    before = jnp.where(lane == 8, edge48, before)
+    left, right = packed_of(chi, (after - before) * 0.5), packed_of(grad_x, h)
+    low = low_half()
     oy = oy_of()
     slope = turned([twist[2] * left[c] for c in range(2)])
     third = tuple(jnp.where(low, slope[c], oy * right[c]) for c in range(2))
@@ -435,12 +535,15 @@
     spread = call(splat_body, "splat", [(GY, 8, 256)], route, target_here, zf)
     got = swap(spread, "gy")
     y_args = (table["y_rows"], table["y_lanes"], table["ty"])
-    spread = call(forward_y_body, "forward_y", [(GX, 24, 128)], got, *y_args)
+    words = jax.ShapeDtypeStruct((GX, 16, 128), jnp.int32)
+    spread = call(forward_y_body, "forward_y", [words], got, *y_args)
     got = swap(spread, "gx")
     x_args = (table["x_rows"], table["x_lanes"], table["tx"], table["mirror"])
-    spread = call(spectrum_body, "spectrum", [(GX, 16, 256)], got, *x_args)
-    got = swap(spread, "gx")
-    spread = call(inverse_y_body, "inverse_y", [(GY, 8, 384)], got, *y_args)
+    words = jax.ShapeDtypeStruct((GX * ROWS, 128), jnp.int32)
+    edges = (pltpu.VMEM((128, 128), jnp.int32),)
+    spread = call(spectrum_body, "spectrum", [words], got, *x_args, scratch=edges)
+    got = swap(spread.reshape(GX, ROWS, 1, 128), "gx").reshape(words.shape)
+    spread = call(inverse_y_body, "inverse_y", [(GY, 8, 384)], got, *y_args, scratch=edges)
     got = swap(spread, "gy")
     chi, slope, picked = call(
         pick_body, "pick", [brick, (3,) + brick, message], got, table["zb"], route

time: 119 us -> 114 us (0.958)
  blocking collectives: 108 us -> 102 us
  Pallas kernels: 9.78 us -> 11.4 us
    all_to_all x6, blocking collectives: 108 us -> 102 us  [swap(): return lax.all_to_all(x, axis, split_axis=0, concat_axis=0, tiled=True)]
    pallas_call x7, Pallas kernels: 9.78 us -> 11.4 us  [call(): pl.pallas_call(body, name=name, out_shape=shapes[0] if single else shapes...]
where the time goes in v3:
time: 114 us
  blocking collectives  102 us (89%)
  Pallas kernels  11.4 us (10%)
    all_to_all x6, blocking collectives, swap(): return lax.all_to_all(x, axis, split_axis=0, concat_axis=0, tiled=True)  102 us
    pallas_call x7, Pallas kernels, call(): pl.pallas_call(body, name=name, out_shape=shapes[0] if single else shapes...  11.4 us

profile of v3, /device:TPU:1, one launch (start us, length us, event | category | flops | bytes accessed | tf_op | source)
XLA Modules:
  0.0 114.1 jit_solution(4668587946994371871)
XLA Ops:
  0.6 1.1 route.1
  1.7 17.0 %all_to_all.30.route = f32[32,4,128]{2,1,0:T(4,128)S(1)} all-to-all(f32[32,4,128]{2,1,0:T(4,128)S(1)} %get-tuple-element.9), channel_id=1, replica_groups=mesh['gx'=16,'gy'=32] {'gy'}, dimensions={0} | all-to-all | bytes 131072 | tf_op jit(solution)/shard_map/all_to_all | solution.py:506
  18.7 1.3 %splat.1 = f32[32,8,256]{2,1,0:T(8,128)S(1)} custom-call(f32[32,4,128]{2,1,0:T(4,128)S(1)} %all_to_all.30.route, f32[8,8,256]{2,1,0:T(8,128)S(1)} %get-tuple-element.10.target, bf16[2,256,256]{2,1,0:T(8,128)(2,1)S(1)} %get-tuple-element.11.zf), custom_call_target="tpu_custom_call" | custom-call | tf_op jit(solution)/shard_map/splat/pallas_call | solution.py:490
  20.0 0.0 copy-start
  20.0 0.0 copy-start.1
  20.0 12.6 %all_to_all.31.got = f32[32,8,256]{2,1,0:T(8,128)S(1)} all-to-all(f32[32,8,256]{2,1,0:T(8,128)S(1)} %splat.1), channel_id=1, replica_groups=mesh['gx'=16,'gy'=32] {'gy'}, dimensions={0} | all-to-all | bytes 524288 | tf_op jit(solution)/shard_map/all_to_all | solution.py:506
  32.6 0.0 copy-done.2
  32.7 0.0 copy-start.5
  32.7 0.0 copy-start.6
  32.7 0.0 copy-start.7
  32.7 1.2 %forward_y.1 = s32[16,16,128]{2,1,0:T(8,128)S(1)} custom-call(f32[32,8,256]{2,1,0:T(8,128)S(1)} %all_to_all.31.got, bf16[2,256,256]{2,1,0:T(8,128)(2,1)S(1)} %copy-done, bf16[2,128,256]{2,1,0:T(8,128)(2,1)S(1)} %copy-done.2, f32[3,128,128]{2,1,0:T(8,128)S(1)} %copy-done.1), custom_call_target="tpu_custom_call" | custom-call | tf_op jit(solution)/shard_map/forward_y/pallas_call | solution.py:490
  33.9 0.0 copy-start.3
  34.0 25.8 %all_to_all.32.got = s32[16,16,128]{2,1,0:T(8,128)S(1)} all-to-all(s32[16,16,128]{2,1,0:T(8,128)S(1)} %forward_y.1), channel_id=1, replica_groups=mesh['gx'=16,'gy'=32] {'gx'}, dimensions={0} | all-to-all | bytes 262144 | tf_op jit(solution)/shard_map/all_to_all | solution.py:506
  59.7 0.0 copy-done.7
  59.7 0.0 copy-done.3
  59.8 3.0 %spectrum.1 = s32[288,128]{1,0:T(8,128)S(1)} custom-call(s32[16,16,128]{2,1,0:T(8,128)S(1)} %all_to_all.32.got, bf16[2,256,256]{2,1,0:T(8,128)(2,1)S(1)} %copy-done.3, bf16[2,128,256]{2,1,0:T(8,128)(2,1)S(1)} %copy-done.7, f32[2,128,128]{2,1,0:T(8,128)S(1)} %copy-done.6, bf16[512,128]{1,0:T(8,128)(2,1)S(1)} %copy-done.5), custom_call_target="tpu_custom_call" | custom-call | tf_op jit(solution)/shard_map/spectrum/pallas_call | solution.py:490
  62.7 18.4 %all_to_all.33 = s32[16,18,1,128]{3,2,1,0:T(1,128)S(1)} all-to-all(s32[16,18,1,128]{3,2,1,0:T(1,128)S(1)} %bitcast.6), channel_id=1, replica_groups=mesh['gx'=16,'gy'=32] {'gx'}, dimensions={0} | all-to-all | bytes 294912 | tf_op jit(solution)/shard_map/all_to_all | solution.py:506
  81.1 1.8 %inverse_y.1 = f32[32,8,384]{2,1,0:T(8,128)S(1)} custom-call(s32[288,128]{1,0:T(8,128)S(1)} %bitcast.5, bf16[2,256,256]{2,1,0:T(8,128)(2,1)S(1)} %copy-done, bf16[2,128,256]{2,1,0:T(8,128)(2,1)S(1)} %copy-done.2, f32[3,128,128]{2,1,0:T(8,128)S(1)} %copy-done.1), custom_call_target="tpu_custom_call" | custom-call | tf_op jit(solution)/shard_map/inverse_y/pallas_call | solution.py:490
  82.9 0.0 copy-start.4
  82.9 17.5 %all_to_all.34.got = f32[32,8,384]{2,1,0:T(8,128)S(1)} all-to-all(f32[32,8,384]{2,1,0:T(8,128)S(1)} %inverse_y.1), channel_id=1, replica_groups=mesh['gx'=16,'gy'=32] {'gy'}, dimensions={0} | all-to-all | bytes 786432 | tf_op jit(solution)/shard_map/all_to_all | solution.py:506
  100.4 1.6 %pick.1 = (f32[8,8,256]{2,1,0:T(8,128)}, f32[3,8,8,256]{3,2,1,0:T(8,128)}, f32[32,4,128]{2,1,0:T(4,128)S(1)}) custom-call(f32[32,8,384]{2,1,0:T(8,128)S(1)} %all_to_all.34.got, bf16[2,256,256]{2,1,0:T(8,128)(2,1)S(1)} %copy-done.4, f32[32,4,128]{2,1,0:T(4,128)S(1)} %all_to_all.30.route), custom_call_target="tpu_custom_call" | custom-call | tf_op jit(solution)/shard_map/pick/pallas_call | solution.py:490
  102.0 0.0 copy-start.8
  102.0 10.7 %all_to_all.35.got = f32[32,4,128]{2,1,0:T(4,128)S(1)} all-to-all(f32[32,4,128]{2,1,0:T(4,128)S(1)} %get-tuple-element.14), channel_id=1, replica_groups=mesh['gx'=16,'gy'=32] {'gy'}, dimensions={0} | all-to-all | bytes 131072 | tf_op jit(solution)/shard_map/all_to_all | solution.py:506
  112.7 1.4 %deliver.1 = f32[3,32,64]{2,1,0:T(8,128)} custom-call(s32[32]{0:T(128)S(1)} %bitcast.8, f32[32,4,128]{2,1,0:T(4,128)S(1)} %all_to_all.35.got), custom_call_target="tpu_custom_call" | custom-call | tf_op jit(solution)/shard_map/deliver/pallas_call | solution.py:490
  (7 shorter events, 0.0 us)
Async XLA Ops:
  18.7 14.0 %copy-start.2 = (bf16[2,128,256]{2,1,0:T(8,128)(2,1)S(1)}, bf16[2,128,256]{2,1,0:T(8,128)(2,1)}, u32[]{:S(2)}) copy-start(bf16[2,128,256]{2,1,0:T(8,128)(2,1)} %constant.22.clone.lanes) | copy-start | bytes 393220
  20.0 12.7 %copy-start = (bf16[2,256,256]{2,1,0:T(8,128)(2,1)S(1)}, bf16[2,256,256]{2,1,0:T(8,128)(2,1)}, u32[]{:S(2)}) copy-start(bf16[2,256,256]{2,1,0:T(8,128)(2,1)} %constant.20.clone.rows) | copy-start | bytes 786436
  20.0 12.6 %copy-start.1 = (f32[3,128,128]{2,1,0:T(8,128)S(1)}, f32[3,128,128]{2,1,0:T(8,128)}, u32[]{:S(2)}) copy-start(f32[3,128,128]{2,1,0:T(8,128)} %constant.24.clone.twist) | copy-start | bytes 589828
  32.7 27.1 %copy-start.5 = (bf16[512,128]{1,0:T(8,128)(2,1)S(1)}, bf16[512,128]{1,0:T(8,128)(2,1)}, u32[]{:S(2)}) copy-start(bf16[512,128]{1,0:T(8,128)(2,1)} %constant.26.clone.mirror) | copy-start | bytes 393220
  32.7 27.1 %copy-start.6 = (f32[2,128,128]{2,1,0:T(8,128)S(1)}, f32[2,128,128]{2,1,0:T(8,128)}, u32[]{:S(2)}) copy-start(f32[2,128,128]{2,1,0:T(8,128)} %constant.25.clone.twist) | copy-start | bytes 393220
  32.7 27.1 %copy-start.7 = (bf16[2,128,256]{2,1,0:T(8,128)(2,1)S(1)}, bf16[2,128,256]{2,1,0:T(8,128)(2,1)}, u32[]{:S(2)}) copy-start(bf16[2,128,256]{2,1,0:T(8,128)(2,1)} %constant.23.clone.lanes) | copy-start | bytes 393220
  33.9 25.8 %copy-start.3 = (bf16[2,256,256]{2,1,0:T(8,128)(2,1)S(1)}, bf16[2,256,256]{2,1,0:T(8,128)(2,1)}, u32[]{:S(2)}) copy-start(bf16[2,256,256]{2,1,0:T(8,128)(2,1)} %constant.21.clone.rows) | copy-start | bytes 786436
  82.9 17.5 %copy-start.4 = (bf16[2,256,256]{2,1,0:T(8,128)(2,1)S(1)}, bf16[2,256,256]{2,1,0:T(8,128)(2,1)}, u32[]{:S(2)}) copy-start(bf16[2,256,256]{2,1,0:T(8,128)(2,1)} %constant.19.clone.zb) | copy-start | bytes 786436
  102.0 10.7 %copy-start.8 = (s32[32,1]{0,1:T(1,128)S(1)}, s32[32,1]{0,1:T(1,128)}, u32[]{:S(2)}) copy-start(s32[32,1]{0,1:T(1,128)} %param.14) | copy-start | bytes 388

commit v4 on v3

--- a/solution.py
+++ b/solution.py
@@ -19,10 +19,10 @@
 F32, BF16 = jnp.float32, jnp.bfloat16
 
 
-def halves(table):
+def halves(table, axis):
     high = table.astype(ml_dtypes.bfloat16)
     low = (table - high.astype(np.float64)).astype(ml_dtypes.bfloat16)
-    return np.stack([high, low])
+    return np.concatenate([high, low, high], axis)
 
 
 def unit(turns):
@@ -76,15 +76,19 @@
                         src = f * 64 + (-a - m) % 8 * 8 + (-b - n) % 8
                         mirror[m, n, src, f * 64 + a * 8 + b] = 1.0
     return dict(
-        zf=halves(order(zf)),
-        zb=halves(order(zb)),
-        y_rows=halves(y_rows),
-        x_rows=halves(x_rows),
-        y_lanes=halves(y_lanes),
-        x_lanes=halves(x_lanes),
+        zf=halves(order(zf), 1),
+        zb=halves(order(zb), 0),
+        y_rows=halves(y_rows, 1),
+        x_rows=halves(x_rows, 1),
+        y_back=halves(y_rows.T, 1),
+        x_back=halves(x_rows.T, 1),
+        y_lanes=halves(y_lanes, 0),
+        x_lanes=halves(x_lanes, 0),
         ty=twist(ty, slope_y),
         tx=twist(tx, slope_x)[:2],
-        mirror=mirror.reshape(512, 128).astype(ml_dtypes.bfloat16),
+        mirror=np.tile(np.concatenate([mirror[:, 0], mirror[:, 1]], 2), (1, 2, 1)).astype(
+            ml_dtypes.bfloat16
+        ),
     )
 
 
@@ -100,14 +104,19 @@
     return lax.dot_general(a, b, (((ca,), (cb,)), ((), ())), preferred_element_type=F32)
 
 
-def mm3(a, b, ca=1, cb=0):
-    return mm(a[0], b[0], ca, cb) + (mm(a[0], b[1], ca, cb) + mm(a[1], b[0], ca, cb))
+def thrice(x, axis):
+    high, low = split(x)
+    return jnp.concatenate([high, high, low], axis)
+
+
+def twice(x, axis):
+    return jnp.concatenate(split(x), axis)
 
 
 def lanes_of(pairs, table, sign):
     count, rows = len(pairs), pairs[0][0].shape[0]
     stacked = jnp.concatenate([p[0] for p in pairs] + [p[1] for p in pairs], 0)
-    out = mm3(split(stacked), table)
+    out = mm(thrice(stacked, 1), table[...])
     result = []
     for i in range(count):
         a = out[i * rows : (i + 1) * rows]
@@ -132,10 +141,6 @@
 
 def whole_of(pairs):
     return tuple(jnp.concatenate([p[c] for p in pairs], 1) for c in range(2))
-
-
-def table_of(ref):
-    return ref[0], ref[1]
 
 
 def iota(shape, dim):
@@ -187,7 +192,7 @@
         hot = jnp.where(levels == level, 1.0, 0.0).astype(BF16)
         field = field + mm(weighted, hot, 1, 1)
     both = jnp.concatenate([field, target[...].reshape(BX * BY, NZ)], 0)
-    spread = mm3(table_of(zf), split(both), 1, 1)
+    spread = mm(zf[...], thrice(both, 1), 1, 1)
     right = spread[:, 128:]
     right = jnp.where(iota((NZ, 128), 1) < 64, right * kz_of(NZ), right)
     out[...] = jnp.concatenate([spread[:, :128], right], 1).reshape(out.shape)
@@ -211,7 +216,9 @@
     gx = row >> 3 if gx is None else gx
     uy, _ = odd(ky_of(gx, row, lane), NY)
     uz = (KZ * gy + (row & 3)).astype(F32)
-    return jnp.sqrt(uy * uy + uz * uz + 1.0)
+    square = uy * uy + uz * uz + 1.0
+    small = lax.rsqrt(square)
+    return small, square * small
 
 
 BITS, SPLIT, BIAS, EDGE_BITS = 20, 11, 128, 30
@@ -252,20 +259,20 @@
         exponents.append(jnp.sum(here, 1, keepdims=True).astype(jnp.int32) - BIAS)
     a, b = first >> SPLIT, second >> SPLIT
     c = (((second & 0x3FF) << 22) >> SPLIT) | (first & 0x7FF)
-    fields = [x.astype(F32) / scale_of(e, BITS) for x, e in zip((a, b, c), exponents)]
+    fields = [x.astype(F32) * (1.0 / scale_of(e, BITS)) for x, e in zip((a, b, c), exponents)]
     return fields, exponents
 
 
 def forward_y_body(got, rows, lanes, twist, out):
-    x = mm3(table_of(rows), split(got[...].reshape(NZ, NZ)))
+    x = mm(rows[...], thrice(got[...].reshape(NZ, NZ), 0))
     pairs = twisted(halves_of(x[:128], x[128:]), twist, 1)
-    left, right = lanes_of(pairs, table_of(lanes), 1)
+    left, right = lanes_of(pairs, lanes, 1)
     low = low_half()
     oy = oy_of()
     real, imag = (jnp.where(low, left[c], oy * left[c] + swapped(right[c])) for c in range(2))
     target = jnp.where(low, swapped(right[0]), right[1])
     part_x, part_yz = packed_of(real, imag)
-    fields = (part_x, part_yz / weight_of(None, lax.axis_index("gy")), target)
+    fields = (part_x, part_yz * weight_of(None, lax.axis_index("gy"))[0], target)
     first, second = encode(fields, [exponent_of(x) for x in fields])
     out[:, 0:8, :] = first.reshape(GX, 8, 128)
     out[:, 8:16, :] = second.reshape(GX, 8, 128)
@@ -292,45 +299,36 @@
 
 
 def mirrored(pair, gx, mirror):
-    row, other = iota((32, 128), 0), iota((32, 128), 1)
-    swap = jnp.where(gx == 0, 0, 4)
-    partner = (((16 - (row >> 1)) & 15) << 3) | (((row & 1) << 2) ^ swap)
-    moves = jnp.where(other == partner, 1.0, 0.0).astype(BF16)
-    high, low = split(jnp.concatenate(pair, 1))
-    moved = mm(moves, high) + mm(moves, low)
-    moved = jnp.concatenate([moved[:, :128], moved[:, 128:]], 0)
-    row = iota((64, 128), 0) & 31
-    half_x = (row >> 1) == 8
-    half_y = ((row & 1) == 1) & (gx == 0)
-    cases = [
-        jnp.where((half_x == (case >= 2)) & (half_y == (case % 2 == 1)), moved, 0.0)
-        for case in range(4)
-    ]
-    high, low = split(jnp.concatenate(cases, 1))
-    turned_back = mm(high, mirror[...]) + mm(low, mirror[...])
-    high, low = split(jnp.concatenate([turned_back[:32], -turned_back[32:]], 1))
-    row, other = iota((128, 32), 0), iota((128, 32), 1)
-    home = jnp.where(row == other * 4, 1.0, 0.0).astype(BF16)
-    total = mm(home, high) + mm(home, low)
-    return total[:, :128], total[:, 128:]
+    x = jnp.concatenate(pair, 0).reshape(2, GX, 8, 128)
+    x = jnp.concatenate([x[:, (GX - i) % GX : (GX - i) % GX + 1] for i in range(GX)], 1)
+    x = x.reshape(2 * GX, 8, 128)
+    x = jnp.where(gx == 0, x, jnp.concatenate([x[:, 4:], x[:, :4]], 1)).reshape(256, 128)
+    special = jnp.concatenate([x[64:72], x[192:200]], 0)
+    whole, special = (mm(twice(part, 1), mirror[i]) for i, part in enumerate((x, special)))
+    parts = [whole[:64], special[:8], whole[72:192], special[8:], whole[200:]]
+    whole = jnp.concatenate(parts, 0)
+    half_y = (((iota((256, 128), 0) >> 2) & 1) == 1) & (gx == 0)
+    whole = jnp.where(half_y, whole[:, 128:], whole[:, :128])
+    return whole[:128], -whole[128:]
 
 
 def turned(pair):
     return -pair[1], pair[0]
 
 
-def spectrum_body(got, rows, lanes, twist, mirror, out, edges):
+def spectrum_body(got, rows, back, lanes, twist, mirror, out, edges):
     gx, gy = lax.axis_index("gx"), lax.axis_index("gy")
     words = (got[:, i * 8 : i * 8 + 8, :].reshape(128, 128) for i in range(2))
     (part_x, part_yz, target), _ = decode(*words)
-    part_yz = part_yz * weight_of(gx, gy)
+    weight = weight_of(gx, gy)[1]
+    part_yz = part_yz * weight
     x = [*packed_of(part_x, part_yz), target, swapped(target)]
     x = [part.reshape(GX, 8, 128) for part in x]
     x = [jnp.concatenate(x[i : i + 2], 1).reshape(NZ, 128) for i in (0, 2)]
     x = jnp.concatenate(x, 1)
-    x = mm3(table_of(rows), split(x))
+    x = mm(rows[...], thrice(x, 0))
     pairs = twisted(halves_of(x[:128], x[128:]), twist, 1)
-    left, right = lanes_of(pairs, table_of(lanes), 1)
+    left, right = lanes_of(pairs, lanes, 1)
     ox, mean, diff = filters(gx, gy)
     low = low_half()
 
@@ -347,9 +345,9 @@
     ]
     h = turned(h)
     pairs = [chi, tuple(jnp.where(low, ox * h[c], h[c]) for c in range(2))]
-    pairs = twisted(lanes_of(pairs, table_of(lanes), -1), twist, -1)
+    pairs = twisted(lanes_of(pairs, lanes, -1), twist, -1)
     both = jnp.concatenate(whole_of(pairs), 0)
-    x = mm3(table_of(rows), split(both), 0, 0).reshape(GX, 16, NZ)
+    x = mm(back[...], thrice(both, 0)).reshape(GX, 16, NZ)
     chi, _ = packed_of(*(x[:, c : c + 8, :128].reshape(128, 128) for c in (0, 8)))
     gradients = packed_of(*(x[:, c : c + 8, 128:].reshape(128, 128) for c in (0, 8)))
 
@@ -361,7 +359,7 @@
     edge = jnp.where(lane == 2, pltpu.roll(below, 24, 1), edge)
     edge = jnp.where(lane == 3, pltpu.roll(above, 88, 1), edge)
     grad_x, h = gradients
-    fields = (chi, grad_x, h * weight_of(gx, gy))
+    fields = (chi, grad_x, h * weight)
     exponents = [exponent_of(x) for x in fields]
     exponents[0] = jnp.maximum(exponents[0], exponent_of(edge))
     first, second = encode(fields, exponents)
@@ -377,16 +375,16 @@
         out[at + 16 : at + 18, :] = folded[g * 2 : g * 2 + 2]
 
 
-def inverse_y_body(got, rows, lanes, twist, out, edges):
+def inverse_y_body(got, back, lanes, twist, out, edges):
     pick = lambda at, count: [got[g * ROWS + at : g * ROWS + at + count, :] for g in range(GX)]
     first, second = (jnp.concatenate(pick(at, 8), 0) for at in (0, 8))
     folded = jnp.concatenate(pick(16, 2), 0)
     (chi, grad_x, h), exponents = decode(first, second)
-    h = h / weight_of(None, lax.axis_index("gy"))
+    h = h * weight_of(None, lax.axis_index("gy"))[0]
     edges[pl.ds(0, 32, stride=4), :] = folded
     for i in range(1, 4):
         edges[pl.ds(i, 32, stride=4), :] = pltpu.roll(folded, 128 - 32 * i, 1)
-    edge = edges[...].astype(F32) / scale_of(exponents[0], EDGE_BITS)
+    edge = edges[...].astype(F32) * (1.0 / scale_of(exponents[0], EDGE_BITS))
     lane = iota((128, 128), 1) >> 3
     edge48, edge96 = pltpu.roll(edge, 48, 1), pltpu.roll(edge, 96, 1)
     after = jnp.where(lane == 7, edge48, pltpu.roll(chi, 120, 1))
@@ -398,10 +396,10 @@
     oy = oy_of()
     slope = turned([twist[2] * left[c] for c in range(2)])
     third = tuple(jnp.where(low, slope[c], oy * right[c]) for c in range(2))
-    pairs = lanes_of([left, right, third], table_of(lanes), -1)
+    pairs = lanes_of([left, right, third], lanes, -1)
     pairs = twisted(pairs, twist, -1)
     both = jnp.concatenate(whole_of(pairs), 0)
-    out[...] = mm3(table_of(rows), split(both), 0, 0).reshape(out.shape)
+    out[...] = mm(back[...], thrice(both, 0)).reshape(out.shape)
 
 
 def pick_body(got, zb, route, chi, slope, picked):
@@ -409,7 +407,7 @@
     middle = fields[:, 128:256]
     middle = jnp.where(iota((NZ, 128), 1) < 64, middle, middle * kz_of(NZ))
     fields = jnp.concatenate([fields[:, :128], middle, fields[:, 256:]], 1)
-    values = mm3(split(fields), table_of(zb), 0, 0)
+    values = mm(thrice(fields, 0), zb[...], 0, 0)
     cells = BX * BY
     solid, slope_x, grad_x, grad_z, slope_y, grad_y = (
         values[i * cells : (i + 1) * cells] for i in range(6)
@@ -420,14 +418,14 @@
     slope[1] = slope_y.reshape(brick)
     slope_z = (pltpu.roll(solid, NZ - 1, 1) - pltpu.roll(solid, 1, 1)) * 0.5
     slope[2] = slope_z.reshape(brick)
-    high, low = split(jnp.concatenate([grad_x, grad_y, grad_z], 0))
+    grads = twice(jnp.concatenate([grad_x, grad_y, grad_z], 0), 1)
     width = STEP * CAP * POINTS
     columns = iota((cells, width), 0).astype(F32)
     levels = iota((NZ, width), 0).astype(F32)
     for first in range(0, GY, STEP):
         _, column, level = places(route, first, STEP)
         hot = jnp.where(levels == level, 1.0, 0.0).astype(BF16)
-        at_level = mm(high, hot) + mm(low, hot)
+        at_level = mm(grads, jnp.concatenate([hot, hot], 0))
         here = columns == column
         lines = [
             jnp.sum(jnp.where(here, at_level[j * cells : (j + 1) * cells], 0.0), 0, keepdims=True)
@@ -439,16 +437,22 @@
 
 
 def route_body(*refs):
-    sources, (out, target, zf), (owners, normals, cells, count, sems) = refs[:5], refs[5:8], refs[8:]
+    sources, (out, target, zf, row), (owners, normals, cells, count, sems) = (
+        refs[:5],
+        refs[5:9],
+        refs[9:],
+    )
     fetches = [
         pltpu.make_async_copy(source, place, sems.at[i])
-        for i, (source, place) in enumerate(zip(sources, (owners, normals, cells, target, zf)))
+        for i, (source, place) in enumerate(
+            zip(sources + sources[:1], (owners, normals, cells, target, zf, row))
+        )
     ]
     for fetch in fetches:
         fetch.start()
-    row = iota((4, 128), 0)
+    line = iota((4, 128), 0)
     half = iota((4, 128), 1) >> 6
-    empty = jnp.where(row == 3, -1.0, 0.0)
+    empty = jnp.where(line == 3, -1.0, 0.0)
     for o in range(GY):
         out[o] = empty
         count[o] = 0
@@ -456,7 +460,7 @@
         fetch.wait()
     parts = [normals[j].astype(F32) for j in range(3)] + [cells[...].astype(F32)]
     for b in range(BLOCKS):
-        owner = owners[b]
+        owner = owners[0, b]
         rank = count[owner]
         count[owner] = rank + 1
         value = jnp.concatenate([p[b : b + 1] for p in parts], 0)
@@ -466,17 +470,24 @@
         fetch.wait()
 
 
-def return_body(owners, got, out, count, rows):
-    for o in range(GY):
-        count[o] = 0
-    for b in range(BLOCKS):
-        owner = owners[b]
-        rank = count[owner]
-        count[owner] = rank + 1
-        value = got[owner]
-        rows[b] = jnp.where(rank == 0, value, pltpu.roll(value, 64, 1))
+def return_body(owners, got, out):
+    square = (BLOCKS, BLOCKS)
+    row, column = iota(square, 0), iota(square, 1)
+    across = jnp.broadcast_to(owners[...], square)
+    down = jnp.sum(jnp.where(row == column, across, 0), 1, keepdims=True)
+    earlier = (down == across) & (column < row)
+    rank = jnp.sum(jnp.where(earlier, 1, 0), 1, keepdims=True)
+    hot = [jnp.where((down == column) & (rank == r), 1.0, 0.0) for r in range(CAP)]
+    hot = jnp.concatenate(hot, 0).astype(BF16)
+    x = jnp.concatenate([got[:, j, :] for j in range(3)], 1)
+    parts = []
+    for _ in range(3):
+        parts.append(x.astype(BF16))
+        x = x - parts[-1].astype(F32)
+    total = mm(jnp.concatenate([hot] * 3, 1), jnp.concatenate(parts, 0))
     for j in range(3):
-        out[j] = rows[:, j, :][:, :64]
+        lines = total[:, j * 128 : (j + 1) * 128]
+        out[j] = (lines[:BLOCKS] + swapped(lines[BLOCKS:]))[:, :POINTS]
 
 
 VMEM = pl.BlockSpec(memory_space=pltpu.VMEM)
@@ -508,7 +519,7 @@
 
 def local(normals, owners, cells, target):
     table = {k: jnp.asarray(v) for k, v in TABLES.items()}
-    owner = owners.reshape(BLOCKS)
+    owner = owners.reshape(1, BLOCKS)
     counts = pltpu.SMEM((GY,), jnp.int32)
     brick = (BX, BY, NZ)
     message = (GY, 4, CAP * POINTS)
@@ -519,14 +530,15 @@
         pltpu.VMEM(by_part.shape, BF16),
         pltpu.VMEM(cells.shape, jnp.int32),
         counts,
-        pltpu.SemaphoreType.DMA((5,)),
+        pltpu.SemaphoreType.DMA((6,)),
     )
     tables_z = jax.ShapeDtypeStruct(table["zf"].shape, BF16)
     sources = (owner, by_part, cells, target, table["zf"])
-    sent, target_here, zf = call(
+    row = jax.ShapeDtypeStruct(owner.shape, jnp.int32)
+    sent, target_here, zf, owner_here = call(
         route_body,
         "route",
-        [message, brick, tables_z],
+        [message, brick, tables_z, row],
         *map(kept, sources),
         specs=[HBM] * 5,
         scratch=scratch,
@@ -534,30 +546,23 @@
     route = swap(sent, "gy")
     spread = call(splat_body, "splat", [(GY, 8, 256)], route, target_here, zf)
     got = swap(spread, "gy")
-    y_args = (table["y_rows"], table["y_lanes"], table["ty"])
+    y_args = (table["y_lanes"], table["ty"])
     words = jax.ShapeDtypeStruct((GX, 16, 128), jnp.int32)
-    spread = call(forward_y_body, "forward_y", [words], got, *y_args)
+    spread = call(forward_y_body, "forward_y", [words], got, table["y_rows"], *y_args)
     got = swap(spread, "gx")
-    x_args = (table["x_rows"], table["x_lanes"], table["tx"], table["mirror"])
+    x_args = [table[k] for k in ("x_rows", "x_back", "x_lanes", "tx", "mirror")]
     words = jax.ShapeDtypeStruct((GX * ROWS, 128), jnp.int32)
     edges = (pltpu.VMEM((128, 128), jnp.int32),)
     spread = call(spectrum_body, "spectrum", [words], got, *x_args, scratch=edges)
     got = swap(spread.reshape(GX, ROWS, 1, 128), "gx").reshape(words.shape)
+    y_args = (table["y_back"],) + y_args
     spread = call(inverse_y_body, "inverse_y", [(GY, 8, 384)], got, *y_args, scratch=edges)
     got = swap(spread, "gy")
     chi, slope, picked = call(
         pick_body, "pick", [brick, (3,) + brick, message], got, table["zb"], route
     )
     returned = swap(picked, "gy")
-    normal_grad = call(
-        return_body,
-        "deliver",
-        [(3, BLOCKS, POINTS)],
-        owner,
-        returned,
-        specs=[SMEM, VMEM],
-        scratch=(counts, pltpu.VMEM((BLOCKS, 4, CAP * POINTS), F32)),
-    )
+    normal_grad = call(return_body, "deliver", [(3, BLOCKS, POINTS)], owner_here, returned)
     return chi, slope, jnp.moveaxis(normal_grad, 0, 1)
 
 

time: 114 us -> 113 us (level)
  no operation moved by 1% of the time
where the time goes in v4:
time: 113 us
  blocking collectives  102 us (90%)
  Pallas kernels  10.3 us (9%)
    all_to_all x6, blocking collectives, swap(): return lax.all_to_all(x, axis, split_axis=0, concat_axis=0, tiled=True)  102 us
    pallas_call x7, Pallas kernels, call(): pl.pallas_call(body, name=name, out_shape=shapes[0] if single else shapes...  10.3 us

profile of v4, /device:TPU:1, one launch (start us, length us, event | category | flops | bytes accessed | tf_op | source)
XLA Modules:
  0.0 113.0 jit_solution(12880007445868303396)
XLA Ops:
  0.6 1.1 route.1
  1.8 17.0 %all_to_all.30.route = f32[32,4,128]{2,1,0:T(4,128)S(1)} all-to-all(f32[32,4,128]{2,1,0:T(4,128)S(1)} %get-tuple-element.10), channel_id=1, replica_groups=mesh['gx'=16,'gy'=32] {'gy'}, dimensions={0} | all-to-all | bytes 131072 | tf_op jit(solution)/shard_map/all_to_all | solution.py:517
  18.7 1.3 %splat.1 = f32[32,8,256]{2,1,0:T(8,128)S(1)} custom-call(f32[32,4,128]{2,1,0:T(4,128)S(1)} %all_to_all.30.route, f32[8,8,256]{2,1,0:T(8,128)S(1)} %get-tuple-element.11.target, bf16[256,768]{1,0:T(8,128)(2,1)S(1)} %get-tuple-element.12.zf), custom_call_target="tpu_custom_call" | custom-call | tf_op jit(solution)/shard_map/splat/pallas_call | solution.py:501
  20.1 0.0 copy-start
  20.1 0.0 copy-start.1
  20.1 12.6 %all_to_all.31.got = f32[32,8,256]{2,1,0:T(8,128)S(1)} all-to-all(f32[32,8,256]{2,1,0:T(8,128)S(1)} %splat.1), channel_id=1, replica_groups=mesh['gx'=16,'gy'=32] {'gy'}, dimensions={0} | all-to-all | bytes 524288 | tf_op jit(solution)/shard_map/all_to_all | solution.py:517
  32.7 0.0 copy-start.3
  32.7 0.0 copy-start.4
  32.7 0.0 copy-start.8
  32.7 0.0 copy-start.9
  32.8 1.2 %forward_y.1 = s32[16,16,128]{2,1,0:T(8,128)S(1)} custom-call(f32[32,8,256]{2,1,0:T(8,128)S(1)} %all_to_all.31.got, bf16[256,768]{1,0:T(8,128)(2,1)S(1)} %copy-done.5, bf16[384,256]{1,0:T(8,128)(2,1)S(1)} %copy-done.1, f32[3,128,128]{2,1,0:T(8,128)S(1)} %copy-done), custom_call_target="tpu_custom_call" | custom-call | tf_op jit(solution)/shard_map/forward_y/pallas_call | solution.py:501
  33.9 0.0 copy-start.7
  33.9 25.8 %all_to_all.32.got = s32[16,16,128]{2,1,0:T(8,128)S(1)} all-to-all(s32[16,16,128]{2,1,0:T(8,128)S(1)} %forward_y.1), channel_id=1, replica_groups=mesh['gx'=16,'gy'=32] {'gx'}, dimensions={0} | all-to-all | bytes 262144 | tf_op jit(solution)/shard_map/all_to_all | solution.py:517
  59.7 0.0 copy-done.8
  59.7 0.0 copy-done.9
  59.7 0.0 copy-start.6
  59.8 2.4 %spectrum.1 = s32[288,128]{1,0:T(8,128)S(1)} custom-call(s32[16,16,128]{2,1,0:T(8,128)S(1)} %all_to_all.32.got, bf16[256,768]{1,0:T(8,128)(2,1)S(1)} %copy-done.4, bf16[256,768]{1,0:T(8,128)(2,1)S(1)} %copy-done.3, bf16[384,256]{1,0:T(8,128)(2,1)S(1)} %copy-done.8, f32[2,128,128]{2,1,0:T(8,128)S(1)} %copy-done.9, bf16[2,256,256]{2,1,0:T(8,128)(2,1)S(1)} %copy-done.7), custom_call_target="tpu_custom_call" | custom-call | tf_op jit(solution)/shard_map/spectrum/pallas_call | solution.py:501
  62.1 18.3 %all_to_all.33 = s32[16,18,1,128]{3,2,1,0:T(1,128)S(1)} all-to-all(s32[16,18,1,128]{3,2,1,0:T(1,128)S(1)} %bitcast.5), channel_id=1, replica_groups=mesh['gx'=16,'gy'=32] {'gx'}, dimensions={0} | all-to-all | bytes 294912 | tf_op jit(solution)/shard_map/all_to_all | solution.py:517
  80.5 1.7 %inverse_y.1 = f32[32,8,384]{2,1,0:T(8,128)S(1)} custom-call(s32[288,128]{1,0:T(8,128)S(1)} %bitcast.6, bf16[256,768]{1,0:T(8,128)(2,1)S(1)} %copy-done.6, bf16[384,256]{1,0:T(8,128)(2,1)S(1)} %copy-done.1, f32[3,128,128]{2,1,0:T(8,128)S(1)} %copy-done), custom_call_target="tpu_custom_call" | custom-call | tf_op jit(solution)/shard_map/inverse_y/pallas_call | solution.py:501
  82.2 0.0 copy-start.2
  82.2 17.5 %all_to_all.34.got = f32[32,8,384]{2,1,0:T(8,128)S(1)} all-to-all(f32[32,8,384]{2,1,0:T(8,128)S(1)} %inverse_y.1), channel_id=1, replica_groups=mesh['gx'=16,'gy'=32] {'gy'}, dimensions={0} | all-to-all | bytes 786432 | tf_op jit(solution)/shard_map/all_to_all | solution.py:517
  99.7 1.6 %pick.1 = (f32[8,8,256]{2,1,0:T(8,128)}, f32[3,8,8,256]{3,2,1,0:T(8,128)}, f32[32,4,128]{2,1,0:T(4,128)S(1)}) custom-call(f32[32,8,384]{2,1,0:T(8,128)S(1)} %all_to_all.34.got, bf16[768,256]{1,0:T(8,128)(2,1)S(1)} %copy-done.2, f32[32,4,128]{2,1,0:T(4,128)S(1)} %all_to_all.30.route), custom_call_target="tpu_custom_call" | custom-call | tf_op jit(solution)/shard_map/pick/pallas_call | solution.py:501
  101.2 10.7 %all_to_all.35.got = f32[32,4,128]{2,1,0:T(4,128)S(1)} all-to-all(f32[32,4,128]{2,1,0:T(4,128)S(1)} %get-tuple-element.16), channel_id=1, replica_groups=mesh['gx'=16,'gy'=32] {'gy'}, dimensions={0} | all-to-all | bytes 131072 | tf_op jit(solution)/shard_map/all_to_all | solution.py:517
  112.0 1.1 deliver.1
  (9 shorter events, 0.0 us)
Async XLA Ops:
  18.7 14.0 %copy-start.5 = (bf16[256,768]{1,0:T(8,128)(2,1)S(1)}, bf16[256,768]{1,0:T(8,128)(2,1)}, u32[]{:S(2)}) copy-start(bf16[256,768]{1,0:T(8,128)(2,1)} %constant.24.clone.rows) | copy-start | bytes 1179652
  20.1 12.7 %copy-start = (f32[3,128,128]{2,1,0:T(8,128)S(1)}, f32[3,128,128]{2,1,0:T(8,128)}, u32[]{:S(2)}) copy-start(f32[3,128,128]{2,1,0:T(8,128)} %constant.30.clone.twist) | copy-start | bytes 589828
  20.1 12.6 %copy-start.1 = (bf16[384,256]{1,0:T(8,128)(2,1)S(1)}, bf16[384,256]{1,0:T(8,128)(2,1)}, u32[]{:S(2)}) copy-start(bf16[384,256]{1,0:T(8,128)(2,1)} %constant.28.clone.lanes) | copy-start | bytes 589828
  32.7 27.0 %copy-start.3 = (bf16[256,768]{1,0:T(8,128)(2,1)S(1)}, bf16[256,768]{1,0:T(8,128)(2,1)}, u32[]{:S(2)}) copy-start(bf16[256,768]{1,0:T(8,128)(2,1)} %constant.27.clone.back) | copy-start | bytes 1179652
  32.7 27.0 %copy-start.4 = (bf16[256,768]{1,0:T(8,128)(2,1)S(1)}, bf16[256,768]{1,0:T(8,128)(2,1)}, u32[]{:S(2)}) copy-start(bf16[256,768]{1,0:T(8,128)(2,1)} %constant.25.clone.rows) | copy-start | bytes 1179652
  32.7 27.0 %copy-start.8 = (bf16[384,256]{1,0:T(8,128)(2,1)S(1)}, bf16[384,256]{1,0:T(8,128)(2,1)}, u32[]{:S(2)}) copy-start(bf16[384,256]{1,0:T(8,128)(2,1)} %constant.29.clone.lanes) | copy-start | bytes 589828
  32.7 27.0 %copy-start.9 = (f32[2,128,128]{2,1,0:T(8,128)S(1)}, f32[2,128,128]{2,1,0:T(8,128)}, u32[]{:S(2)}) copy-start(f32[2,128,128]{2,1,0:T(8,128)} %constant.31.clone.twist) | copy-start | bytes 393220
  33.9 25.8 %copy-start.7 = (bf16[2,256,256]{2,1,0:T(8,128)(2,1)S(1)}, bf16[2,256,256]{2,1,0:T(8,128)(2,1)}, u32[]{:S(2)}) copy-start(bf16[2,256,256]{2,1,0:T(8,128)(2,1)} %constant.32.clone.mirror) | copy-start | bytes 786436
  59.7 20.8 %copy-start.6 = (bf16[256,768]{1,0:T(8,128)(2,1)S(1)}, bf16[256,768]{1,0:T(8,128)(2,1)}, u32[]{:S(2)}) copy-start(bf16[256,768]{1,0:T(8,128)(2,1)} %constant.26.clone.back) | copy-start | bytes 1179652
  82.2 17.5 %copy-start.2 = (bf16[768,256]{1,0:T(8,128)(2,1)S(1)}, bf16[768,256]{1,0:T(8,128)(2,1)}, u32[]{:S(2)}) copy-start(bf16[768,256]{1,0:T(8,128)(2,1)} %constant.23.clone.zb) | copy-start | bytes 1179652

commit v5 on v4

--- a/solution.py
+++ b/solution.py
@@ -151,7 +151,11 @@
     rows = jnp.concatenate([route[s] for s in range(first, first + count)], 1)
     cell = rows[3:4]
     column = jnp.floor(cell * (1.0 / NZ))
-    return rows, column, cell - column * NZ
+    return rows.astype(BF16), column.astype(BF16), (cell - column * NZ).astype(BF16)
+
+
+def hot_of(labels, values):
+    return jnp.where(labels == values, jnp.ones_like(labels), jnp.zeros_like(labels))
 
 
 def kz_of(rows):
@@ -181,16 +185,14 @@
 
 def splat_body(route, target, zf, out):
     width = STEP * CAP * POINTS
-    columns = iota((BX * BY, width), 0).astype(F32)
-    levels = iota((NZ, width), 0).astype(F32)
+    columns = iota((BX * BY, width), 0).astype(BF16)
+    levels = iota((NZ, width), 0).astype(BF16)
     field = jnp.zeros((3 * BX * BY, NZ), F32)
     for first in range(0, GY, STEP):
         rows, column, level = places(route, first, STEP)
-        here = columns == column
-        weighted = [jnp.where(here, rows[j : j + 1], 0.0) for j in range(3)]
-        weighted = jnp.concatenate(weighted, 0).astype(BF16)
-        hot = jnp.where(levels == level, 1.0, 0.0).astype(BF16)
-        field = field + mm(weighted, hot, 1, 1)
+        here = hot_of(columns, column)
+        weighted = jnp.concatenate([here * rows[j : j + 1] for j in range(3)], 0)
+        field = field + mm(weighted, hot_of(levels, level), 1, 1)
     both = jnp.concatenate([field, target[...].reshape(BX * BY, NZ)], 0)
     spread = mm(zf[...], thrice(both, 1), 1, 1)
     right = spread[:, 128:]
@@ -230,7 +232,7 @@
 
 
 def exponent_of(x):
-    top = jnp.max(jnp.abs(x), 1, keepdims=True)
+    top = jnp.broadcast_to(jnp.max(jnp.abs(x), 1, keepdims=True), x.shape)
     power = jnp.floor(jnp.log2(jnp.maximum(top, 1e-26)) + 0.001) + 1.0
     return power.astype(jnp.int32)
 
@@ -256,7 +258,8 @@
     exponents = []
     for i in range(3):
         here = jnp.where((lane >> 3) == i, bit, 0).astype(F32)
-        exponents.append(jnp.sum(here, 1, keepdims=True).astype(jnp.int32) - BIAS)
+        total = jnp.broadcast_to(jnp.sum(here, 1, keepdims=True), here.shape)
+        exponents.append(total.astype(jnp.int32) - BIAS)
     a, b = first >> SPLIT, second >> SPLIT
     c = (((second & 0x3FF) << 22) >> SPLIT) | (first & 0x7FF)
     fields = [x.astype(F32) * (1.0 / scale_of(e, BITS)) for x, e in zip((a, b, c), exponents)]
@@ -402,7 +405,7 @@
     out[...] = mm(back[...], thrice(both, 0)).reshape(out.shape)
 
 
-def pick_body(got, zb, route, chi, slope, picked):
+def pick_body(got, zb, route, chi_hbm, slope_hbm, picked, chi, slope, sems):
     fields = got[...].reshape(NZ, 384)
     middle = fields[:, 128:256]
     middle = jnp.where(iota((NZ, 128), 1) < 64, middle, middle * kz_of(NZ))
@@ -418,15 +421,21 @@
     slope[1] = slope_y.reshape(brick)
     slope_z = (pltpu.roll(solid, NZ - 1, 1) - pltpu.roll(solid, 1, 1)) * 0.5
     slope[2] = slope_z.reshape(brick)
+    writes = [
+        pltpu.make_async_copy(chi, chi_hbm, sems.at[0]),
+        pltpu.make_async_copy(slope, slope_hbm, sems.at[1]),
+    ]
+    for write in writes:
+        write.start()
     grads = twice(jnp.concatenate([grad_x, grad_y, grad_z], 0), 1)
     width = STEP * CAP * POINTS
     columns = iota((cells, width), 0).astype(F32)
-    levels = iota((NZ, width), 0).astype(F32)
+    levels = iota((NZ, width), 0).astype(BF16)
     for first in range(0, GY, STEP):
         _, column, level = places(route, first, STEP)
-        hot = jnp.where(levels == level, 1.0, 0.0).astype(BF16)
+        hot = hot_of(levels, level)
         at_level = mm(grads, jnp.concatenate([hot, hot], 0))
-        here = columns == column
+        here = columns == column.astype(F32)
         lines = [
             jnp.sum(jnp.where(here, at_level[j * cells : (j + 1) * cells], 0.0), 0, keepdims=True)
             for j in range(3)
@@ -434,6 +443,8 @@
         lines = jnp.concatenate(lines + [jnp.zeros((1, width), F32)], 0)
         for s in range(STEP):
             picked[first + s] = lines[:, s * 128 : (s + 1) * 128]
+    for write in writes:
+        write.wait()
 
 
 def route_body(*refs):
@@ -495,7 +506,7 @@
 HBM = pl.BlockSpec(memory_space=pltpu.HBM)
 
 
-def call(body, name, outs, *operands, specs=None, scratch=()):
+def call(body, name, outs, *operands, specs=None, out_specs=None, scratch=()):
     shapes = [s if hasattr(s, "dtype") else jax.ShapeDtypeStruct(s, F32) for s in outs]
     single = len(shapes) == 1
     return pl.pallas_call(
@@ -503,7 +514,7 @@
         name=name,
         out_shape=shapes[0] if single else shapes,
         in_specs=specs or [VMEM] * len(operands),
-        out_specs=VMEM if single else [VMEM] * len(shapes),
+        out_specs=out_specs or (VMEM if single else [VMEM] * len(shapes)),
         scratch_shapes=list(scratch),
         compiler_params=pltpu.CompilerParams(vmem_limit_bytes=40 * 1024 * 1024),
     )(*operands)
@@ -558,8 +569,16 @@
     y_args = (table["y_back"],) + y_args
     spread = call(inverse_y_body, "inverse_y", [(GY, 8, 384)], got, *y_args, scratch=edges)
     got = swap(spread, "gy")
+    bricks = (3,) + brick
     chi, slope, picked = call(
-        pick_body, "pick", [brick, (3,) + brick, message], got, table["zb"], route
+        pick_body,
+        "pick",
+        [brick, bricks, message],
+        got,
+        table["zb"],
+        route,
+        out_specs=[HBM, HBM, VMEM],
+        scratch=(pltpu.VMEM(brick, F32), pltpu.VMEM(bricks, F32), pltpu.SemaphoreType.DMA((2,))),
     )
     returned = swap(picked, "gy")
     normal_grad = call(return_body, "deliver", [(3, BLOCKS, POINTS)], owner_here, returned)

time: 113 us -> 113 us (level)
  no operation moved by 1% of the time
where the time goes in v5:
time: 113 us
  blocking collectives  102 us (90%)
  Pallas kernels  10.2 us (9%)
    all_to_all x6, blocking collectives, swap(): return lax.all_to_all(x, axis, split_axis=0, concat_axis=0, tiled=True)  102 us
    pallas_call x7, Pallas kernels, call(): pl.pallas_call(body, name=name, out_shape=shapes[0] if single else shapes...  10.2 us

profile of v5, /device:TPU:1, one launch (start us, length us, event | category | flops | bytes accessed | tf_op | source)
XLA Modules:
  0.0 113.0 jit_solution(18406683212278331643)
XLA Ops:
  0.6 1.1 route.1
  1.8 17.0 %all_to_all.30.route = f32[32,4,128]{2,1,0:T(4,128)S(1)} all-to-all(f32[32,4,128]{2,1,0:T(4,128)S(1)} %get-tuple-element.10), channel_id=1, replica_groups=mesh['gx'=16,'gy'=32] {'gy'}, dimensions={0} | all-to-all | bytes 131072 | tf_op jit(solution)/shard_map/all_to_all | solution.py:528
  18.7 1.3 %splat.1 = f32[32,8,256]{2,1,0:T(8,128)S(1)} custom-call(f32[32,4,128]{2,1,0:T(4,128)S(1)} %all_to_all.30.route, f32[8,8,256]{2,1,0:T(8,128)S(1)} %get-tuple-element.11.target, bf16[256,768]{1,0:T(8,128)(2,1)S(1)} %get-tuple-element.12.zf), custom_call_target="tpu_custom_call" | custom-call | tf_op jit(solution)/shard_map/splat/pallas_call | solution.py:512
  20.1 0.0 copy-start
  20.1 0.0 copy-start.1
  20.1 12.6 %all_to_all.31.got = f32[32,8,256]{2,1,0:T(8,128)S(1)} all-to-all(f32[32,8,256]{2,1,0:T(8,128)S(1)} %splat.1), channel_id=1, replica_groups=mesh['gx'=16,'gy'=32] {'gy'}, dimensions={0} | all-to-all | bytes 524288 | tf_op jit(solution)/shard_map/all_to_all | solution.py:528
  32.7 0.0 copy-done.5
  32.7 0.0 copy-done.1
  32.7 0.0 copy-start.3
  32.7 0.0 copy-start.4
  32.7 0.0 copy-start.8
  32.7 0.0 copy-start.9
  32.8 1.2 %forward_y.1 = s32[16,16,128]{2,1,0:T(8,128)S(1)} custom-call(f32[32,8,256]{2,1,0:T(8,128)S(1)} %all_to_all.31.got, bf16[256,768]{1,0:T(8,128)(2,1)S(1)} %copy-done.5, bf16[384,256]{1,0:T(8,128)(2,1)S(1)} %copy-done.1, f32[3,128,128]{2,1,0:T(8,128)S(1)} %copy-done), custom_call_target="tpu_custom_call" | custom-call | tf_op jit(solution)/shard_map/forward_y/pallas_call | solution.py:512
  33.9 0.0 copy-start.7
  33.9 25.8 %all_to_all.32.got = s32[16,16,128]{2,1,0:T(8,128)S(1)} all-to-all(s32[16,16,128]{2,1,0:T(8,128)S(1)} %forward_y.1), channel_id=1, replica_groups=mesh['gx'=16,'gy'=32] {'gx'}, dimensions={0} | all-to-all | bytes 262144 | tf_op jit(solution)/shard_map/all_to_all | solution.py:528
  59.7 0.0 copy-start.6
  59.8 2.4 %spectrum.1 = s32[288,128]{1,0:T(8,128)S(1)} custom-call(s32[16,16,128]{2,1,0:T(8,128)S(1)} %all_to_all.32.got, bf16[256,768]{1,0:T(8,128)(2,1)S(1)} %copy-done.4, bf16[256,768]{1,0:T(8,128)(2,1)S(1)} %copy-done.3, bf16[384,256]{1,0:T(8,128)(2,1)S(1)} %copy-done.8, f32[2,128,128]{2,1,0:T(8,128)S(1)} %copy-done.9, bf16[2,256,256]{2,1,0:T(8,128)(2,1)S(1)} %copy-done.7), custom_call_target="tpu_custom_call" | custom-call | tf_op jit(solution)/shard_map/spectrum/pallas_call | solution.py:512
  62.1 18.3 %all_to_all.33 = s32[16,18,1,128]{3,2,1,0:T(1,128)S(1)} all-to-all(s32[16,18,1,128]{3,2,1,0:T(1,128)S(1)} %bitcast.5), channel_id=1, replica_groups=mesh['gx'=16,'gy'=32] {'gx'}, dimensions={0} | all-to-all | bytes 294912 | tf_op jit(solution)/shard_map/all_to_all | solution.py:528
  80.5 1.7 %inverse_y.1 = f32[32,8,384]{2,1,0:T(8,128)S(1)} custom-call(s32[288,128]{1,0:T(8,128)S(1)} %bitcast.6, bf16[256,768]{1,0:T(8,128)(2,1)S(1)} %copy-done.6, bf16[384,256]{1,0:T(8,128)(2,1)S(1)} %copy-done.1, f32[3,128,128]{2,1,0:T(8,128)S(1)} %copy-done), custom_call_target="tpu_custom_call" | custom-call | tf_op jit(solution)/shard_map/inverse_y/pallas_call | solution.py:512
  82.2 0.0 copy-start.2
  82.2 17.5 %all_to_all.34.got = f32[32,8,384]{2,1,0:T(8,128)S(1)} all-to-all(f32[32,8,384]{2,1,0:T(8,128)S(1)} %inverse_y.1), channel_id=1, replica_groups=mesh['gx'=16,'gy'=32] {'gy'}, dimensions={0} | all-to-all | bytes 786432 | tf_op jit(solution)/shard_map/all_to_all | solution.py:528
  99.7 1.5 %pick.1 = (f32[8,8,256]{2,1,0:T(8,128)}, f32[3,8,8,256]{3,2,1,0:T(8,128)}, f32[32,4,128]{2,1,0:T(4,128)S(1)}) custom-call(f32[32,8,384]{2,1,0:T(8,128)S(1)} %all_to_all.34.got, bf16[768,256]{1,0:T(8,128)(2,1)S(1)} %copy-done.2, f32[32,4,128]{2,1,0:T(4,128)S(1)} %all_to_all.30.route), custom_call_target="tpu_custom_call" | custom-call | tf_op jit(solution)/shard_map/pick/pallas_call | solution.py:512
  101.2 10.7 %all_to_all.35.got = f32[32,4,128]{2,1,0:T(4,128)S(1)} all-to-all(f32[32,4,128]{2,1,0:T(4,128)S(1)} %get-tuple-element.16), channel_id=1, replica_groups=mesh['gx'=16,'gy'=32] {'gy'}, dimensions={0} | all-to-all | bytes 131072 | tf_op jit(solution)/shard_map/all_to_all | solution.py:528
  111.9 1.1 deliver.1
  (9 shorter events, 0.0 us)
Async XLA Ops:
  18.7 14.0 %copy-start.5 = (bf16[256,768]{1,0:T(8,128)(2,1)S(1)}, bf16[256,768]{1,0:T(8,128)(2,1)}, u32[]{:S(2)}) copy-start(bf16[256,768]{1,0:T(8,128)(2,1)} %constant.24.clone.rows) | copy-start | bytes 1179652
  20.1 12.7 %copy-start = (f32[3,128,128]{2,1,0:T(8,128)S(1)}, f32[3,128,128]{2,1,0:T(8,128)}, u32[]{:S(2)}) copy-start(f32[3,128,128]{2,1,0:T(8,128)} %constant.30.clone.twist) | copy-start | bytes 589828
  20.1 12.6 %copy-start.1 = (bf16[384,256]{1,0:T(8,128)(2,1)S(1)}, bf16[384,256]{1,0:T(8,128)(2,1)}, u32[]{:S(2)}) copy-start(bf16[384,256]{1,0:T(8,128)(2,1)} %constant.28.clone.lanes) | copy-start | bytes 589828
  32.7 27.0 %copy-start.3 = (bf16[256,768]{1,0:T(8,128)(2,1)S(1)}, bf16[256,768]{1,0:T(8,128)(2,1)}, u32[]{:S(2)}) copy-start(bf16[256,768]{1,0:T(8,128)(2,1)} %constant.27.clone.back) | copy-start | bytes 1179652
  32.7 27.0 %copy-start.4 = (bf16[256,768]{1,0:T(8,128)(2,1)S(1)}, bf16[256,768]{1,0:T(8,128)(2,1)}, u32[]{:S(2)}) copy-start(bf16[256,768]{1,0:T(8,128)(2,1)} %constant.25.clone.rows) | copy-start | bytes 1179652
  32.7 27.0 %copy-start.8 = (bf16[384,256]{1,0:T(8,128)(2,1)S(1)}, bf16[384,256]{1,0:T(8,128)(2,1)}, u32[]{:S(2)}) copy-start(bf16[384,256]{1,0:T(8,128)(2,1)} %constant.29.clone.lanes) | copy-start | bytes 589828
  32.7 27.0 %copy-start.9 = (f32[2,128,128]{2,1,0:T(8,128)S(1)}, f32[2,128,128]{2,1,0:T(8,128)}, u32[]{:S(2)}) copy-start(f32[2,128,128]{2,1,0:T(8,128)} %constant.31.clone.twist) | copy-start | bytes 393220
  33.9 25.8 %copy-start.7 = (bf16[2,256,256]{2,1,0:T(8,128)(2,1)S(1)}, bf16[2,256,256]{2,1,0:T(8,128)(2,1)}, u32[]{:S(2)}) copy-start(bf16[2,256,256]{2,1,0:T(8,128)(2,1)} %constant.32.clone.mirror) | copy-start | bytes 786436
  59.7 20.8 %copy-start.6 = (bf16[256,768]{1,0:T(8,128)(2,1)S(1)}, bf16[256,768]{1,0:T(8,128)(2,1)}, u32[]{:S(2)}) copy-start(bf16[256,768]{1,0:T(8,128)(2,1)} %constant.26.clone.back) | copy-start | bytes 1179652
  82.2 17.5 %copy-start.2 = (bf16[768,256]{1,0:T(8,128)(2,1)S(1)}, bf16[768,256]{1,0:T(8,128)(2,1)}, u32[]{:S(2)}) copy-start(bf16[768,256]{1,0:T(8,128)(2,1)} %constant.23.clone.zb) | copy-start | bytes 1179652

commit v6 on v5

--- a/solution.py
+++ b/solution.py
@@ -180,21 +180,23 @@
     return odd(ky_of(row >> 3, row, lane), NY)[1]
 
 
-STEP = 4
+STEP, PICK_STEP = 8, 2
 
 
 def splat_body(route, target, zf, out):
     width = STEP * CAP * POINTS
     columns = iota((BX * BY, width), 0).astype(BF16)
     levels = iota((NZ, width), 0).astype(BF16)
-    field = jnp.zeros((3 * BX * BY, NZ), F32)
+    cells = BX * BY
+    nothing = jnp.zeros((cells, width), BF16)
+    blank = jnp.zeros((3 * cells, NZ), F32)
+    field = jnp.concatenate([blank, target[...].reshape(cells, NZ)], 0).T
     for first in range(0, GY, STEP):
         rows, column, level = places(route, first, STEP)
         here = hot_of(columns, column)
-        weighted = jnp.concatenate([here * rows[j : j + 1] for j in range(3)], 0)
-        field = field + mm(weighted, hot_of(levels, level), 1, 1)
-    both = jnp.concatenate([field, target[...].reshape(BX * BY, NZ)], 0)
-    spread = mm(zf[...], thrice(both, 1), 1, 1)
+        weighted = [here * rows[j : j + 1] for j in range(3)] + [nothing]
+        field = field + mm(hot_of(levels, level), jnp.concatenate(weighted, 0), 1, 1)
+    spread = mm(zf[...], thrice(field, 0))
     right = spread[:, 128:]
     right = jnp.where(iota((NZ, 128), 1) < 64, right * kz_of(NZ), right)
     out[...] = jnp.concatenate([spread[:, :128], right], 1).reshape(out.shape)
@@ -428,11 +430,11 @@
     for write in writes:
         write.start()
     grads = twice(jnp.concatenate([grad_x, grad_y, grad_z], 0), 1)
-    width = STEP * CAP * POINTS
+    width = PICK_STEP * CAP * POINTS
     columns = iota((cells, width), 0).astype(F32)
     levels = iota((NZ, width), 0).astype(BF16)
-    for first in range(0, GY, STEP):
-        _, column, level = places(route, first, STEP)
+    for first in range(0, GY, PICK_STEP):
+        _, column, level = places(route, first, PICK_STEP)
         hot = hot_of(levels, level)
         at_level = mm(grads, jnp.concatenate([hot, hot], 0))
         here = columns == column.astype(F32)
@@ -441,7 +443,7 @@
             for j in range(3)
         ]
         lines = jnp.concatenate(lines + [jnp.zeros((1, width), F32)], 0)
-        for s in range(STEP):
+        for s in range(PICK_STEP):
             picked[first + s] = lines[:, s * 128 : (s + 1) * 128]
     for write in writes:
         write.wait()

time: 113 us -> 113 us (level)
  no operation moved by 1% of the time
where the time goes in v6:
time: 113 us
  blocking collectives  102 us (90%)
  Pallas kernels  10.1 us (9%)
    all_to_all x6, blocking collectives, swap(): return lax.all_to_all(x, axis, split_axis=0, concat_axis=0, tiled=True)  102 us
    pallas_call x7, Pallas kernels, call(): pl.pallas_call(body, name=name, out_shape=shapes[0] if single else shapes...  10.1 us

profile of v6, /device:TPU:1, one launch (start us, length us, event | category | flops | bytes accessed | tf_op | source)
XLA Modules:
  0.0 112.8 jit_solution(15689222359051978979)
XLA Ops:
  0.6 1.1 %route.1 = (f32[32,4,128]{2,1,0:T(4,128)S(1)}, f32[8,8,256]{2,1,0:T(8,128)S(1)}, bf16[256,768]{1,0:T(8,128)(2,1)S(1)}, s32[1,32]{1,0:T(1,128)S(1)}) custom-call(s32[1,32]{1,0:T(1,128)} %bitcast.9, bf16[3,32,64]{2,1,0:T(8,128)(2,1)} %bitcast.8, s32[32,64]{1,0:T(8,128)} %refs_2_.1, f32[8,8,256]{2,1,0:T(8,128)} %refs_3_.1, bf16[256,768]{1,0:T(8,128)(2,1)} %constant.22.clone.refs_4_), custom_call_target="tpu_custom_call" | custom-call | tf_op jit(solution)/shard_map/route/pallas_call | solution.py:514
  1.8 17.0 %all_to_all.30.route = f32[32,4,128]{2,1,0:T(4,128)S(1)} all-to-all(f32[32,4,128]{2,1,0:T(4,128)S(1)} %get-tuple-element.10), channel_id=1, replica_groups=mesh['gx'=16,'gy'=32] {'gy'}, dimensions={0} | all-to-all | bytes 131072 | tf_op jit(solution)/shard_map/all_to_all | solution.py:530
  18.7 1.2 %splat.1 = f32[32,8,256]{2,1,0:T(8,128)S(1)} custom-call(f32[32,4,128]{2,1,0:T(4,128)S(1)} %all_to_all.30.route, f32[8,8,256]{2,1,0:T(8,128)S(1)} %get-tuple-element.11.target, bf16[256,768]{1,0:T(8,128)(2,1)S(1)} %get-tuple-element.12.zf), custom_call_target="tpu_custom_call" | custom-call | tf_op jit(solution)/shard_map/splat/pallas_call | solution.py:514
  19.9 0.0 copy-start
  19.9 0.0 copy-start.1
  20.0 12.6 %all_to_all.31.got = f32[32,8,256]{2,1,0:T(8,128)S(1)} all-to-all(f32[32,8,256]{2,1,0:T(8,128)S(1)} %splat.1), channel_id=1, replica_groups=mesh['gx'=16,'gy'=32] {'gy'}, dimensions={0} | all-to-all | bytes 524288 | tf_op jit(solution)/shard_map/all_to_all | solution.py:530
  32.6 0.0 copy-start.3
  32.6 0.0 copy-start.4
  32.6 0.0 copy-start.8
  32.6 0.0 copy-start.9
  32.6 1.2 %forward_y.1 = s32[16,16,128]{2,1,0:T(8,128)S(1)} custom-call(f32[32,8,256]{2,1,0:T(8,128)S(1)} %all_to_all.31.got, bf16[256,768]{1,0:T(8,128)(2,1)S(1)} %copy-done.5, bf16[384,256]{1,0:T(8,128)(2,1)S(1)} %copy-done.1, f32[3,128,128]{2,1,0:T(8,128)S(1)} %copy-done), custom_call_target="tpu_custom_call" | custom-call | tf_op jit(solution)/shard_map/forward_y/pallas_call | solution.py:514
  33.8 0.0 copy-start.7
  33.8 25.8 %all_to_all.32.got = s32[16,16,128]{2,1,0:T(8,128)S(1)} all-to-all(s32[16,16,128]{2,1,0:T(8,128)S(1)} %forward_y.1), channel_id=1, replica_groups=mesh['gx'=16,'gy'=32] {'gx'}, dimensions={0} | all-to-all | bytes 262144 | tf_op jit(solution)/shard_map/all_to_all | solution.py:530
  59.6 0.0 copy-done.3
  59.6 0.0 copy-done.8
  59.6 0.0 copy-start.6
  59.6 2.4 %spectrum.1 = s32[288,128]{1,0:T(8,128)S(1)} custom-call(s32[16,16,128]{2,1,0:T(8,128)S(1)} %all_to_all.32.got, bf16[256,768]{1,0:T(8,128)(2,1)S(1)} %copy-done.4, bf16[256,768]{1,0:T(8,128)(2,1)S(1)} %copy-done.3, bf16[384,256]{1,0:T(8,128)(2,1)S(1)} %copy-done.8, f32[2,128,128]{2,1,0:T(8,128)S(1)} %copy-done.9, bf16[2,256,256]{2,1,0:T(8,128)(2,1)S(1)} %copy-done.7), custom_call_target="tpu_custom_call" | custom-call | tf_op jit(solution)/shard_map/spectrum/pallas_call | solution.py:514
  62.0 18.3 %all_to_all.33 = s32[16,18,1,128]{3,2,1,0:T(1,128)S(1)} all-to-all(s32[16,18,1,128]{3,2,1,0:T(1,128)S(1)} %bitcast.5), channel_id=1, replica_groups=mesh['gx'=16,'gy'=32] {'gx'}, dimensions={0} | all-to-all | bytes 294912 | tf_op jit(solution)/shard_map/all_to_all | solution.py:530
  80.4 1.7 %inverse_y.1 = f32[32,8,384]{2,1,0:T(8,128)S(1)} custom-call(s32[288,128]{1,0:T(8,128)S(1)} %bitcast.6, bf16[256,768]{1,0:T(8,128)(2,1)S(1)} %copy-done.6, bf16[384,256]{1,0:T(8,128)(2,1)S(1)} %copy-done.1, f32[3,128,128]{2,1,0:T(8,128)S(1)} %copy-done), custom_call_target="tpu_custom_call" | custom-call | tf_op jit(solution)/shard_map/inverse_y/pallas_call | solution.py:514
  82.0 0.0 copy-start.2
  82.0 17.5 %all_to_all.34.got = f32[32,8,384]{2,1,0:T(8,128)S(1)} all-to-all(f32[32,8,384]{2,1,0:T(8,128)S(1)} %inverse_y.1), channel_id=1, replica_groups=mesh['gx'=16,'gy'=32] {'gy'}, dimensions={0} | all-to-all | bytes 786432 | tf_op jit(solution)/shard_map/all_to_all | solution.py:530
  99.5 1.5 %pick.1 = (f32[8,8,256]{2,1,0:T(8,128)}, f32[3,8,8,256]{3,2,1,0:T(8,128)}, f32[32,4,128]{2,1,0:T(4,128)S(1)}) custom-call(f32[32,8,384]{2,1,0:T(8,128)S(1)} %all_to_all.34.got, bf16[768,256]{1,0:T(8,128)(2,1)S(1)} %copy-done.2, f32[32,4,128]{2,1,0:T(4,128)S(1)} %all_to_all.30.route), custom_call_target="tpu_custom_call" | custom-call | tf_op jit(solution)/shard_map/pick/pallas_call | solution.py:514
  101.1 10.7 %all_to_all.35.got = f32[32,4,128]{2,1,0:T(4,128)S(1)} all-to-all(f32[32,4,128]{2,1,0:T(4,128)S(1)} %get-tuple-element.16), channel_id=1, replica_groups=mesh['gx'=16,'gy'=32] {'gy'}, dimensions={0} | all-to-all | bytes 131072 | tf_op jit(solution)/shard_map/all_to_all | solution.py:530
  111.8 1.1 deliver.1
  (9 shorter events, 0.0 us)
Async XLA Ops:
  18.7 13.8 %copy-start.5 = (bf16[256,768]{1,0:T(8,128)(2,1)S(1)}, bf16[256,768]{1,0:T(8,128)(2,1)}, u32[]{:S(2)}) copy-start(bf16[256,768]{1,0:T(8,128)(2,1)} %constant.24.clone.rows) | copy-start | bytes 1179652
  19.9 12.7 %copy-start = (f32[3,128,128]{2,1,0:T(8,128)S(1)}, f32[3,128,128]{2,1,0:T(8,128)}, u32[]{:S(2)}) copy-start(f32[3,128,128]{2,1,0:T(8,128)} %constant.30.clone.twist) | copy-start | bytes 589828
  19.9 12.6 %copy-start.1 = (bf16[384,256]{1,0:T(8,128)(2,1)S(1)}, bf16[384,256]{1,0:T(8,128)(2,1)}, u32[]{:S(2)}) copy-start(bf16[384,256]{1,0:T(8,128)(2,1)} %constant.28.clone.lanes) | copy-start | bytes 589828
  32.6 27.0 %copy-start.3 = (bf16[256,768]{1,0:T(8,128)(2,1)S(1)}, bf16[256,768]{1,0:T(8,128)(2,1)}, u32[]{:S(2)}) copy-start(bf16[256,768]{1,0:T(8,128)(2,1)} %constant.27.clone.back) | copy-start | bytes 1179652
  32.6 27.0 %copy-start.4 = (bf16[256,768]{1,0:T(8,128)(2,1)S(1)}, bf16[256,768]{1,0:T(8,128)(2,1)}, u32[]{:S(2)}) copy-start(bf16[256,768]{1,0:T(8,128)(2,1)} %constant.25.clone.rows) | copy-start | bytes 1179652
  32.6 27.0 %copy-start.8 = (bf16[384,256]{1,0:T(8,128)(2,1)S(1)}, bf16[384,256]{1,0:T(8,128)(2,1)}, u32[]{:S(2)}) copy-start(bf16[384,256]{1,0:T(8,128)(2,1)} %constant.29.clone.lanes) | copy-start | bytes 589828
  32.6 27.0 %copy-start.9 = (f32[2,128,128]{2,1,0:T(8,128)S(1)}, f32[2,128,128]{2,1,0:T(8,128)}, u32[]{:S(2)}) copy-start(f32[2,128,128]{2,1,0:T(8,128)} %constant.31.clone.twist) | copy-start | bytes 393220
  33.8 25.8 %copy-start.7 = (bf16[2,256,256]{2,1,0:T(8,128)(2,1)S(1)}, bf16[2,256,256]{2,1,0:T(8,128)(2,1)}, u32[]{:S(2)}) copy-start(bf16[2,256,256]{2,1,0:T(8,128)(2,1)} %constant.32.clone.mirror) | copy-start | bytes 786436
  59.6 20.8 %copy-start.6 = (bf16[256,768]{1,0:T(8,128)(2,1)S(1)}, bf16[256,768]{1,0:T(8,128)(2,1)}, u32[]{:S(2)}) copy-start(bf16[256,768]{1,0:T(8,128)(2,1)} %constant.26.clone.back) | copy-start | bytes 1179652
  82.0 17.5 %copy-start.2 = (bf16[768,256]{1,0:T(8,128)(2,1)S(1)}, bf16[768,256]{1,0:T(8,128)(2,1)}, u32[]{:S(2)}) copy-start(bf16[768,256]{1,0:T(8,128)(2,1)} %constant.23.clone.zb) | copy-start | bytes 1179652

commit v7 on v6

--- a/solution.py
+++ b/solution.py
@@ -450,35 +450,35 @@
 
 
 def route_body(*refs):
-    sources, (out, target, zf, row), (owners, normals, cells, count, sems) = (
-        refs[:5],
-        refs[5:9],
-        refs[9:],
-    )
+    sources, (out, target, zf, owners), (normals, cells, sems) = refs[:5], refs[5:9], refs[9:]
     fetches = [
         pltpu.make_async_copy(source, place, sems.at[i])
-        for i, (source, place) in enumerate(
-            zip(sources + sources[:1], (owners, normals, cells, target, zf, row))
-        )
+        for i, (source, place) in enumerate(zip(sources, (owners, normals, cells, target, zf)))
     ]
     for fetch in fetches:
         fetch.start()
-    line = iota((4, 128), 0)
-    half = iota((4, 128), 1) >> 6
-    empty = jnp.where(line == 3, -1.0, 0.0)
-    for o in range(GY):
-        out[o] = empty
-        count[o] = 0
     for fetch in fetches[:3]:
         fetch.wait()
-    parts = [normals[j].astype(F32) for j in range(3)] + [cells[...].astype(F32)]
-    for b in range(BLOCKS):
-        owner = owners[0, b]
-        rank = count[owner]
-        count[owner] = rank + 1
-        value = jnp.concatenate([p[b : b + 1] for p in parts], 0)
-        value = jnp.concatenate([value, value], 1)
-        out[owner] = jnp.where(half == rank, value, out[owner])
+    square = (BLOCKS, BLOCKS)
+    row, column = iota(square, 0), iota(square, 1)
+    across = jnp.broadcast_to(owners[...], square)
+    down = jnp.sum(jnp.where(row == column, across, 0), 1, keepdims=True)
+    earlier = (down == across) & (row < column)
+    rank = jnp.sum(jnp.where(earlier, 1, 0), 0, keepdims=True)
+    hot = [jnp.where((row == across) & (rank == r), 1.0, 0.0) for r in range(CAP)]
+    hot = jnp.concatenate(hot, 1).astype(BF16)
+    cell = cells[...]
+    parts = [normals[j].astype(F32) for j in range(3)]
+    parts += [((cell >> 8) + 1).astype(F32), (cell & 255).astype(F32)]
+    blank = jnp.zeros((BLOCKS, POINTS), F32)
+    first = [jnp.concatenate([p, blank], 1) for p in parts]
+    second = [jnp.concatenate([blank, p], 1) for p in parts]
+    values = [jnp.concatenate(lines, 1) for lines in (first, second)]
+    lines = mm(hot, jnp.concatenate(values, 0).astype(BF16))
+    lines = [lines[:, i * 128 : (i + 1) * 128] for i in range(5)]
+    for j in range(3):
+        out[:, j, :] = lines[j]
+    out[:, 3, :] = (lines[3] - 1.0) * float(NZ) + lines[4]
     for fetch in fetches[3:]:
         fetch.wait()
 
@@ -533,17 +533,14 @@
 def local(normals, owners, cells, target):
     table = {k: jnp.asarray(v) for k, v in TABLES.items()}
     owner = owners.reshape(1, BLOCKS)
-    counts = pltpu.SMEM((GY,), jnp.int32)
     brick = (BX, BY, NZ)
     message = (GY, 4, CAP * POINTS)
 
     by_part = jnp.moveaxis(normals, 1, 0)
     scratch = (
-        pltpu.SMEM(owner.shape, jnp.int32),
         pltpu.VMEM(by_part.shape, BF16),
         pltpu.VMEM(cells.shape, jnp.int32),
-        counts,
-        pltpu.SemaphoreType.DMA((6,)),
+        pltpu.SemaphoreType.DMA((5,)),
     )
     tables_z = jax.ShapeDtypeStruct(table["zf"].shape, BF16)
     sources = (owner, by_part, cells, target, table["zf"])

time: 113 us -> 113 us (level)
  no operation moved by 1% of the time
where the time goes in v7:
time: 113 us
  blocking collectives  102 us (90%)
  Pallas kernels  10.1 us (9%)
    all_to_all x6, blocking collectives, swap(): return lax.all_to_all(x, axis, split_axis=0, concat_axis=0, tiled=True)  102 us
    pallas_call x7, Pallas kernels, call(): pl.pallas_call(body, name=name, out_shape=shapes[0] if single else shapes...  10.1 us

profile of v7, /device:TPU:1, one launch (start us, length us, event | category | flops | bytes accessed | tf_op | source)
XLA Modules:
  0.0 112.8 jit_solution(49450957463345256)
XLA Ops:
  0.6 1.1 %route.1 = (f32[32,4,128]{2,1,0:T(4,128)S(1)}, f32[8,8,256]{2,1,0:T(8,128)S(1)}, bf16[256,768]{1,0:T(8,128)(2,1)S(1)}, s32[1,32]{1,0:T(1,128)S(1)}) custom-call(s32[1,32]{1,0:T(1,128)} %bitcast.9, bf16[3,32,64]{2,1,0:T(8,128)(2,1)} %bitcast.8, s32[32,64]{1,0:T(8,128)} %refs_2_.1, f32[8,8,256]{2,1,0:T(8,128)} %refs_3_.1, bf16[256,768]{1,0:T(8,128)(2,1)} %constant.22.clone.refs_4_), custom_call_target="tpu_custom_call" | custom-call | tf_op jit(solution)/shard_map/route/pallas_call | solution.py:514
  1.8 17.0 %all_to_all.30.route = f32[32,4,128]{2,1,0:T(4,128)S(1)} all-to-all(f32[32,4,128]{2,1,0:T(4,128)S(1)} %get-tuple-element.10), channel_id=1, replica_groups=mesh['gx'=16,'gy'=32] {'gy'}, dimensions={0} | all-to-all | bytes 131072 | tf_op jit(solution)/shard_map/all_to_all | solution.py:530
  18.7 1.2 %splat.1 = f32[32,8,256]{2,1,0:T(8,128)S(1)} custom-call(f32[32,4,128]{2,1,0:T(4,128)S(1)} %all_to_all.30.route, f32[8,8,256]{2,1,0:T(8,128)S(1)} %get-tuple-element.11.target, bf16[256,768]{1,0:T(8,128)(2,1)S(1)} %get-tuple-element.12.zf), custom_call_target="tpu_custom_call" | custom-call | tf_op jit(solution)/shard_map/splat/pallas_call | solution.py:514
  19.9 0.0 copy-start
  19.9 0.0 copy-start.1
  20.0 12.6 %all_to_all.31.got = f32[32,8,256]{2,1,0:T(8,128)S(1)} all-to-all(f32[32,8,256]{2,1,0:T(8,128)S(1)} %splat.1), channel_id=1, replica_groups=mesh['gx'=16,'gy'=32] {'gy'}, dimensions={0} | all-to-all | bytes 524288 | tf_op jit(solution)/shard_map/all_to_all | solution.py:530
  32.6 0.0 copy-done
  32.6 0.0 copy-start.3
  32.6 0.0 copy-start.4
  32.6 0.0 copy-start.8
  32.6 0.0 copy-start.9
  32.6 1.2 %forward_y.1 = s32[16,16,128]{2,1,0:T(8,128)S(1)} custom-call(f32[32,8,256]{2,1,0:T(8,128)S(1)} %all_to_all.31.got, bf16[256,768]{1,0:T(8,128)(2,1)S(1)} %copy-done.5, bf16[384,256]{1,0:T(8,128)(2,1)S(1)} %copy-done.1, f32[3,128,128]{2,1,0:T(8,128)S(1)} %copy-done), custom_call_target="tpu_custom_call" | custom-call | tf_op jit(solution)/shard_map/forward_y/pallas_call | solution.py:514
  33.8 0.0 copy-start.7
  33.8 25.8 %all_to_all.32.got = s32[16,16,128]{2,1,0:T(8,128)S(1)} all-to-all(s32[16,16,128]{2,1,0:T(8,128)S(1)} %forward_y.1), channel_id=1, replica_groups=mesh['gx'=16,'gy'=32] {'gx'}, dimensions={0} | all-to-all | bytes 262144 | tf_op jit(solution)/shard_map/all_to_all | solution.py:530
  59.6 0.0 copy-done.4
  59.6 0.0 copy-start.6
  59.6 2.4 %spectrum.1 = s32[288,128]{1,0:T(8,128)S(1)} custom-call(s32[16,16,128]{2,1,0:T(8,128)S(1)} %all_to_all.32.got, bf16[256,768]{1,0:T(8,128)(2,1)S(1)} %copy-done.4, bf16[256,768]{1,0:T(8,128)(2,1)S(1)} %copy-done.3, bf16[384,256]{1,0:T(8,128)(2,1)S(1)} %copy-done.8, f32[2,128,128]{2,1,0:T(8,128)S(1)} %copy-done.9, bf16[2,256,256]{2,1,0:T(8,128)(2,1)S(1)} %copy-done.7), custom_call_target="tpu_custom_call" | custom-call | tf_op jit(solution)/shard_map/spectrum/pallas_call | solution.py:514
  62.0 18.3 %all_to_all.33 = s32[16,18,1,128]{3,2,1,0:T(1,128)S(1)} all-to-all(s32[16,18,1,128]{3,2,1,0:T(1,128)S(1)} %bitcast.5), channel_id=1, replica_groups=mesh['gx'=16,'gy'=32] {'gx'}, dimensions={0} | all-to-all | bytes 294912 | tf_op jit(solution)/shard_map/all_to_all | solution.py:530
  80.4 1.7 %inverse_y.1 = f32[32,8,384]{2,1,0:T(8,128)S(1)} custom-call(s32[288,128]{1,0:T(8,128)S(1)} %bitcast.6, bf16[256,768]{1,0:T(8,128)(2,1)S(1)} %copy-done.6, bf16[384,256]{1,0:T(8,128)(2,1)S(1)} %copy-done.1, f32[3,128,128]{2,1,0:T(8,128)S(1)} %copy-done), custom_call_target="tpu_custom_call" | custom-call | tf_op jit(solution)/shard_map/inverse_y/pallas_call | solution.py:514
  82.0 0.0 copy-start.2
  82.1 17.5 %all_to_all.34.got = f32[32,8,384]{2,1,0:T(8,128)S(1)} all-to-all(f32[32,8,384]{2,1,0:T(8,128)S(1)} %inverse_y.1), channel_id=1, replica_groups=mesh['gx'=16,'gy'=32] {'gy'}, dimensions={0} | all-to-all | bytes 786432 | tf_op jit(solution)/shard_map/all_to_all | solution.py:530
  99.6 1.5 %pick.1 = (f32[8,8,256]{2,1,0:T(8,128)}, f32[3,8,8,256]{3,2,1,0:T(8,128)}, f32[32,4,128]{2,1,0:T(4,128)S(1)}) custom-call(f32[32,8,384]{2,1,0:T(8,128)S(1)} %all_to_all.34.got, bf16[768,256]{1,0:T(8,128)(2,1)S(1)} %copy-done.2, f32[32,4,128]{2,1,0:T(4,128)S(1)} %all_to_all.30.route), custom_call_target="tpu_custom_call" | custom-call | tf_op jit(solution)/shard_map/pick/pallas_call | solution.py:514
  101.1 10.7 %all_to_all.35.got = f32[32,4,128]{2,1,0:T(4,128)S(1)} all-to-all(f32[32,4,128]{2,1,0:T(4,128)S(1)} %get-tuple-element.16), channel_id=1, replica_groups=mesh['gx'=16,'gy'=32] {'gy'}, dimensions={0} | all-to-all | bytes 131072 | tf_op jit(solution)/shard_map/all_to_all | solution.py:530
  111.8 1.1 deliver.1
  (9 shorter events, 0.0 us)
Async XLA Ops:
  18.7 13.8 %copy-start.5 = (bf16[256,768]{1,0:T(8,128)(2,1)S(1)}, bf16[256,768]{1,0:T(8,128)(2,1)}, u32[]{:S(2)}) copy-start(bf16[256,768]{1,0:T(8,128)(2,1)} %constant.24.clone.rows) | copy-start | bytes 1179652
  19.9 12.7 %copy-start = (f32[3,128,128]{2,1,0:T(8,128)S(1)}, f32[3,128,128]{2,1,0:T(8,128)}, u32[]{:S(2)}) copy-start(f32[3,128,128]{2,1,0:T(8,128)} %constant.30.clone.twist) | copy-start | bytes 589828
  19.9 12.7 %copy-start.1 = (bf16[384,256]{1,0:T(8,128)(2,1)S(1)}, bf16[384,256]{1,0:T(8,128)(2,1)}, u32[]{:S(2)}) copy-start(bf16[384,256]{1,0:T(8,128)(2,1)} %constant.28.clone.lanes) | copy-start | bytes 589828
  32.6 27.0 %copy-start.3 = (bf16[256,768]{1,0:T(8,128)(2,1)S(1)}, bf16[256,768]{1,0:T(8,128)(2,1)}, u32[]{:S(2)}) copy-start(bf16[256,768]{1,0:T(8,128)(2,1)} %constant.27.clone.back) | copy-start | bytes 1179652
  32.6 27.0 %copy-start.4 = (bf16[256,768]{1,0:T(8,128)(2,1)S(1)}, bf16[256,768]{1,0:T(8,128)(2,1)}, u32[]{:S(2)}) copy-start(bf16[256,768]{1,0:T(8,128)(2,1)} %constant.25.clone.rows) | copy-start | bytes 1179652
  32.6 27.0 %copy-start.8 = (bf16[384,256]{1,0:T(8,128)(2,1)S(1)}, bf16[384,256]{1,0:T(8,128)(2,1)}, u32[]{:S(2)}) copy-start(bf16[384,256]{1,0:T(8,128)(2,1)} %constant.29.clone.lanes) | copy-start | bytes 589828
  32.6 27.0 %copy-start.9 = (f32[2,128,128]{2,1,0:T(8,128)S(1)}, f32[2,128,128]{2,1,0:T(8,128)}, u32[]{:S(2)}) copy-start(f32[2,128,128]{2,1,0:T(8,128)} %constant.31.clone.twist) | copy-start | bytes 393220
  33.8 25.8 %copy-start.7 = (bf16[2,256,256]{2,1,0:T(8,128)(2,1)S(1)}, bf16[2,256,256]{2,1,0:T(8,128)(2,1)}, u32[]{:S(2)}) copy-start(bf16[2,256,256]{2,1,0:T(8,128)(2,1)} %constant.32.clone.mirror) | copy-start | bytes 786436
  59.6 20.8 %copy-start.6 = (bf16[256,768]{1,0:T(8,128)(2,1)S(1)}, bf16[256,768]{1,0:T(8,128)(2,1)}, u32[]{:S(2)}) copy-start(bf16[256,768]{1,0:T(8,128)(2,1)} %constant.26.clone.back) | copy-start | bytes 1179652
  82.0 17.5 %copy-start.2 = (bf16[768,256]{1,0:T(8,128)(2,1)S(1)}, bf16[768,256]{1,0:T(8,128)(2,1)}, u32[]{:S(2)}) copy-start(bf16[768,256]{1,0:T(8,128)(2,1)} %constant.23.clone.zb) | copy-start | bytes 1179652

commit v8 on v7

--- a/solution.py
+++ b/solution.py
@@ -76,7 +76,7 @@
                         src = f * 64 + (-a - m) % 8 * 8 + (-b - n) % 8
                         mirror[m, n, src, f * 64 + a * 8 + b] = 1.0
     return dict(
-        zf=halves(order(zf), 1),
+        zf=halves(order(zf), 1)[:, : 2 * NZ].reshape(NZ, 2, NZ).swapaxes(0, 1),
         zb=halves(order(zb), 0),
         y_rows=halves(y_rows, 1),
         x_rows=halves(x_rows, 1),
@@ -196,7 +196,7 @@
         here = hot_of(columns, column)
         weighted = [here * rows[j : j + 1] for j in range(3)] + [nothing]
         field = field + mm(hot_of(levels, level), jnp.concatenate(weighted, 0), 1, 1)
-    spread = mm(zf[...], thrice(field, 0))
+    spread = mm(jnp.concatenate([zf[0], zf[1], zf[0]], 1), thrice(field, 0))
     right = spread[:, 128:]
     right = jnp.where(iota((NZ, 128), 1) < 64, right * kz_of(NZ), right)
     out[...] = jnp.concatenate([spread[:, :128], right], 1).reshape(out.shape)
@@ -453,8 +453,10 @@
     sources, (out, target, zf, owners), (normals, cells, sems) = refs[:5], refs[5:9], refs[9:]
     fetches = [
         pltpu.make_async_copy(source, place, sems.at[i])
-        for i, (source, place) in enumerate(zip(sources, (owners, normals, cells, target, zf)))
+        for i, (source, place) in enumerate(zip(sources[:4], (owners, normals, cells, target)))
     ]
+    table = sources[4]
+    fetches += [pltpu.make_async_copy(table.at[i], zf.at[i], sems.at[4 + i]) for i in range(2)]
     for fetch in fetches:
         fetch.start()
     for fetch in fetches[:3]:
@@ -540,7 +542,7 @@
     scratch = (
         pltpu.VMEM(by_part.shape, BF16),
         pltpu.VMEM(cells.shape, jnp.int32),
-        pltpu.SemaphoreType.DMA((5,)),
+        pltpu.SemaphoreType.DMA((6,)),
     )
     tables_z = jax.ShapeDtypeStruct(table["zf"].shape, BF16)
     sources = (owner, by_part, cells, target, table["zf"])

time: 113 us -> 113 us (level)
  no operation moved by 1% of the time
where the time goes in v8:
time: 113 us
  blocking collectives  102 us (90%)
  Pallas kernels  10.1 us (9%)
    all_to_all x6, blocking collectives, swap(): return lax.all_to_all(x, axis, split_axis=0, concat_axis=0, tiled=True)  102 us
    pallas_call x7, Pallas kernels, call(): pl.pallas_call(body, name=name, out_shape=shapes[0] if single else shapes...  10.1 us

profile of v8, /device:TPU:1, one launch (start us, length us, event | category | flops | bytes accessed | tf_op | source)
XLA Modules:
  0.0 112.8 jit_solution(13423595141673281241)
XLA Ops:
  0.6 1.1 %route.1 = (f32[32,4,128]{2,1,0:T(4,128)S(1)}, f32[8,8,256]{2,1,0:T(8,128)S(1)}, bf16[2,256,256]{2,1,0:T(8,128)(2,1)S(1)}, s32[1,32]{1,0:T(1,128)S(1)}) custom-call(s32[1,32]{1,0:T(1,128)} %bitcast.9, bf16[3,32,64]{2,1,0:T(8,128)(2,1)} %bitcast.8, s32[32,64]{1,0:T(8,128)} %refs_2_.1, f32[8,8,256]{2,1,0:T(8,128)} %refs_3_.1, ...), custom_call_target="tpu_custom_call" | custom-call | tf_op jit(solution)/shard_map/route/pallas_call | solution.py:516
  1.8 17.0 %all_to_all.30.route = f32[32,4,128]{2,1,0:T(4,128)S(1)} all-to-all(f32[32,4,128]{2,1,0:T(4,128)S(1)} %get-tuple-element.10), channel_id=1, replica_groups=mesh['gx'=16,'gy'=32] {'gy'}, dimensions={0} | all-to-all | bytes 131072 | tf_op jit(solution)/shard_map/all_to_all | solution.py:532
  18.8 1.2 %splat.1 = f32[32,8,256]{2,1,0:T(8,128)S(1)} custom-call(f32[32,4,128]{2,1,0:T(4,128)S(1)} %all_to_all.30.route, f32[8,8,256]{2,1,0:T(8,128)S(1)} %get-tuple-element.11.target, bf16[2,256,256]{2,1,0:T(8,128)(2,1)S(1)} %get-tuple-element.12.zf), custom_call_target="tpu_custom_call" | custom-call | tf_op jit(solution)/shard_map/splat/pallas_call | solution.py:516
  19.9 0.0 copy-start
  20.0 0.0 copy-start.1
  20.0 12.6 %all_to_all.31.got = f32[32,8,256]{2,1,0:T(8,128)S(1)} all-to-all(f32[32,8,256]{2,1,0:T(8,128)S(1)} %splat.1), channel_id=1, replica_groups=mesh['gx'=16,'gy'=32] {'gy'}, dimensions={0} | all-to-all | bytes 524288 | tf_op jit(solution)/shard_map/all_to_all | solution.py:532
  32.6 0.0 copy-done.5
  32.6 0.0 copy-done.1
  32.6 0.0 copy-start.3
  32.6 0.0 copy-start.4
  32.6 0.0 copy-start.8
  32.6 0.0 copy-start.9
  32.6 1.2 %forward_y.1 = s32[16,16,128]{2,1,0:T(8,128)S(1)} custom-call(f32[32,8,256]{2,1,0:T(8,128)S(1)} %all_to_all.31.got, bf16[256,768]{1,0:T(8,128)(2,1)S(1)} %copy-done.5, bf16[384,256]{1,0:T(8,128)(2,1)S(1)} %copy-done.1, f32[3,128,128]{2,1,0:T(8,128)S(1)} %copy-done), custom_call_target="tpu_custom_call" | custom-call | tf_op jit(solution)/shard_map/forward_y/pallas_call | solution.py:516
  33.8 0.0 copy-start.7
  33.8 25.8 %all_to_all.32.got = s32[16,16,128]{2,1,0:T(8,128)S(1)} all-to-all(s32[16,16,128]{2,1,0:T(8,128)S(1)} %forward_y.1), channel_id=1, replica_groups=mesh['gx'=16,'gy'=32] {'gx'}, dimensions={0} | all-to-all | bytes 262144 | tf_op jit(solution)/shard_map/all_to_all | solution.py:532
  59.6 0.0 copy-start.6
  59.6 2.4 %spectrum.1 = s32[288,128]{1,0:T(8,128)S(1)} custom-call(s32[16,16,128]{2,1,0:T(8,128)S(1)} %all_to_all.32.got, bf16[256,768]{1,0:T(8,128)(2,1)S(1)} %copy-done.4, bf16[256,768]{1,0:T(8,128)(2,1)S(1)} %copy-done.3, bf16[384,256]{1,0:T(8,128)(2,1)S(1)} %copy-done.8, f32[2,128,128]{2,1,0:T(8,128)S(1)} %copy-done.9, bf16[2,256,256]{2,1,0:T(8,128)(2,1)S(1)} %copy-done.7), custom_call_target="tpu_custom_call" | custom-call | tf_op jit(solution)/shard_map/spectrum/pallas_call | solution.py:516
  62.0 18.3 %all_to_all.33 = s32[16,18,1,128]{3,2,1,0:T(1,128)S(1)} all-to-all(s32[16,18,1,128]{3,2,1,0:T(1,128)S(1)} %bitcast.5), channel_id=1, replica_groups=mesh['gx'=16,'gy'=32] {'gx'}, dimensions={0} | all-to-all | bytes 294912 | tf_op jit(solution)/shard_map/all_to_all | solution.py:532
  80.4 1.7 %inverse_y.1 = f32[32,8,384]{2,1,0:T(8,128)S(1)} custom-call(s32[288,128]{1,0:T(8,128)S(1)} %bitcast.6, bf16[256,768]{1,0:T(8,128)(2,1)S(1)} %copy-done.6, bf16[384,256]{1,0:T(8,128)(2,1)S(1)} %copy-done.1, f32[3,128,128]{2,1,0:T(8,128)S(1)} %copy-done), custom_call_target="tpu_custom_call" | custom-call | tf_op jit(solution)/shard_map/inverse_y/pallas_call | solution.py:516
  82.0 0.0 copy-start.2
  82.1 17.5 %all_to_all.34.got = f32[32,8,384]{2,1,0:T(8,128)S(1)} all-to-all(f32[32,8,384]{2,1,0:T(8,128)S(1)} %inverse_y.1), channel_id=1, replica_groups=mesh['gx'=16,'gy'=32] {'gy'}, dimensions={0} | all-to-all | bytes 786432 | tf_op jit(solution)/shard_map/all_to_all | solution.py:532
  99.6 1.5 %pick.1 = (f32[8,8,256]{2,1,0:T(8,128)}, f32[3,8,8,256]{3,2,1,0:T(8,128)}, f32[32,4,128]{2,1,0:T(4,128)S(1)}) custom-call(f32[32,8,384]{2,1,0:T(8,128)S(1)} %all_to_all.34.got, bf16[768,256]{1,0:T(8,128)(2,1)S(1)} %copy-done.2, f32[32,4,128]{2,1,0:T(4,128)S(1)} %all_to_all.30.route), custom_call_target="tpu_custom_call" | custom-call | tf_op jit(solution)/shard_map/pick/pallas_call | solution.py:516
  101.1 10.7 %all_to_all.35.got = f32[32,4,128]{2,1,0:T(4,128)S(1)} all-to-all(f32[32,4,128]{2,1,0:T(4,128)S(1)} %get-tuple-element.16), channel_id=1, replica_groups=mesh['gx'=16,'gy'=32] {'gy'}, dimensions={0} | all-to-all | bytes 131072 | tf_op jit(solution)/shard_map/all_to_all | solution.py:532
  111.8 1.1 deliver.1
  (9 shorter events, 0.0 us)
Async XLA Ops:
  18.8 13.8 %copy-start.5 = (bf16[256,768]{1,0:T(8,128)(2,1)S(1)}, bf16[256,768]{1,0:T(8,128)(2,1)}, u32[]{:S(2)}) copy-start(bf16[256,768]{1,0:T(8,128)(2,1)} %constant.24.clone.rows) | copy-start | bytes 1179652
  19.9 12.7 %copy-start = (f32[3,128,128]{2,1,0:T(8,128)S(1)}, f32[3,128,128]{2,1,0:T(8,128)}, u32[]{:S(2)}) copy-start(f32[3,128,128]{2,1,0:T(8,128)} %constant.30.clone.twist) | copy-start | bytes 589828
  20.0 12.6 %copy-start.1 = (bf16[384,256]{1,0:T(8,128)(2,1)S(1)}, bf16[384,256]{1,0:T(8,128)(2,1)}, u32[]{:S(2)}) copy-start(bf16[384,256]{1,0:T(8,128)(2,1)} %constant.28.clone.lanes) | copy-start | bytes 589828
  32.6 27.0 %copy-start.3 = (bf16[256,768]{1,0:T(8,128)(2,1)S(1)}, bf16[256,768]{1,0:T(8,128)(2,1)}, u32[]{:S(2)}) copy-start(bf16[256,768]{1,0:T(8,128)(2,1)} %constant.27.clone.back) | copy-start | bytes 1179652
  32.6 27.0 %copy-start.4 = (bf16[256,768]{1,0:T(8,128)(2,1)S(1)}, bf16[256,768]{1,0:T(8,128)(2,1)}, u32[]{:S(2)}) copy-start(bf16[256,768]{1,0:T(8,128)(2,1)} %constant.25.clone.rows) | copy-start | bytes 1179652
  32.6 27.0 %copy-start.8 = (bf16[384,256]{1,0:T(8,128)(2,1)S(1)}, bf16[384,256]{1,0:T(8,128)(2,1)}, u32[]{:S(2)}) copy-start(bf16[384,256]{1,0:T(8,128)(2,1)} %constant.29.clone.lanes) | copy-start | bytes 589828
  32.6 27.0 %copy-start.9 = (f32[2,128,128]{2,1,0:T(8,128)S(1)}, f32[2,128,128]{2,1,0:T(8,128)}, u32[]{:S(2)}) copy-start(f32[2,128,128]{2,1,0:T(8,128)} %constant.31.clone.twist) | copy-start | bytes 393220
  33.8 25.8 %copy-start.7 = (bf16[2,256,256]{2,1,0:T(8,128)(2,1)S(1)}, bf16[2,256,256]{2,1,0:T(8,128)(2,1)}, u32[]{:S(2)}) copy-start(bf16[2,256,256]{2,1,0:T(8,128)(2,1)} %constant.32.clone.mirror) | copy-start | bytes 786436
  59.6 20.8 %copy-start.6 = (bf16[256,768]{1,0:T(8,128)(2,1)S(1)}, bf16[256,768]{1,0:T(8,128)(2,1)}, u32[]{:S(2)}) copy-start(bf16[256,768]{1,0:T(8,128)(2,1)} %constant.26.clone.back) | copy-start | bytes 1179652
  82.0 17.5 %copy-start.2 = (bf16[768,256]{1,0:T(8,128)(2,1)S(1)}, bf16[768,256]{1,0:T(8,128)(2,1)}, u32[]{:S(2)}) copy-start(bf16[768,256]{1,0:T(8,128)(2,1)} %constant.23.clone.zb) | copy-start | bytes 1179652

commit v9 on v8

--- a/solution.py
+++ b/solution.py
@@ -365,8 +365,8 @@
     edge = jnp.where(lane == 3, pltpu.roll(above, 88, 1), edge)
     grad_x, h = gradients
     fields = (chi, grad_x, h * weight)
-    exponents = [exponent_of(x) for x in fields]
-    exponents[0] = jnp.maximum(exponents[0], exponent_of(edge))
+    largest = jnp.maximum(jnp.abs(chi), jnp.abs(edge))
+    exponents = [exponent_of(x) for x in (largest,) + fields[1:]]
     first, second = encode(fields, exponents)
     edges[...] = fixed(edge, exponents[0], EDGE_BITS)
     folded = edges[pl.ds(0, 32, stride=4), :]

time: 113 us -> 113 us (level)
  no operation moved by 1% of the time
where the time goes in v9:
time: 113 us
  blocking collectives  102 us (90%)
  Pallas kernels  10 us (9%)
    all_to_all x6, blocking collectives, swap(): return lax.all_to_all(x, axis, split_axis=0, concat_axis=0, tiled=True)  102 us
    pallas_call x7, Pallas kernels, call(): pl.pallas_call(body, name=name, out_shape=shapes[0] if single else shapes...  10 us

profile of v9, /device:TPU:1, one launch (start us, length us, event | category | flops | bytes accessed | tf_op | source)
XLA Modules:
  0.0 112.8 jit_solution(11321057444091653023)
XLA Ops:
  0.6 1.1 %route.1 = (f32[32,4,128]{2,1,0:T(4,128)S(1)}, f32[8,8,256]{2,1,0:T(8,128)S(1)}, bf16[2,256,256]{2,1,0:T(8,128)(2,1)S(1)}, s32[1,32]{1,0:T(1,128)S(1)}) custom-call(s32[1,32]{1,0:T(1,128)} %bitcast.9, bf16[3,32,64]{2,1,0:T(8,128)(2,1)} %bitcast.8, s32[32,64]{1,0:T(8,128)} %refs_2_.1, f32[8,8,256]{2,1,0:T(8,128)} %refs_3_.1, ...), custom_call_target="tpu_custom_call" | custom-call | tf_op jit(solution)/shard_map/route/pallas_call | solution.py:516
  1.8 17.0 %all_to_all.30.route = f32[32,4,128]{2,1,0:T(4,128)S(1)} all-to-all(f32[32,4,128]{2,1,0:T(4,128)S(1)} %get-tuple-element.10), channel_id=1, replica_groups=mesh['gx'=16,'gy'=32] {'gy'}, dimensions={0} | all-to-all | bytes 131072 | tf_op jit(solution)/shard_map/all_to_all | solution.py:532
  18.8 1.2 %splat.1 = f32[32,8,256]{2,1,0:T(8,128)S(1)} custom-call(f32[32,4,128]{2,1,0:T(4,128)S(1)} %all_to_all.30.route, f32[8,8,256]{2,1,0:T(8,128)S(1)} %get-tuple-element.11.target, bf16[2,256,256]{2,1,0:T(8,128)(2,1)S(1)} %get-tuple-element.12.zf), custom_call_target="tpu_custom_call" | custom-call | tf_op jit(solution)/shard_map/splat/pallas_call | solution.py:516
  19.9 0.0 copy-start
  20.0 0.0 copy-start.1
  20.0 12.6 %all_to_all.31.got = f32[32,8,256]{2,1,0:T(8,128)S(1)} all-to-all(f32[32,8,256]{2,1,0:T(8,128)S(1)} %splat.1), channel_id=1, replica_groups=mesh['gx'=16,'gy'=32] {'gy'}, dimensions={0} | all-to-all | bytes 524288 | tf_op jit(solution)/shard_map/all_to_all | solution.py:532
  32.6 0.0 copy-done.5
  32.6 0.0 copy-start.3
  32.6 0.0 copy-start.4
  32.6 0.0 copy-start.8
  32.6 0.0 copy-start.9
  32.6 1.2 %forward_y.1 = s32[16,16,128]{2,1,0:T(8,128)S(1)} custom-call(f32[32,8,256]{2,1,0:T(8,128)S(1)} %all_to_all.31.got, bf16[256,768]{1,0:T(8,128)(2,1)S(1)} %copy-done.5, bf16[384,256]{1,0:T(8,128)(2,1)S(1)} %copy-done.1, f32[3,128,128]{2,1,0:T(8,128)S(1)} %copy-done), custom_call_target="tpu_custom_call" | custom-call | tf_op jit(solution)/shard_map/forward_y/pallas_call | solution.py:516
  33.8 0.0 copy-start.7
  33.8 25.8 %all_to_all.32.got = s32[16,16,128]{2,1,0:T(8,128)S(1)} all-to-all(s32[16,16,128]{2,1,0:T(8,128)S(1)} %forward_y.1), channel_id=1, replica_groups=mesh['gx'=16,'gy'=32] {'gx'}, dimensions={0} | all-to-all | bytes 262144 | tf_op jit(solution)/shard_map/all_to_all | solution.py:532
  59.6 0.0 copy-done.9
  59.6 0.0 copy-start.6
  59.6 2.3 %spectrum.1 = s32[288,128]{1,0:T(8,128)S(1)} custom-call(s32[16,16,128]{2,1,0:T(8,128)S(1)} %all_to_all.32.got, bf16[256,768]{1,0:T(8,128)(2,1)S(1)} %copy-done.4, bf16[256,768]{1,0:T(8,128)(2,1)S(1)} %copy-done.3, bf16[384,256]{1,0:T(8,128)(2,1)S(1)} %copy-done.8, f32[2,128,128]{2,1,0:T(8,128)S(1)} %copy-done.9, bf16[2,256,256]{2,1,0:T(8,128)(2,1)S(1)} %copy-done.7), custom_call_target="tpu_custom_call" | custom-call | tf_op jit(solution)/shard_map/spectrum/pallas_call | solution.py:516
  62.0 18.4 %all_to_all.33 = s32[16,18,1,128]{3,2,1,0:T(1,128)S(1)} all-to-all(s32[16,18,1,128]{3,2,1,0:T(1,128)S(1)} %bitcast.5), channel_id=1, replica_groups=mesh['gx'=16,'gy'=32] {'gx'}, dimensions={0} | all-to-all | bytes 294912 | tf_op jit(solution)/shard_map/all_to_all | solution.py:532
  80.3 1.7 %inverse_y.1 = f32[32,8,384]{2,1,0:T(8,128)S(1)} custom-call(s32[288,128]{1,0:T(8,128)S(1)} %bitcast.6, bf16[256,768]{1,0:T(8,128)(2,1)S(1)} %copy-done.6, bf16[384,256]{1,0:T(8,128)(2,1)S(1)} %copy-done.1, f32[3,128,128]{2,1,0:T(8,128)S(1)} %copy-done), custom_call_target="tpu_custom_call" | custom-call | tf_op jit(solution)/shard_map/inverse_y/pallas_call | solution.py:516
  82.0 0.0 copy-start.2
  82.0 17.5 %all_to_all.34.got = f32[32,8,384]{2,1,0:T(8,128)S(1)} all-to-all(f32[32,8,384]{2,1,0:T(8,128)S(1)} %inverse_y.1), channel_id=1, replica_groups=mesh['gx'=16,'gy'=32] {'gy'}, dimensions={0} | all-to-all | bytes 786432 | tf_op jit(solution)/shard_map/all_to_all | solution.py:532
  99.5 1.5 %pick.1 = (f32[8,8,256]{2,1,0:T(8,128)}, f32[3,8,8,256]{3,2,1,0:T(8,128)}, f32[32,4,128]{2,1,0:T(4,128)S(1)}) custom-call(f32[32,8,384]{2,1,0:T(8,128)S(1)} %all_to_all.34.got, bf16[768,256]{1,0:T(8,128)(2,1)S(1)} %copy-done.2, f32[32,4,128]{2,1,0:T(4,128)S(1)} %all_to_all.30.route), custom_call_target="tpu_custom_call" | custom-call | tf_op jit(solution)/shard_map/pick/pallas_call | solution.py:516
  101.0 10.7 %all_to_all.35.got = f32[32,4,128]{2,1,0:T(4,128)S(1)} all-to-all(f32[32,4,128]{2,1,0:T(4,128)S(1)} %get-tuple-element.16), channel_id=1, replica_groups=mesh['gx'=16,'gy'=32] {'gy'}, dimensions={0} | all-to-all | bytes 131072 | tf_op jit(solution)/shard_map/all_to_all | solution.py:532
  111.7 1.1 deliver.1
  (9 shorter events, 0.0 us)
Async XLA Ops:
  18.8 13.8 %copy-start.5 = (bf16[256,768]{1,0:T(8,128)(2,1)S(1)}, bf16[256,768]{1,0:T(8,128)(2,1)}, u32[]{:S(2)}) copy-start(bf16[256,768]{1,0:T(8,128)(2,1)} %constant.24.clone.rows) | copy-start | bytes 1179652
  19.9 12.7 %copy-start = (f32[3,128,128]{2,1,0:T(8,128)S(1)}, f32[3,128,128]{2,1,0:T(8,128)}, u32[]{:S(2)}) copy-start(f32[3,128,128]{2,1,0:T(8,128)} %constant.30.clone.twist) | copy-start | bytes 589828
  20.0 12.6 %copy-start.1 = (bf16[384,256]{1,0:T(8,128)(2,1)S(1)}, bf16[384,256]{1,0:T(8,128)(2,1)}, u32[]{:S(2)}) copy-start(bf16[384,256]{1,0:T(8,128)(2,1)} %constant.28.clone.lanes) | copy-start | bytes 589828
  32.6 27.0 %copy-start.3 = (bf16[256,768]{1,0:T(8,128)(2,1)S(1)}, bf16[256,768]{1,0:T(8,128)(2,1)}, u32[]{:S(2)}) copy-start(bf16[256,768]{1,0:T(8,128)(2,1)} %constant.27.clone.back) | copy-start | bytes 1179652
  32.6 27.0 %copy-start.4 = (bf16[256,768]{1,0:T(8,128)(2,1)S(1)}, bf16[256,768]{1,0:T(8,128)(2,1)}, u32[]{:S(2)}) copy-start(bf16[256,768]{1,0:T(8,128)(2,1)} %constant.25.clone.rows) | copy-start | bytes 1179652
  32.6 27.0 %copy-start.8 = (bf16[384,256]{1,0:T(8,128)(2,1)S(1)}, bf16[384,256]{1,0:T(8,128)(2,1)}, u32[]{:S(2)}) copy-start(bf16[384,256]{1,0:T(8,128)(2,1)} %constant.29.clone.lanes) | copy-start | bytes 589828
  32.6 27.0 %copy-start.9 = (f32[2,128,128]{2,1,0:T(8,128)S(1)}, f32[2,128,128]{2,1,0:T(8,128)}, u32[]{:S(2)}) copy-start(f32[2,128,128]{2,1,0:T(8,128)} %constant.31.clone.twist) | copy-start | bytes 393220
  33.8 25.8 %copy-start.7 = (bf16[2,256,256]{2,1,0:T(8,128)(2,1)S(1)}, bf16[2,256,256]{2,1,0:T(8,128)(2,1)}, u32[]{:S(2)}) copy-start(bf16[2,256,256]{2,1,0:T(8,128)(2,1)} %constant.32.clone.mirror) | copy-start | bytes 786436
  59.6 20.7 %copy-start.6 = (bf16[256,768]{1,0:T(8,128)(2,1)S(1)}, bf16[256,768]{1,0:T(8,128)(2,1)}, u32[]{:S(2)}) copy-start(bf16[256,768]{1,0:T(8,128)(2,1)} %constant.26.clone.back) | copy-start | bytes 1179652
  82.0 17.5 %copy-start.2 = (bf16[768,256]{1,0:T(8,128)(2,1)S(1)}, bf16[768,256]{1,0:T(8,128)(2,1)}, u32[]{:S(2)}) copy-start(bf16[768,256]{1,0:T(8,128)(2,1)} %constant.23.clone.zb) | copy-start | bytes 1179652
